TPU v7x, 256 devices: a whole 4x4x8 slice. The times are simulated.
256 devices in a mesh: mesh: 256 (over x, y, z, core).
Axes of the slice: x: 4, y: 4, z: 8, core: 2. Of those that a mesh axis runs over, the one named last changes fastest.
Arguments:
- state: float32 [256, 65536], P(None, 'mesh'), may hold values from -6 to 6
- target: float32 [256, 65536], P(None, 'mesh'), may hold values from -15 to 15
- weight_in: float32 [256, 256], replicated, may hold values from -0.375 to 0.375
- bias_in: float32 [256], replicated, may hold values from -3 to 3
- weight_out: float32 [256, 256], replicated, may hold values from -0.375 to 0.375
- bias_out: float32 [256], replicated, may hold values from -4 to 4
- nbr_face: int32 [6, 65536], P(None, 'mesh'), may hold values from 0 to 2047, as said below
- send_faces: int32 [2, 65536], P(None, 'mesh'), may hold values from 0 to 511, as said below
Outputs:
- final_state: float32 [256, 65536], P(None, 'mesh')
- loss: float32 [], replicated
- step_weight_in: float32 [256, 256], replicated
- step_bias_in: float32 [256], replicated
- step_weight_out: float32 [256, 256], replicated
- step_bias_out: float32 [256], replicated
Inputs may be any that keep to these rules, and one draw needn't show every extreme that they name: `nbr_face`: A face of the device's own elements refers to a column of the opposite face (f xor 1) of a neighbouring element, with the same order of nodes; faces on the first dimension at a device's lower or upper end refer to the received columns. Every received column is referred to by exactly one face. `send_faces`: entries of row 0 are face-0 columns of the device's own elements (below 256), entries of row 1 face-1 columns (256 to 511), none twice in a block; entry t of row 1 (row 0) is the face seen across by the face that refers to received slot t on the device above (below).
All inputs are finite; a program needn't handle non-finite values.
Results may differ from a plain program's by a relative error of at most 0.0001.
Values sent between devices are 32-bit elements; how exact they have to be, the bound alone decides.
No kernel may reach another device: no remote copies, remote signals or barrier semaphores. Data moves between devices by JAX's collectives and lax.ppermute only.
A program may use at most 64 MiB of HBM per device.

v0:
```python
import jax
import jax.numpy as jnp
import numpy as np
from jax import lax
from jax.sharding import PartitionSpec as P

TSTEPS = 2


HIGH = lax.Precision.HIGHEST
TIME_STEP = 0.05
LIFT_FACTOR = 6.0
TINY = 1e-20


def padded(cells, sides, width):
    for axis, dim in sides:
        count = lax.axis_size(axis)
        head = lax.slice_in_dim(cells, 0, width, axis=dim)
        tail = lax.slice_in_dim(cells, cells.shape[dim] - width, cells.shape[dim], axis=dim)
        cells = jnp.concatenate(
            [
                lax.ppermute(tail, axis, [(i, (i + 1) % count) for i in range(count)]),
                cells,
                lax.ppermute(head, axis, [((i + 1) % count, i) for i in range(count)]),
            ],
            axis=dim,
        )
    return cells


def derivative_tables():
    gll_points = np.array([-1.0, -1.0 / np.sqrt(5.0), 1.0 / np.sqrt(5.0), 1.0])
    bary_weights = np.array(
        [
            1.0
            / np.prod(
                [gll_points[first] - gll_points[second] for second in range(4) if second != first]
            )
            for first in range(4)
        ]
    )
    derivative = np.zeros((4, 4))
    for first in range(4):
        for second in range(4):
            if first != second:
                derivative[first, second] = (
                    bary_weights[second]
                    / bary_weights[first]
                    / (gll_points[first] - gll_points[second])
                )
        derivative[first, first] = -np.sum(derivative[first])
    identity_four = np.eye(4)
    along_first = np.kron(np.kron(derivative, identity_four), identity_four)
    along_second = np.kron(np.kron(identity_four, derivative), identity_four)
    along_third = np.kron(identity_four, np.kron(identity_four, derivative))
    return jnp.asarray(np.stack([along_first, along_second, along_third]), dtype=jnp.float32)


def matmul(left, right):
    return jnp.dot(left, right, precision=HIGH, preferred_element_type=jnp.float32)


def face_part(block, face):
    layer = 0 if face % 2 == 0 else 3
    direction = face // 2
    if direction == 0:
        piece = block[layer]
    elif direction == 1:
        piece = block[:, layer]
    else:
        piece = block[:, :, layer]
    return piece.reshape(16, block.shape[-1])


def face_index(field, face):
    layer = 0 if face % 2 == 0 else 3
    direction = face // 2
    if direction == 0:
        return (field, layer)
    if direction == 1:
        return (field, slice(None), layer)
    return (field, slice(None), slice(None), layer)


def traces(state_now):
    cells = state_now.shape[1]
    blocks = state_now.reshape(4, 4, 4, 4, cells)
    columns = []
    for face in range(6):
        pressure = face_part(blocks[0], face)
        normal_speed = face_part(blocks[1 + face // 2], face)
        columns.append(jnp.concatenate([pressure, normal_speed], axis=0))
    return jnp.concatenate(columns, axis=1)


def local_rhs(state_now, outside, weight_in, bias_in, weight_out, bias_out):
    cells = state_now.shape[1]
    tables = derivative_tables()
    inner = traces(state_now)
    pressure = state_now[0:64]
    volume_p = -(
        matmul(tables[0], state_now[64:128])
        + matmul(tables[1], state_now[128:192])
        + matmul(tables[2], state_now[192:256])
    )
    volume_v = [-matmul(tables[axis_num], pressure) for axis_num in range(3)]
    result = jnp.concatenate([volume_p] + volume_v, axis=0).reshape(4, 4, 4, 4, cells)
    for face in range(6):
        sign = -1.0 if face % 2 == 0 else 1.0
        inner_face = inner[:, face * cells : (face + 1) * cells]
        outer_face = outside[:, face * cells : (face + 1) * cells]
        jump_p = inner_face[:16] - outer_face[:16]
        jump_v = sign * (inner_face[16:] - outer_face[16:])
        flux = 0.5 * jump_v - 0.5 * jump_p
        result = result.at[face_index(0, face)].add((LIFT_FACTOR * flux).reshape(4, 4, cells))
        result = result.at[face_index(1 + face // 2, face)].add(
            (-LIFT_FACTOR * sign * flux).reshape(4, 4, cells)
        )
    hidden = jnp.tanh(matmul(weight_in, state_now) + bias_in[:, None])
    closure = matmul(weight_out, hidden) + bias_out[:, None]
    return result.reshape(state_now.shape[0], cells) + closure


def exterior(inner, nbr_flat, send_flat, halo_width):
    outgoing = inner[:, send_flat]
    received = padded(outgoing, (("mesh", 1),), halo_width)
    table = jnp.concatenate(
        [inner, received[:, :halo_width], received[:, 3 * halo_width :]], axis=1
    )
    return table[:, nbr_flat]


def adjoint_rhs(state_now, outside, cotangent, params, nbr_flat, send_flat, halo_width):
    unused, pullback = jax.vjp(local_rhs, state_now, outside, *params)
    results = pullback(cotangent)
    grad_state = results[0]
    grad_outside = results[1]
    own_columns = grad_outside.shape[1]
    grad_table = (
        jnp.zeros((grad_outside.shape[0], own_columns + 2 * halo_width), jnp.float32)
        .at[:, nbr_flat]
        .add(grad_outside)
    )
    returned = padded(grad_table[:, own_columns:], (("mesh", 1),), halo_width)
    grad_outgoing = jnp.concatenate(
        [returned[:, :halo_width], returned[:, 3 * halo_width :]], axis=1
    )
    grad_inner = grad_table[:, :own_columns].at[:, send_flat].add(grad_outgoing)
    unused_trace, trace_pull = jax.vjp(traces, state_now)
    return (grad_state + trace_pull(grad_inner)[0], tuple(results[2:]))


def local(state, target, weight_in, bias_in, weight_out, bias_out, nbr_face, send_faces):
    params = (weight_in, bias_in, weight_out, bias_out)
    cells = state.shape[1]
    halo_width = send_faces.shape[1]
    nbr_flat = nbr_face.reshape(-1)
    send_flat = send_faces.reshape(-1)
    saved = []
    current = state
    for step_index in range(TSTEPS):
        outside_first = exterior(traces(current), nbr_flat, send_flat, halo_width)
        first_section = current + TIME_STEP * local_rhs(current, outside_first, *params)
        outside_second = exterior(traces(first_section), nbr_flat, send_flat, halo_width)
        next_state = 0.5 * current + 0.5 * (
            first_section + TIME_STEP * local_rhs(first_section, outside_second, *params)
        )
        saved.append((current, outside_first, first_section, outside_second))
        current = next_state
    count = float(state.shape[0] * cells * lax.axis_size("mesh"))
    mismatch = current - target
    loss_part = 0.5 * jnp.sum(mismatch * mismatch)
    loss_total = lax.psum(loss_part, "mesh")
    loss_member = jnp.zeros((), jnp.float32)
    adjoint = mismatch / count
    gradients = tuple((jnp.zeros_like(param_item) for param_item in params))
    for step_index in reversed(range(TSTEPS)):
        state_first, outside_first, state_second, outside_second = saved[step_index]
        back_second, grads_second = adjoint_rhs(
            state_second,
            outside_second,
            0.5 * TIME_STEP * adjoint,
            params,
            nbr_flat,
            send_flat,
            halo_width,
        )
        cot_second = 0.5 * adjoint + back_second
        back_first, grads_first = adjoint_rhs(
            state_first,
            outside_first,
            TIME_STEP * cot_second,
            params,
            nbr_flat,
            send_flat,
            halo_width,
        )
        adjoint = 0.5 * adjoint + cot_second + back_first
        gradients = jax.tree.map(
            lambda total_item, second_item, first_item: total_item + second_item + first_item,
            gradients,
            grads_second,
            grads_first,
        )
    param_count = float(sum((param_item.size for param_item in params)))
    summed = lax.psum((gradients[0], gradients[1], gradients[2], gradients[3], loss_member), "mesh")
    full_in, full_bias_in, full_out, full_bias_out, loss_back = summed
    total_sq = (
        jnp.sum(full_in * full_in)
        + jnp.sum(full_bias_in * full_bias_in)
        + jnp.sum(full_out * full_out)
        + jnp.sum(full_bias_out * full_bias_out)
    )
    scale = lax.rsqrt(total_sq / param_count + TINY)
    step_weight_in = full_in * scale
    step_weight_out = full_out * scale
    loss = loss_total / count
    return (
        current,
        loss,
        step_weight_in,
        full_bias_in * scale,
        step_weight_out,
        full_bias_out * scale,
    )


def solution(mesh):
    in_specs = (
        P(None, "mesh"),
        P(None, "mesh"),
        P(),
        P(),
        P(),
        P(),
        P(None, "mesh"),
        P(None, "mesh"),
    )
    out_specs = (P(None, "mesh"), P(), P(), P(), P(), P())
    return jax.shard_map(local, mesh=mesh, in_specs=in_specs, out_specs=out_specs, check_vma=False)
```

profile of v0, /device:TPU:1, one launch (start us, length us, event | category | flops | bytes accessed | tf_op | source)
XLA Modules:
  0.0 575.0 jit_solution(1900342720889298683)
XLA Ops:
  12.2 3.3 collective-permute-start.1
  16.1 1.4 concatenate.237
  17.4 1.4 concatenate.236
  24.7 3.7 gather_fusion.1
  28.4 1.4 copy.407
  30.0 2.0 fusion.91
  32.1 2.0 fusion.92
  34.4 1.9 broadcast_select_fusion.3
  36.3 1.4 scatter-add.216
  42.9 8.1 %collective-permute-start.3 = (f32[32,256]{1,0:T(8,128)S(1)}, f32[32,256]{1,0:T(8,128)S(1)}, u32[]{:S(2)}, u32[]{:S(2)}) collective-permute-start(f32[32,256]{1,0:T(8,128)S(1)} %get-tuple-element.827), channel_id=1, source_target_pairs={{1,0},{2,1},{3,2},{4,3},{5,4},{6,5},{7,6},{8,7},{9,8},{10,9},{11,1... | collective-permute-start | bytes 98312 | tf_op jit(solution)/shard_map/ppermute | solution.py:25
  52.2 3.7 gather_fusion.3
  55.9 1.4 copy.427
  57.6 2.0 fusion.93
  59.6 2.0 fusion.94
  61.9 1.9 broadcast_select_fusion.2
  63.8 1.4 scatter-add.236
  79.8 8.0 %collective-permute-start.5 = (f32[32,256]{1,0:T(8,128)S(1)}, f32[32,256]{1,0:T(8,128)S(1)}, u32[]{:S(2)}, u32[]{:S(2)}) collective-permute-start(f32[32,256]{1,0:T(8,128)S(1)} %get-tuple-element.821), channel_id=1, source_target_pairs={{1,0},{2,1},{3,2},{4,3},{5,4},{6,5},{7,6},{8,7},{9,8},{10,9},{11,1... | collective-permute-start | bytes 98312 | tf_op jit(solution)/shard_map/ppermute | solution.py:25
  89.3 1.3 copy.447
  90.5 4.0 gather_fusion.5
  94.6 1.4 copy.448
  97.0 2.0 fusion.95
  99.0 2.0 fusion.96
  101.2 1.9 broadcast_select_fusion.1
  103.2 1.4 scatter-add.256
  118.8 8.0 %collective-permute-start.7 = (f32[32,256]{1,0:T(8,128)S(1)}, f32[32,256]{1,0:T(8,128)S(1)}, u32[]{:S(2)}, u32[]{:S(2)}) collective-permute-start(f32[32,256]{1,0:T(8,128)S(1)} %get-tuple-element.815), channel_id=1, source_target_pairs={{1,0},{2,1},{3,2},{4,3},{5,4},{6,5},{7,6},{8,7},{9,8},{10,9},{11,1... | collective-permute-start | bytes 98312 | tf_op jit(solution)/shard_map/ppermute | solution.py:25
  128.3 1.3 copy.468
  129.6 4.0 gather_fusion.7
  133.6 1.4 copy.469
  136.0 2.0 fusion.97
  138.1 2.0 fusion.98
  140.3 1.9 broadcast_select_fusion
  142.3 1.4 scatter-add.328
  164.6 9.4 %scatter_custom_fusion = f32[32,2048]{0,1:T(8,128)S(1)} fusion(s32[1536]{0:T(1024)} %copy-done.116, f32[1536,32]{1,0:T(8,128)} %copy.489, f32[]{:T(128)} %constant.1151.clone.1), kind=kCustom, calls=%fused_computation.130 | custom fusion | flops 49152 | bytes 262656 | tf_op jit(solution)/shard_map/scatter-add | solution.py:143
  174.8 7.9 %collective-permute-start.9 = (f32[32,256]{0,1:T(8,128)}, f32[32,256]{0,1:T(8,128)}, u32[]{:S(2)}, u32[]{:S(2)}) collective-permute-start(f32[32,256]{0,1:T(8,128)} %get-tuple-element.648), channel_id=1, source_target_pairs={{1,0},{2,1},{3,2},{4,3},{5,4},{6,5},{7,6},{8,7},{9,8},{10,9},{11,1... | collective-permute-start | bytes 98312 | tf_op jit(solution)/shard_map/ppermute | solution.py:25
  187.5 3.8 scatter_fusion
  204.2 1.9 fusion.290
  217.7 9.4 %scatter_custom_fusion.2 = f32[32,2048]{0,1:T(8,128)S(1)} fusion(s32[1536]{0:T(1024)} %copy-done.116, f32[1536,32]{1,0:T(8,128)} %copy.524, f32[]{:T(128)} %constant.1151.clone.1), kind=kCustom, calls=%fused_computation.128 | custom fusion | flops 49152 | bytes 262656 | tf_op jit(solution)/shard_map/scatter-add | solution.py:143
  227.8 8.0 %collective-permute-start.11 = (f32[32,256]{0,1:T(8,128)}, f32[32,256]{0,1:T(8,128)}, u32[]{:S(2)}, u32[]{:S(2)}) collective-permute-start(f32[32,256]{0,1:T(8,128)} %get-tuple-element.646), channel_id=1, source_target_pairs={{1,0},{2,1},{3,2},{4,3},{5,4},{6,5},{7,6},{8,7},{9,8},{10,9},{11,1... | collective-permute-start | bytes 98312 | tf_op jit(solution)/shard_map/ppermute | solution.py:25
  239.7 3.8 scatter_fusion.1
  250.8 1.3 fusion.252
  255.7 1.3 fusion.288
  266.4 9.1 %scatter_custom_fusion.4 = f32[32,2048]{0,1:T(8,128)S(1)} fusion(s32[1536]{0:T(1024)} %copy-done.116, f32[1536,32]{1,0:T(8,128)S(1)} %copy.560, f32[]{:T(128)} %constant.1151.clone.1), kind=kCustom, calls=%fused_computation.126 | custom fusion | flops 49152 | bytes 262656 | tf_op jit(solution)/shard_map/scatter-add | solution.py:143
  276.3 8.6 %collective-permute-start.13 = (f32[32,256]{0,1:T(8,128)}, f32[32,256]{0,1:T(8,128)}, u32[]{:S(2)}, u32[]{:S(2)}) collective-permute-start(f32[32,256]{0,1:T(8,128)} %get-tuple-element.644), channel_id=1, source_target_pairs={{1,0},{2,1},{3,2},{4,3},{5,4},{6,5},{7,6},{8,7},{9,8},{10,9},{11,1... | collective-permute-start | bytes 98312 | tf_op jit(solution)/shard_map/ppermute | solution.py:25
  288.5 3.6 scatter_fusion.2
  301.4 1.3 convolution_add_fusion.3
  304.1 85.3 %all-reduce.264 = (f32[]{:T(128)}, f32[256]{0:T(256)S(1)}, f32[256]{0:T(256)S(1)}) all-reduce(f32[]{:T(128)S(6)} %mul.865, f32[256]{0:T(256)S(1)} %add_add_fusion.1, f32[256]{0:T(256)S(1)} %add_add_fusion), channel_id=1, replica_groups=mesh['mesh'=256] {'mesh'}, use_global_device_ids=true, to_apply=%region_4.0 | all-reduce | flops 513 | bytes 4104 | tf_op jit(solution)/shard_map/psum | solution.py:174
  391.3 167.7 %all-reduce.268.cloned.1.call-done = (f32[256,256]{1,0:T(8,128)}, f32[256,256]{1,0:T(8,128)}) async-done(((f32[256,256]{1,0:T(8,128)}, f32[256,256]{1,0:T(8,128)}), (f32[256,256]{1,0:T(8,128)}, f32[256,256]{1,0:T(8,128)})) %all-reduce.268.cloned.1.call-update) | async-done | bytes 524304 | tf_op jit(solution)/shard_map/psum | solution.py:207
  559.0 1.7 multiply_reduce_fusion
  (1045 shorter events, 143.6 us)
Async XLA Ops:
  7.2 30.8 %copy-start = (f32[256,256]{1,0:T(8,128)S(1)}, f32[256,256]{1,0:T(8,128)}, u32[]{:S(2)}) copy-start(f32[256,256]{1,0:T(8,128)} %param.115) | copy-start | bytes 786436
  7.2 551.8 %all-reduce.268.cloned.1.call-start = ((), (), s32[]{:S(2)}) async-start(), calls=%async_computation | async-start | bytes 1048576 | tf_op jit(solution)/shard_map/psum | solution.py:207
  10.3 31.1 %copy-start.113 = (s32[1024]{0:T(1024)}, s32[1024]{0:T(1024)S(1)}, u32[]{:S(2)}) copy-start(s32[1024]{0:T(1024)S(1)} %pad_clamp_fusion.1) | copy-start | bytes 12292
  12.0 6.8 %copy-start.2 = (f32[256,256]{1,0:T(8,128)S(1)}, f32[256,256]{1,0:T(8,128)}, u32[]{:S(2)}) copy-start(f32[256,256]{1,0:T(8,128)} %param.111) | copy-start | bytes 786436
  12.1 6.7 %copy-start.6 = (f32[64,64]{1,0:T(8,128)S(1)}, f32[64,64]{1,0:T(8,128)}, u32[]{:S(2)}) copy-start(f32[64,64]{1,0:T(8,128)} %constant.1689) | copy-start | bytes 49156
  12.2 12.2 %collective-permute-start.1 = (f32[32,256]{1,0:T(8,128)S(1)}, f32[32,256]{1,0:T(8,128)S(1)}, u32[]{:S(2)}, u32[]{:S(2)}) collective-permute-start(f32[32,256]{1,0:T(8,128)S(1)} %get-tuple-element.833), channel_id=1, source_target_pairs={{1,0},{2,1},{3,2},{4,3},{5,4},{6,5},{7,6},{8,7},{9,8},{10,9},{11,1... | collective-permute-start | bytes 98312 | tf_op jit(solution)/shard_map/ppermute | solution.py:25
  15.5 8.9 %collective-permute-start = (f32[32,256]{1,0:T(8,128)S(1)}, f32[32,256]{1,0:T(8,128)S(1)}, u32[]{:S(2)}, u32[]{:S(2)}) collective-permute-start(f32[32,256]{1,0:T(8,128)S(1)} %get-tuple-element.834), channel_id=1, source_target_pairs={{0,1},{1,2},{2,3},{3,4},{4,5},{5,6},{6,7},{7,8},{8,9},{9,10},{10,1... | collective-permute-start | bytes 98312 | tf_op jit(solution)/shard_map/ppermute | solution.py:23
  20.5 3.6 copy-start.116
  23.3 14.6 %copy-start.9 = (f32[256,256]{0,1:T(8,128)}, f32[256,256]{0,1:T(8,128)S(1)}, u32[]{:S(2)}) copy-start(f32[256,256]{0,1:T(8,128)S(1)} %fusion.18) | copy-start | bytes 786436
  24.1 28.2 %copy-start.110 = (s32[2048]{0:T(1024)}, s32[2048]{0:T(1024)S(1)}, u32[]{:S(2)}) copy-start(s32[2048]{0:T(1024)S(1)} %pad_clamp_fusion) | copy-start | bytes 24580
  42.7 8.8 %collective-permute-start.2 = (f32[32,256]{1,0:T(8,128)S(1)}, f32[32,256]{1,0:T(8,128)S(1)}, u32[]{:S(2)}, u32[]{:S(2)}) collective-permute-start(f32[32,256]{1,0:T(8,128)S(1)} %get-tuple-element.828), channel_id=1, source_target_pairs={{0,1},{1,2},{2,3},{3,4},{4,5},{5,6},{6,7},{7,8},{8,9},{9,10},{10,1... | collective-permute-start | bytes 98312 | tf_op jit(solution)/shard_map/ppermute | solution.py:23
  42.9 8.9 %collective-permute-start.3 = (f32[32,256]{1,0:T(8,128)S(1)}, f32[32,256]{1,0:T(8,128)S(1)}, u32[]{:S(2)}, u32[]{:S(2)}) collective-permute-start(f32[32,256]{1,0:T(8,128)S(1)} %get-tuple-element.827), channel_id=1, source_target_pairs={{1,0},{2,1},{3,2},{4,3},{5,4},{6,5},{7,6},{8,7},{9,8},{10,9},{11,1... | collective-permute-start | bytes 98312 | tf_op jit(solution)/shard_map/ppermute | solution.py:25
  69.5 4.4 copy-start.81
  69.5 6.8 %copy-start.85 = (f32[16,256]{1,0:T(8,128)}, f32[16,256]{1,0:T(8,128)S(1)}, u32[]{:S(2)}) copy-start(f32[16,256]{1,0:T(8,128)S(1)} %reshape_squeeze.86) | copy-start | bytes 49156
  69.6 3.1 copy-start.83
  69.7 4.3 copy-start.97
  69.7 3.0 copy-start.91
  70.8 34.0 %copy-start.11 = (f32[256,256]{0,1:T(8,128)}, f32[256,256]{0,1:T(8,128)S(1)}, u32[]{:S(2)}) copy-start(f32[256,256]{0,1:T(8,128)S(1)} %fusion.12) | copy-start | bytes 786436
  78.2 9.5 %collective-permute-start.4 = (f32[32,256]{1,0:T(8,128)S(1)}, f32[32,256]{1,0:T(8,128)S(1)}, u32[]{:S(2)}, u32[]{:S(2)}) collective-permute-start(f32[32,256]{1,0:T(8,128)S(1)} %get-tuple-element.822), channel_id=1, source_target_pairs={{0,1},{1,2},{2,3},{3,4},{4,5},{5,6},{6,7},{7,8},{8,9},{9,10},{10,1... | collective-permute-start | bytes 98312 | tf_op jit(solution)/shard_map/ppermute | solution.py:23
  79.8 8.8 %collective-permute-start.5 = (f32[32,256]{1,0:T(8,128)S(1)}, f32[32,256]{1,0:T(8,128)S(1)}, u32[]{:S(2)}, u32[]{:S(2)}) collective-permute-start(f32[32,256]{1,0:T(8,128)S(1)} %get-tuple-element.821), channel_id=1, source_target_pairs={{1,0},{2,1},{3,2},{4,3},{5,4},{6,5},{7,6},{8,7},{9,8},{10,9},{11,1... | collective-permute-start | bytes 98312 | tf_op jit(solution)/shard_map/ppermute | solution.py:25
  109.7 4.5 copy-start.87
  109.8 4.4 copy-start.93
  109.9 3.1 copy-start.89
  117.3 9.6 %collective-permute-start.6 = (f32[32,256]{1,0:T(8,128)S(1)}, f32[32,256]{1,0:T(8,128)S(1)}, u32[]{:S(2)}, u32[]{:S(2)}) collective-permute-start(f32[32,256]{1,0:T(8,128)S(1)} %get-tuple-element.816), channel_id=1, source_target_pairs={{0,1},{1,2},{2,3},{3,4},{4,5},{5,6},{6,7},{7,8},{8,9},{9,10},{10,1... | collective-permute-start | bytes 98312 | tf_op jit(solution)/shard_map/ppermute | solution.py:23
  118.8 8.9 %collective-permute-start.7 = (f32[32,256]{1,0:T(8,128)S(1)}, f32[32,256]{1,0:T(8,128)S(1)}, u32[]{:S(2)}, u32[]{:S(2)}) collective-permute-start(f32[32,256]{1,0:T(8,128)S(1)} %get-tuple-element.815), channel_id=1, source_target_pairs={{1,0},{2,1},{3,2},{4,3},{5,4},{6,5},{7,6},{8,7},{9,8},{10,9},{11,1... | collective-permute-start | bytes 98312 | tf_op jit(solution)/shard_map/ppermute | solution.py:25
  153.0 9.2 %copy-start.15 = (f32[256,256]{0,1:T(8,128)}, f32[256,256]{0,1:T(8,128)S(1)}, u32[]{:S(2)}) copy-start(f32[256,256]{0,1:T(8,128)S(1)} %get-tuple-element.867) | copy-start | bytes 786436
  174.0 9.8 %copy-start.3 = (f32[32,2048]{0,1:T(8,128)}, f32[32,2048]{0,1:T(8,128)S(1)}, u32[]{:S(2)}) copy-start(f32[32,2048]{0,1:T(8,128)S(1)} %scatter_custom_fusion) | copy-start | bytes 786436
  174.0 8.7 %copy-start.47 = (f32[1,4,4,4,256]{4,2,1,3,0:T(4,128)S(1)}, f32[1,4,4,4,256]{4,2,1,3,0:T(4,128)}, u32[]{:S(2)}) copy-start(f32[1,4,4,4,256]{4,2,1,3,0:T(4,128)} %pad_bitcast_fusion.70) | copy-start | bytes 196612
  174.0 8.7 %copy-start.50 = (f32[1,4,4,4,256]{4,2,1,3,0:T(4,128)S(1)}, f32[1,4,4,4,256]{4,2,1,3,0:T(4,128)}, u32[]{:S(2)}) copy-start(f32[1,4,4,4,256]{4,2,1,3,0:T(4,128)} %pad_bitcast_fusion.69) | copy-start | bytes 196612
  174.0 8.7 %copy-start.53 = (f32[1,4,4,4,256]{4,2,1,3,0:T(4,128)S(1)}, f32[1,4,4,4,256]{4,2,1,3,0:T(4,128)}, u32[]{:S(2)}) copy-start(f32[1,4,4,4,256]{4,2,1,3,0:T(4,128)} %pad_bitcast_fusion.68) | copy-start | bytes 196612
  174.0 8.7 %copy-start.56 = (f32[1,4,4,4,256]{4,2,1,3,0:T(4,128)S(1)}, f32[1,4,4,4,256]{4,2,1,3,0:T(4,128)}, u32[]{:S(2)}) copy-start(f32[1,4,4,4,256]{4,2,1,3,0:T(4,128)} %pad_bitcast_fusion.67) | copy-start | bytes 196612
  174.1 8.7 %copy-start.59 = (f32[1,4,4,4,256]{4,2,1,3,0:T(4,128)S(1)}, f32[1,4,4,4,256]{4,2,1,3,0:T(4,128)}, u32[]{:S(2)}) copy-start(f32[1,4,4,4,256]{4,2,1,3,0:T(4,128)} %pad_bitcast_fusion.66) | copy-start | bytes 196612
  174.1 8.7 %copy-start.62 = (f32[1,4,4,4,256]{4,2,1,3,0:T(4,128)S(1)}, f32[1,4,4,4,256]{4,2,1,3,0:T(4,128)}, u32[]{:S(2)}) copy-start(f32[1,4,4,4,256]{4,2,1,3,0:T(4,128)} %pad_bitcast_fusion.65) | copy-start | bytes 196612
  174.1 8.7 %copy-start.65 = (f32[1,4,4,4,256]{4,2,1,3,0:T(4,128)S(1)}, f32[1,4,4,4,256]{4,2,1,3,0:T(4,128)}, u32[]{:S(2)}) copy-start(f32[1,4,4,4,256]{4,2,1,3,0:T(4,128)} %pad_bitcast_fusion.64) | copy-start | bytes 196612
  174.1 8.7 %copy-start.68 = (f32[1,4,4,4,256]{4,2,1,3,0:T(4,128)S(1)}, f32[1,4,4,4,256]{4,2,1,3,0:T(4,128)}, u32[]{:S(2)}) copy-start(f32[1,4,4,4,256]{4,2,1,3,0:T(4,128)} %pad_bitcast_fusion.63) | copy-start | bytes 196612
  174.8 10.0 %collective-permute-start.8 = (f32[32,256]{0,1:T(8,128)}, f32[32,256]{0,1:T(8,128)}, u32[]{:S(2)}, u32[]{:S(2)}) collective-permute-start(f32[32,256]{0,1:T(8,128)} %get-tuple-element.647), channel_id=1, source_target_pairs={{0,1},{1,2},{2,3},{3,4},{4,5},{5,6},{6,7},{7,8},{8,9},{9,10},{10,1... | collective-permute-start | bytes 98312 | tf_op jit(solution)/shard_map/ppermute | solution.py:23
  174.8 11.0 %collective-permute-start.9 = (f32[32,256]{0,1:T(8,128)}, f32[32,256]{0,1:T(8,128)}, u32[]{:S(2)}, u32[]{:S(2)}) collective-permute-start(f32[32,256]{0,1:T(8,128)} %get-tuple-element.648), channel_id=1, source_target_pairs={{1,0},{2,1},{3,2},{4,3},{5,4},{6,5},{7,6},{8,7},{9,8},{10,9},{11,1... | collective-permute-start | bytes 98312 | tf_op jit(solution)/shard_map/ppermute | solution.py:25
  184.0 2.9 slice-start
  227.1 10.2 %copy-start.5 = (f32[32,2048]{0,1:T(8,128)}, f32[32,2048]{0,1:T(8,128)S(1)}, u32[]{:S(2)}) copy-start(f32[32,2048]{0,1:T(8,128)S(1)} %scatter_custom_fusion.2) | copy-start | bytes 786436
  227.1 8.7 %copy-start.13 = (f32[256,256]{0,1:T(8,128)S(1)}, f32[256,256]{0,1:T(8,128)}, u32[]{:S(2)}) copy-start(f32[256,256]{0,1:T(8,128)} %get-tuple-element.869) | copy-start | bytes 786436
  227.1 8.7 %copy-start.19 = (f32[256,256]{1,0:T(8,128)S(1)}, f32[256,256]{1,0:T(8,128)}, u32[]{:S(2)}) copy-start(f32[256,256]{1,0:T(8,128)} %fusion.292) | copy-start | bytes 786436
  227.8 9.8 %collective-permute-start.10 = (f32[32,256]{0,1:T(8,128)}, f32[32,256]{0,1:T(8,128)}, u32[]{:S(2)}, u32[]{:S(2)}) collective-permute-start(f32[32,256]{0,1:T(8,128)} %get-tuple-element.645), channel_id=1, source_target_pairs={{0,1},{1,2},{2,3},{3,4},{4,5},{5,6},{6,7},{7,8},{8,9},{9,10},{10,1... | collective-permute-start | bytes 98312 | tf_op jit(solution)/shard_map/ppermute | solution.py:23
  227.8 10.7 %collective-permute-start.11 = (f32[32,256]{0,1:T(8,128)}, f32[32,256]{0,1:T(8,128)}, u32[]{:S(2)}, u32[]{:S(2)}) collective-permute-start(f32[32,256]{0,1:T(8,128)} %get-tuple-element.646), channel_id=1, source_target_pairs={{1,0},{2,1},{3,2},{4,3},{5,4},{6,5},{7,6},{8,7},{9,8},{10,9},{11,1... | collective-permute-start | bytes 98312 | tf_op jit(solution)/shard_map/ppermute | solution.py:25
  275.5 10.6 %copy-start.4 = (f32[32,2048]{0,1:T(8,128)}, f32[32,2048]{0,1:T(8,128)S(1)}, u32[]{:S(2)}) copy-start(f32[32,2048]{0,1:T(8,128)S(1)} %scatter_custom_fusion.4) | copy-start | bytes 786436
  275.5 9.3 %copy-start.21 = (f32[256,256]{1,0:T(8,128)S(1)}, f32[256,256]{1,0:T(8,128)}, u32[]{:S(2)}) copy-start(f32[256,256]{1,0:T(8,128)} %convolution_add_fusion.5) | copy-start | bytes 786436
  276.3 10.2 %collective-permute-start.12 = (f32[32,256]{0,1:T(8,128)}, f32[32,256]{0,1:T(8,128)}, u32[]{:S(2)}, u32[]{:S(2)}) collective-permute-start(f32[32,256]{0,1:T(8,128)} %get-tuple-element.643), channel_id=1, source_target_pairs={{0,1},{1,2},{2,3},{3,4},{4,5},{5,6},{6,7},{7,8},{8,9},{9,10},{10,1... | collective-permute-start | bytes 98312 | tf_op jit(solution)/shard_map/ppermute | solution.py:23
  276.3 11.2 %collective-permute-start.13 = (f32[32,256]{0,1:T(8,128)}, f32[32,256]{0,1:T(8,128)}, u32[]{:S(2)}, u32[]{:S(2)}) collective-permute-start(f32[32,256]{0,1:T(8,128)} %get-tuple-element.644), channel_id=1, source_target_pairs={{1,0},{2,1},{3,2},{4,3},{5,4},{6,5},{7,6},{8,7},{9,8},{10,9},{11,1... | collective-permute-start | bytes 98312 | tf_op jit(solution)/shard_map/ppermute | solution.py:25
  559.0 5.5 copy-start.18
  (104 other events, 107.5 us)
Sparse Core Ops, SparseCore 0:
  302.9 256.1 all-reduce.267
where the time goes:
time: 586 us; the launch traced here: 575 us
  waiting for transfers between devices  169 us (29%)
  local copies, waits for them, and re-layouts  125 us (21%)
  blocking collectives  85.3 us (15%)
  other arithmetic  77.3 us (13%)
  starting transfers between devices  52.2 us (9%)
  matrix products  40.7 us (7%)
  between operations  24.8 us (4%)
    psum x1, waiting for transfers between devices, local(): lax.psum((gradients[0], gradients[1], gradients[2], gradients[3], loss_me...  168 us
    psum x1, blocking collectives, local(): loss_total = lax.psum(loss_part, 'mesh')  85.3 us
    ppermute x7, starting transfers between devices, padded(): lax.ppermute(head, axis, [((i + 1) % count, i) for i in range(count)])  51.9 us
    dot_general x65, matrix products, matmul(): jnp.dot(left, right, precision=HIGH, preferred_element_type=jnp.float32)  40.7 us
    unnamed x314, local copies, waits for them, and re-layouts  34.1 us
    scatter-add x3, other arithmetic, adjoint_rhs(): grad_table = jnp.zeros((grad_outside.shape[0], own_columns + 2 * halo_wid...  27.9 us
    gather x8, local copies, waits for them, and re-layouts, exterior(): return table[:, nbr_flat]  20.9 us
    scatter-add x16, other arithmetic, local_rhs(): result.at[face_index(0, face)]  15.9 us
  transfers between devices with their start and end apart: 15, of which 6 were waited for; matrix products, arithmetic and copies ran while one was open for 3% of the time, Pallas kernels for 0%

commit v1 on v0

v1 whole, which is shorter than its diff:
```python
import functools

import jax
import jax.numpy as jnp
import ml_dtypes
import numpy as np
from jax import lax
from jax.experimental import pallas as pl
from jax.experimental.pallas import tpu as pltpu
from jax.sharding import Mesh, PartitionSpec as P

AXES = ("x", "y", "z", "core")
PLANE = ("x", "y")
SIZES = (4, 4, 8, 2)
DEVICES = 256
WIDTH = 256
COUNT = 16777216.0
PARAMS = 131584.0
TIME_STEP = 0.05
HALF_STEP = 0.025
TINY = 1e-20
F32 = jnp.float32
BF16 = jnp.bfloat16


def face_rows(face):
    layer = 0 if face % 2 == 0 else 3
    grid = np.arange(64).reshape(4, 4, 4)
    return np.take(grid, layer, axis=face // 2).reshape(16)


def operators():
    points = np.array([-1.0, -1.0 / np.sqrt(5.0), 1.0 / np.sqrt(5.0), 1.0])
    bary = np.array(
        [1.0 / np.prod([points[m] - points[n] for n in range(4) if n != m]) for m in range(4)]
    )
    deriv = np.zeros((4, 4))
    for m in range(4):
        for n in range(4):
            if m != n:
                deriv[m, n] = bary[n] / bary[m] / (points[m] - points[n])
        deriv[m, m] = -np.sum(deriv[m])
    eye = np.eye(4)
    tables = [
        np.kron(np.kron(deriv, eye), eye),
        np.kron(np.kron(eye, deriv), eye),
        np.kron(eye, np.kron(eye, deriv)),
    ]
    inner = np.zeros((256, 256))
    for a in range(3):
        inner[0:64, 64 * (a + 1) : 64 * (a + 2)] -= tables[a]
        inner[64 * (a + 1) : 64 * (a + 2), 0:64] -= tables[a]
    for face in range(6):
        sign = 2.0 * (face % 2) - 1.0
        for row in face_rows(face):
            speed = 64 * (face // 2 + 1) + row
            inner[row, row] -= 3.0
            inner[row, speed] += 3.0 * sign
            inner[speed, speed] -= 3.0
            inner[speed, row] += 3.0 * sign
    leave = np.zeros((64, 256))
    lift = np.zeros((256, 64))
    for face in range(2, 6):
        sign = 2.0 * (face % 2) - 1.0
        base = 16 * (face - 2)
        for n, row in enumerate(face_rows(face ^ 1)):
            leave[base + n, row] = 3.0
            leave[base + n, 64 * (face // 2 + 1) + row] = -3.0 * sign
        for n, row in enumerate(face_rows(face)):
            lift[row, base + n] = 1.0
            lift[64 * (face // 2 + 1) + row, base + n] = -sign
    return inner, leave, lift


def halves(values):
    high = values.astype(ml_dtypes.bfloat16)
    low = (values - high.astype(np.float64)).astype(ml_dtypes.bfloat16)
    return np.stack([high, low])


def split(values):
    high = values.astype(BF16)
    return high, (values - high.astype(F32)).astype(BF16)


def mm(left, right):
    return jnp.dot(left, right, preferred_element_type=F32)


def mm_nt(left, right):
    return lax.dot_general(left, right, (((1,), (1,)), ((), ())), preferred_element_type=F32)


def mm3(left, right, dot=mm):
    return dot(left[0], right[0]) + (dot(left[0], right[1]) + dot(left[1], right[0]))


def pair(ref):
    return ref[0], ref[1]


def call(body, outs, *args, flops=2e8, name):
    specs = [
        pl.BlockSpec(memory_space=pltpu.SMEM)
        if a.shape == (1,)
        else pl.BlockSpec(memory_space=pltpu.VMEM)
        for a in args
    ]
    return list(pl.pallas_call(
        body,
        out_shape=[jax.ShapeDtypeStruct(s, t) for s, t in outs],
        in_specs=specs,
        out_specs=[pl.BlockSpec(memory_space=pltpu.VMEM)] * len(outs),
        cost_estimate=pl.CostEstimate(flops=int(flops), bytes_accessed=2000000, transcendentals=0),
        compiler_params=pltpu.CompilerParams(vmem_limit_bytes=24 * 1024 * 1024),
        name=name,
    )(*args))


SQUARE = ((256, 256), F32)
PAIR = ((2, 256, 256), BF16)
EDGE = ((16, 256), F32)
EXTRA = ((8, 256), F32)


def edges(values):
    return values[0:16], values[48:64], values[64:80], values[112:128]


def leaving(values):
    p_low, p_high, u_low, u_high = edges(values)
    return 3.0 * (p_high + u_high), 3.0 * (p_low - u_low)


def put(parity, upward, downward, in_chip_ref, cross_ref):
    even = parity == 0
    in_chip_ref[0:16] = jnp.where(even, upward, downward)
    cross_ref[0:16] = jnp.where(even, downward, upward)


def take(parity, in_chip, cross):
    even = parity == 0
    return jnp.where(even, cross, in_chip), jnp.where(even, in_chip, cross)


def pick(values, table, dot=mm):
    both = dot(jnp.concatenate(split(values), axis=0), table)
    return both[0:16] + both[16:32]


def add_edges(values_ref, first, second, third, fourth):
    values_ref[0:16] += first
    values_ref[48:64] += second
    values_ref[64:80] += third
    values_ref[112:128] += fourth


def first_kernel(parity_ref, state_ref, send_ref, in_chip_ref, cross_ref):
    upward, downward = leaving(state_ref)
    parity = parity_ref[0]
    put(parity, upward, downward, in_chip_ref, cross_ref)
    down_index = send_ref[0:1].astype(F32)
    up_index = (send_ref[1:2] - 256).astype(F32)
    even = parity == 0
    in_chip_ref[16:24] = jnp.broadcast_to(jnp.where(even, up_index, down_index), (8, 256))
    cross_ref[16:24] = jnp.broadcast_to(jnp.where(even, down_index, up_index), (8, 256))


def setup_kernel(w_in_ref, w_out_ref, nbr_ref, in_ref, out_ref, in_t_ref, out_t_ref, near_ref, far_ref):
    for source, ref, ref_t in ((w_in_ref, in_ref, in_t_ref), (w_out_ref, out_ref, out_t_ref)):
        values = source[...]
        ref[0], ref[1] = split(values)
        ref_t[0], ref_t[1] = split(values.T)
    rows = lax.broadcasted_iota(jnp.int32, (256, 256), 0)
    for face in range(6):
        column = nbr_ref[face : face + 1]
        if face < 2:
            far_ref[face] = (rows + (1536 + 256 * face) == column).astype(F32).astype(BF16)
        else:
            near_ref[face - 2] = (rows + 256 * (face ^ 1) == column).astype(F32).astype(BF16)


def local_rates(values, w_in, b_in, w_out, b_out, inner, leave, lift, near, hidden_ref):
    parts = split(values)
    hidden = jnp.tanh(mm3(w_in, parts) + b_in)
    hidden_ref[...] = hidden
    rates = mm3(inner, parts) + b_out
    out = mm(leave, parts[0]) + mm(leave, parts[1])
    high, low = split(out)
    arrived = []
    for n in range(4):
        both = jnp.concatenate([high[16 * n : 16 * n + 16], low[16 * n : 16 * n + 16]], axis=0)
        arrived.append(mm(both, near[n]).astype(BF16))
    for part in range(2):
        rates += mm(lift, jnp.concatenate([a[16 * part : 16 * part + 16] for a in arrived], axis=0))
    return rates + mm3(w_out, split(hidden))


def forward_kernel(stage, *refs):
    refs = list(refs)
    parity = refs.pop(0)[0]
    base_ref = refs.pop(0)
    if stage % 2 == 1:
        before_ref = refs.pop(0)
    if stage > 0:
        in_chip, cross = refs.pop(0), refs.pop(0)
        far_ref = refs.pop(0)
    w_in, b_in, w_out, b_out, inner, leave, lift, near = refs[:8]
    refs = refs[8:]
    if stage > 0:
        now_ref = refs.pop(0)
    if stage == 1:
        link_ref = refs.pop(0)
    next_ref, hidden_ref = refs[:2]
    refs = refs[2:]
    if stage == 0:
        values = base_ref[...]
    else:
        below, above = take(parity, in_chip[...], cross[...])
        if stage == 1:
            rows = lax.broadcasted_iota(jnp.int32, (256, 256), 0).astype(F32)
            for side, received in enumerate((below, above)):
                chosen = (rows == received[16:17]).astype(F32).astype(BF16)
                link_ref[side] = mm(chosen, far_ref[side]).astype(BF16)
            far_ref = link_ref
        weight = TIME_STEP if stage % 2 == 1 else HALF_STEP
        low = weight * pick(below[0:16], far_ref[0])
        high = weight * pick(above[0:16], far_ref[1])
        now_ref[...] = base_ref[...]
        add_edges(now_ref, low, high, low, -high)
        values = now_ref[...]
    rates = local_rates(
        values, pair(w_in), b_in[...], pair(w_out), b_out[...], pair(inner), leave[...], lift[...], near, hidden_ref
    )
    if stage % 2 == 0:
        next_ref[...] = values + TIME_STEP * rates
    else:
        next_ref[...] = 0.5 * (before_ref[...] + values) + HALF_STEP * rates
    if stage < 3:
        upward, downward = leaving(next_ref)
        put(parity, upward, downward, *refs)


def sensitivities(values, link):
    p_low, p_high, u_low, u_high = edges(values)
    return pick(p_high - u_high, link[1], mm_nt), pick(p_low + u_low, link[0], mm_nt)


def turn_kernel(parity_ref, base_ref, in_chip, cross, link, target_ref, final_ref, adjoint_ref, loss_ref, in_chip_out, cross_out):
    parity = parity_ref[0]
    below, above = take(parity, in_chip[...], cross[...])
    low = HALF_STEP * pick(below, link[0])
    high = HALF_STEP * pick(above, link[1])
    final_ref[...] = base_ref[...]
    add_edges(final_ref, low, high, low, -high)
    mismatch = final_ref[...] - target_ref[...]
    adjoint_ref[...] = (HALF_STEP / COUNT) * mismatch
    loss_ref[...] = jnp.broadcast_to(jnp.sum(mismatch * mismatch, axis=0, keepdims=True), (8, 256))
    upward, downward = sensitivities(adjoint_ref, link)
    put(parity, upward, downward, in_chip_out, cross_out)


def backward_kernel(stage, *refs):
    refs = list(refs)
    parity = refs.pop(0)[0]
    base_ref = refs.pop(0)
    if stage < 3:
        in_chip, cross = refs.pop(0), refs.pop(0)
    if stage == 2:
        after_ref = refs.pop(0)
    state_ref, hidden_ref = refs[:2]
    refs = refs[2:]
    if stage > 0:
        w_in_t, w_out_t, inner_t, leave_t, lift_t, near, link = refs[:7]
        refs = refs[7:]
    else:
        w_out_t = refs.pop(0)
    if stage < 3:
        old_in, old_out, old_extra = refs[:3]
        refs = refs[3:]
    if stage == 0:
        loss_ref, keep_ref, send_ref, now_ref = refs
    else:
        grad_in, grad_out, extra = refs[:3]
        refs = refs[3:]
        next_ref = refs.pop(0)
        if stage < 3:
            now_ref = refs.pop(0)
    if stage < 3:
        weight = 3.0 * (HALF_STEP if stage == 1 else TIME_STEP)
        below, above = take(parity, in_chip[...], cross[...])
        low, high = weight * below, weight * above
        now_ref[...] = base_ref[...]
        add_edges(now_ref, low, high, -low, high)
        values = now_ref[...]
    else:
        values = base_ref[...]
    parts = split(values)
    hidden = hidden_ref[...]
    delta = (1.0 - hidden * hidden) * mm3(pair(w_out_t), parts)
    delta_parts = split(delta)
    if stage > 0:
        rates = mm3(pair(inner_t), parts) + mm3(pair(w_in_t), delta_parts)
        high, low = split(mm(lift_t[...], parts[0]) + mm(lift_t[...], parts[1]))
        arrived = []
        for n in range(4):
            both = jnp.concatenate([high[16 * n : 16 * n + 16], low[16 * n : 16 * n + 16]], axis=0)
            arrived.append(mm_nt(both, near[n]))
        high, low = split(jnp.concatenate([a[0:16] + a[16:32] for a in arrived], axis=0))
        rates += mm(leave_t[...], high) + mm(leave_t[...], low)
        if stage == 2:
            next_ref[...] = 0.5 * (after_ref[...] + values) + HALF_STEP * rates
        else:
            next_ref[...] = values + TIME_STEP * rates
        if stage > 1:
            upward, downward = sensitivities(next_ref, link)
            put(parity, upward, downward, *refs)
    ones = jnp.ones((8, 256), BF16)
    first_bias = mm_nt(ones, delta_parts[0]) + mm_nt(ones, delta_parts[1])
    second_bias = mm_nt(ones, parts[0]) + mm_nt(ones, parts[1])
    rows = lax.broadcasted_iota(jnp.int32, (8, 256), 0)
    bias = jnp.where(rows == 0, first_bias, second_bias)
    first = mm3(delta_parts, split(state_ref[...]), mm_nt)
    second = mm3(parts, split(hidden), mm_nt)
    if stage < 3:
        first += old_in[...]
        second += old_out[...]
        bias += old_extra[...]
    if stage > 0:
        grad_in[...] = first
        grad_out[...] = second
        extra[...] = bias
    else:
        even = parity == 0
        keep_ref[0:256] = jnp.where(even, first, second)
        send_ref[0:256] = jnp.where(even, second, first)
        bias = jnp.where(rows == 2, loss_ref[...], bias)
        keep_ref[256:264] = bias
        send_ref[256:264] = bias


def chip_kernel(keep_ref, got_ref, out_ref):
    for n in range(16):
        out_ref[n, 0:16] = keep_ref[16 * n : 16 * n + 16] + got_ref[16 * n : 16 * n + 16]
        out_ref[n, 16:24] = keep_ref[256:264] + got_ref[256:264]


def plane_kernel(parts_ref, out_ref):
    total = jnp.sum(parts_ref[...], axis=0)
    for n in range(8):
        out_ref[n] = total


def line_kernel(parts_ref, out_ref, extra_ref):
    total = jnp.sum(parts_ref[...], axis=0)
    extra_ref[...] = total[16:24]
    for n in range(16):
        out_ref[n] = total[0:16]


def last_kernel(parity_ref, own_ref, other_ref, extra_ref, in_ref, b_in_ref, out_ref, b_out_ref, loss_ref):
    even = parity_ref[0] == 0
    own, other = own_ref[...], other_ref[...]
    first = jnp.where(even, own, other)
    second = jnp.where(even, other, own)
    bias = extra_ref[0:2]
    total = jnp.sum(first * first + second * second, keepdims=True) + jnp.sum(bias * bias, keepdims=True)
    scale = lax.rsqrt(total / PARAMS + TINY)
    in_ref[...] = first * scale
    out_ref[...] = second * scale
    b_in_ref[...] = extra_ref[0:1] * scale
    b_out_ref[...] = extra_ref[1:2] * scale
    loss_ref[...] = jnp.sum(extra_ref[2:3], keepdims=True) * (0.5 / COUNT)


IN_CHIP = [(n, n ^ 1) for n in range(DEVICES)]
CROSS = [(n, (n - 1) % DEVICES if n % 2 == 0 else (n + 1) % DEVICES) for n in range(DEVICES)]


def exchange(in_chip, cross):
    return lax.ppermute(in_chip, AXES, IN_CHIP), lax.ppermute(cross, AXES, CROSS)


def local(state, target, w_in, b_in, w_out, b_out, nbr, send):
    parity = lax.axis_index("core").reshape(1)
    inner, leave, lift = operators()
    one = lambda values: jnp.asarray(values.astype(ml_dtypes.bfloat16))
    two = lambda values: jnp.asarray(halves(values))
    b_in, b_out = b_in.reshape(256, 1), b_out.reshape(256, 1)

    first = call(first_kernel, [((24, 256), F32)] * 2, parity, state, send, name="traces")
    got = [exchange(*first)]
    w_in2, w_out2, w_in_t, w_out_t, near, far = call(
        setup_kernel, [PAIR] * 4 + [((4, 256, 256), BF16), PAIR], w_in, w_out, nbr, name="tables"
    )
    network = (w_in2, b_in, w_out2, b_out, two(inner), one(leave), one(lift), near)
    states, hiddens = [state], []
    base = state
    for stage in range(4):
        args = [parity, base]
        outs = [SQUARE, SQUARE] + ([EDGE, EDGE] if stage < 3 else [])
        if stage % 2 == 1:
            args.append(states[-1])
        if stage > 0:
            args += [*got[stage - 1], far if stage == 1 else link]
            outs = [SQUARE] + ([PAIR] if stage == 1 else []) + outs
        res = call(functools.partial(forward_kernel, stage), outs, *args, *network, name=f"forward{stage}")
        if stage > 0:
            states.append(res.pop(0))
        if stage == 1:
            link = res.pop(0)
        base = res.pop(0)
        hiddens.append(res.pop(0))
        if stage < 3:
            got.append(exchange(*res))
    final, adjoint, loss, *edge = call(
        turn_kernel, [SQUARE, SQUARE, EXTRA, EDGE, EDGE], parity, base, *got[3], link, target, name="turn"
    )
    got = {2: exchange(*edge)}
    back = (w_in_t, w_out_t, two(inner.T), one(leave.T), one(lift.T), near, link)
    grads = []
    base = adjoint
    for stage in (3, 2, 1):
        args = [parity, base]
        outs = [SQUARE, SQUARE, EXTRA, SQUARE]
        if stage < 3:
            args += got[stage]
            outs.append(SQUARE)
        if stage == 2:
            args.append(adjoint)
        if stage > 1:
            outs += [EDGE, EDGE]
        res = call(
            functools.partial(backward_kernel, stage),
            outs, *args, states[stage], hiddens[stage], *back, *grads, name=f"backward{stage}",
        )
        grads = res[:3]
        base = res[3]
        if stage > 1:
            got[stage - 2] = exchange(*res[-2:])
    keep, give, _ = call(
        functools.partial(backward_kernel, 0),
        [((264, 256), F32)] * 2 + [SQUARE],
        parity, base, *got[0], states[0], hiddens[0], w_out_t, *grads, loss, name="backward0",
    )
    swap = [(0, 1), (1, 0)]
    (parts,) = call(chip_kernel, [((16, 24, 256), F32)], keep, lax.ppermute(give, "core", swap), name="chip_sum")
    parts = lax.all_to_all(parts, PLANE, 0, 0, tiled=True)
    (parts,) = call(plane_kernel, [((8, 24, 256), F32)], parts, name="plane_sum")
    parts = lax.all_to_all(parts, "z", 0, 0, tiled=True)
    parts, extra = call(line_kernel, [((16, 16, 256), F32), EXTRA], parts, name="line_sum")
    own = lax.all_to_all(parts, PLANE, 0, 0, tiled=True).reshape(256, 256)
    other = lax.ppermute(own, "core", swap)
    row = ((1, 256), F32)
    step_in, step_b_in, step_out, step_b_out, loss = call(
        last_kernel, [SQUARE, row, SQUARE, row, ((1, 1), F32)], parity, own, other, extra, name="scale"
    )
    return final, loss.reshape(()), step_in, step_b_in.reshape(256), step_out, step_b_out.reshape(256)


def solution(mesh):
    split_mesh = Mesh(mesh.devices.reshape(SIZES), AXES)
    whole = P(None, AXES)
    return jax.shard_map(
        local,
        mesh=split_mesh,
        in_specs=(whole, whole, P(), P(), P(), P(), whole, whole),
        out_specs=(whole, P(), P(), P(), P(), P()),
        check_vma=False,
    )
```

time: 586 us -> 99.3 us (0.17); the launches traced: 575 us -> 99 us
  waiting for transfers between devices: 169 us -> 5.54 us
  local copies, waits for them, and re-layouts: 125 us -> 2.61 us
  other arithmetic: 77.3 us -> 0 us
  blocking collectives: 85.3 us -> 33.7 us
  matrix products: 40.7 us -> 0 us
  between operations: 24.8 us -> 0.88 us
  Pallas kernels: 0 us -> 13.4 us
  starting transfers between devices: 52.2 us -> 42.9 us
    psum x1 -> x0, waiting for transfers between devices: 168 us -> none  [local(): lax.psum((gradients[0], gradients[1], gradients[2], gradients[3], loss_me...]
    psum x1 -> x0, blocking collectives: 85.3 us -> none  [local(): loss_total = lax.psum(loss_part, 'mesh')]
    scatter-add x38 -> x0, other arithmetic: 55.1 us -> none  [the longest x3 27.9 us: adjoint_rhs(): grad_table = jnp.zeros((grad_outside.shape[0], own_columns + 2 * halo_wid...]
    dot_general x65 -> x0, matrix products: 40.7 us -> none  [matmul(): jnp.dot(left, right, precision=HIGH, preferred_element_type=jnp.float32)]
    all_to_all x0 -> x3, blocking collectives: none -> 33.7 us  [the longest x1 11.9 us: local(): parts = lax.all_to_all(parts, PLANE, 0, 0, tiled=True)]
    unnamed x314 -> x30, local copies, waits for them, and re-layouts: 34.1 us -> 2.35 us
    gather x16 -> x0, local copies, waits for them, and re-layouts: 25.5 us -> none  [the longest x8 20.9 us: exterior(): return table[:, nbr_flat]]
    broadcast_in_dim x72 -> x0, local copies, waits for them, and re-layouts: 22.1 us -> none  [the longest x36 11.1 us: traces(): normal_speed = face_part(blocks[1 + face // 2], face)]
  transfers between devices with their start and end apart: 15 -> 16, of which waited for: 6 -> 4; matrix products, arithmetic and copies ran while one was open for 3% -> 0% of each run, Pallas kernels for 0% -> 11%
where the time goes in v1:
time: 99.3 us; the launch traced here: 99 us
  starting transfers between devices  42.9 us (43%)
  blocking collectives  33.7 us (34%)
  Pallas kernels  13.4 us (13%)
  waiting for transfers between devices  5.54 us (6%)
  local copies, waits for them, and re-layouts  2.61 us (3%)
    ppermute x7, starting transfers between devices, exchange(): lax.ppermute(in_chip, AXES, IN_CHIP)  31.2 us
    pallas_call x15, Pallas kernels, call(): pl.pallas_call(body, out_shape=[jax.ShapeDtypeStruct(s, t) for s, t in ou...  13.4 us
    all_to_all x1, blocking collectives, local(): parts = lax.all_to_all(parts, PLANE, 0, 0, tiled=True)  11.9 us
    all_to_all x1, blocking collectives, local(): own = lax.all_to_all(parts, PLANE, 0, 0, tiled=True).reshape(256, 256)  11 us
    all_to_all x1, blocking collectives, local(): parts = lax.all_to_all(parts, 'z', 0, 0, tiled=True)  10.8 us
    ppermute x1, starting transfers between devices, local(): lax.ppermute(give, 'core', swap)  5.62 us
    ppermute x1, starting transfers between devices, local(): other = lax.ppermute(own, 'core', swap)  4.27 us
    ppermute x7, waiting for transfers between devices, exchange(): lax.ppermute(cross, AXES, CROSS)  3.18 us
  transfers between devices with their start and end apart: 16, of which 4 were waited for; matrix products, arithmetic and copies ran while one was open for 0% of the time, Pallas kernels for 11%

profile of v1, /device:TPU:1, one launch (start us, length us, event | category | flops | bytes accessed | tf_op | source)
XLA Modules:
  0.0 99.0 jit_solution(9666339759397271467)
XLA Ops:
  0.6 0.7 copy-done.12
  1.3 0.9 copy-done.1
  2.3 3.3 %collective-permute-start = (f32[24,256]{1,0:T(8,128)S(1)}, f32[24,256]{1,0:T(8,128)S(1)}, u32[]{:S(2)}, u32[]{:S(2)}) collective-permute-start(f32[24,256]{1,0:T(8,128)S(1)} %get-tuple-element.66), channel_id=1, source_target_pairs={{0,1},{1,0},{2,3},{3,2},{4,5},{5,4},{6,7},{7,6},{8,9},{9,8},{10,11... | collective-permute-start | bytes 73736 | tf_op jit(solution)/shard_map/ppermute | solution.py:381
  5.6 0.0 collective-permute-start.1
  5.6 0.0 copy-start.13
  5.7 0.0 copy-start.14
  5.7 0.0 copy-start.2
  5.7 0.0 copy-start.4
  5.7 0.0 copy-start.6
  5.7 0.4 tables.1
  6.1 0.0 copy-start
  6.1 0.2 copy-done.13
  6.3 0.1 copy.20.refs_3_.refs_7_.refs_6_
  6.5 0.1 copy.21.refs_5_.refs_9_.refs_8_
  6.6 0.0 copy-done.2
  6.6 0.4 copy-done
  7.1 1.2 %forward0.1 = (f32[256,256]{1,0:T(8,128)S(1)}, f32[256,256]{1,0:T(8,128)S(1)}, f32[16,256]{1,0:T(8,128)S(1)}, f32[16,256]{1,0:T(8,128)S(1)}) custom-call(s32[1]{0:T(128)} %bitcast.refs_0_.parity_ref, f32[256,256]{1,0:T(8,128)S(1)} %copy-done.2, bf16[2,256,256]{2,1,0:T(8,128)(2,1)S(1)} %get-tuple-element.62.refs_2_.refs_6_.refs_5_, ...), custom_call_target="tpu_custom_call" | custom-call | flops 200000000 | bytes 2000000 | tf_op jit(solution)/shard_map/forward0/pallas_call | solution.py:109
  8.3 8.9 %collective-permute-start.2 = (f32[16,256]{1,0:T(8,128)S(1)}, f32[16,256]{1,0:T(8,128)S(1)}, u32[]{:S(2)}, u32[]{:S(2)}) collective-permute-start(f32[16,256]{1,0:T(8,128)S(1)} %get-tuple-element.70), channel_id=1, source_target_pairs={{0,1},{1,0},{2,3},{3,2},{4,5},{5,4},{6,7},{7,6},{8,9},{9,8},{10,11... | collective-permute-start | bytes 49160 | tf_op jit(solution)/shard_map/ppermute | solution.py:381
  17.2 1.5 %forward1.1 = (f32[256,256]{1,0:T(8,128)S(1)}, bf16[2,256,256]{2,1,0:T(8,128)(2,1)S(1)}, f32[256,256]{1,0:T(8,128)S(1)}, f32[256,256]{1,0:T(8,128)S(1)}, f32[16,256]{1,0:T(8,128)S(1)}, /*index=5*/f32[16,256]{1,0:T(8,128)S(1)}) custom-call(s32[1]{0:T(128)} %bitcast.refs_0_.parity_ref, f32[256,256]{1,0:T(8,128)S(1)} %get-tuple-element.65.refs_1_, ...), custom_call_target="tpu_custom_call" | custom-call | flops 200000000 | bytes 2000000 | tf_op jit(solution)/shard_map/forward1/pallas_call | solution.py:109
  18.8 1.2 %collective-permute-start.4 = (f32[16,256]{1,0:T(8,128)S(1)}, f32[16,256]{1,0:T(8,128)S(1)}, u32[]{:S(2)}, u32[]{:S(2)}) collective-permute-start(f32[16,256]{1,0:T(8,128)S(1)} %get-tuple-element.75), channel_id=1, source_target_pairs={{0,1},{1,0},{2,3},{3,2},{4,5},{5,4},{6,7},{7,6},{8,9},{9,8},{10,11... | collective-permute-start | bytes 49160 | tf_op jit(solution)/shard_map/ppermute | solution.py:381
  20.0 0.7 collective-permute-start.5
  20.7 0.0 collective-permute-done.2.refs_2_
  20.7 0.0 collective-permute-done.3.refs_3_
  20.7 1.4 %forward2.1 = (f32[256,256]{1,0:T(8,128)S(1)}, f32[256,256]{1,0:T(8,128)S(1)}, f32[256,256]{1,0:T(8,128)S(1)}, f32[16,256]{1,0:T(8,128)S(1)}, f32[16,256]{1,0:T(8,128)S(1)}) custom-call(s32[1]{0:T(128)} %bitcast.refs_0_.parity_ref, f32[256,256]{1,0:T(8,128)S(1)} %get-tuple-element.69.refs_1_, f32[16,256]{1,0:T(8,128)S(1)} %collective-permute-done.2.refs_2_, ...), custom_call_target="tpu_custom_call" | custom-call | flops 200000000 | bytes 2000000 | tf_op jit(solution)/shard_map/forward2/pallas_call | solution.py:109
  22.1 5.6 %collective-permute-start.6 = (f32[16,256]{1,0:T(8,128)S(1)}, f32[16,256]{1,0:T(8,128)S(1)}, u32[]{:S(2)}, u32[]{:S(2)}) collective-permute-start(f32[16,256]{1,0:T(8,128)S(1)} %get-tuple-element.78), channel_id=1, source_target_pairs={{0,1},{1,0},{2,3},{3,2},{4,5},{5,4},{6,7},{7,6},{8,9},{9,8},{10,11... | collective-permute-start | bytes 49160 | tf_op jit(solution)/shard_map/ppermute | solution.py:381
  27.7 0.0 collective-permute-done.5.refs_4_
  27.7 0.0 copy-start.8
  27.7 1.4 %forward3.1 = (f32[256,256]{1,0:T(8,128)S(1)}, f32[256,256]{1,0:T(8,128)S(1)}, f32[256,256]{1,0:T(8,128)S(1)}) custom-call(s32[1]{0:T(128)} %bitcast.refs_0_.parity_ref, f32[256,256]{1,0:T(8,128)S(1)} %get-tuple-element.73.refs_1_, f32[256,256]{1,0:T(8,128)S(1)} %get-tuple-element.74.refs_2_.refs_5_, f32[16,256]{1,0:T(8,128)S(1)} %collective-permute-done.4.refs_3_, ...), custom_call_target="tpu_custom_call" | custom-call | flops 200000000 | bytes 2000000 | tf_op jit(solution)/shard_map/forward3/pallas_call | solution.py:109
  29.1 1.8 %collective-permute-done.7.cross = f32[16,256]{1,0:T(8,128)S(1)} collective-permute-done((f32[16,256]{1,0:T(8,128)S(1)}, f32[16,256]{1,0:T(8,128)S(1)}, u32[]{:S(2)}, u32[]{:S(2)}) %collective-permute-start.7) | collective-permute-done | bytes 16416 | tf_op jit(solution)/shard_map/ppermute | solution.py:381
  30.9 0.9 turn.1
  31.7 5.5 %collective-permute-start.8 = (f32[16,256]{1,0:T(8,128)S(1)}, f32[16,256]{1,0:T(8,128)S(1)}, u32[]{:S(2)}, u32[]{:S(2)}) collective-permute-start(f32[16,256]{1,0:T(8,128)S(1)} %get-tuple-element.87), channel_id=1, source_target_pairs={{0,1},{1,0},{2,3},{3,2},{4,5},{5,4},{6,7},{7,6},{8,9},{9,8},{10,11... | collective-permute-start | bytes 49160 | tf_op jit(solution)/shard_map/ppermute | solution.py:381
  37.3 0.0 collective-permute-start.9
  37.3 1.4 %backward3.1 = (f32[256,256]{1,0:T(8,128)S(1)}, f32[256,256]{1,0:T(8,128)S(1)}, f32[8,256]{1,0:T(8,128)S(1)}, f32[256,256]{1,0:T(8,128)S(1)}, f32[16,256]{1,0:T(8,128)S(1)}, /*index=5*/f32[16,256]{1,0:T(8,128)S(1)}) custom-call(s32[1]{0:T(128)} %bitcast.refs_0_.parity_ref, f32[256,256]{1,0:T(8,128)S(1)} %get-tuple-element.81.refs_1_.refs_4_, ...), custom_call_target="tpu_custom_call" | custom-call | flops 200000000 | bytes 2000000 | tf_op jit(solution)/shard_map/backward3/pallas_call | solution.py:109
  38.7 1.1 %collective-permute-start.10 = (f32[16,256]{1,0:T(8,128)S(1)}, f32[16,256]{1,0:T(8,128)S(1)}, u32[]{:S(2)}, u32[]{:S(2)}) collective-permute-start(f32[16,256]{1,0:T(8,128)S(1)} %get-tuple-element.94), channel_id=1, source_target_pairs={{0,1},{1,0},{2,3},{3,2},{4,5},{5,4},{6,7},{7,6},{8,9},{9,8},{10,11... | collective-permute-start | bytes 49160 | tf_op jit(solution)/shard_map/ppermute | solution.py:381
  39.8 1.0 %collective-permute-start.11 = (f32[16,256]{1,0:T(8,128)S(1)}, f32[16,256]{1,0:T(8,128)S(1)}, u32[]{:S(2)}, u32[]{:S(2)}) collective-permute-start(f32[16,256]{1,0:T(8,128)S(1)} %get-tuple-element.95), channel_id=1, source_target_pairs={{0,255},{1,2},{2,1},{3,4},{4,3},{5,6},{6,5},{7,8},{8,7},{9,10},{10... | collective-permute-start | bytes 49160 | tf_op jit(solution)/shard_map/ppermute | solution.py:381
  40.8 1.4 %backward2.1 = (f32[256,256]{1,0:T(8,128)S(1)}, f32[256,256]{1,0:T(8,128)S(1)}, f32[8,256]{1,0:T(8,128)S(1)}, f32[256,256]{1,0:T(8,128)S(1)}, f32[256,256]{1,0:T...) custom-call(s32[1]{0:T(128)} %bitcast.refs_0_.parity_ref, f32[256,256]{1,0:T(8,128)S(1)} %get-tuple-element.86.refs_1_, ...), custom_call_target="tpu_custom_call" | custom-call | flops 200000000 | bytes 2000000 | tf_op jit(solution)/shard_map/backward2/pallas_call | solution.py:109
  42.3 5.5 %collective-permute-start.12 = (f32[16,256]{1,0:T(8,128)S(1)}, f32[16,256]{1,0:T(8,128)S(1)}, u32[]{:S(2)}, u32[]{:S(2)}) collective-permute-start(f32[16,256]{1,0:T(8,128)S(1)} %get-tuple-element.102), channel_id=1, source_target_pairs={{0,1},{1,0},{2,3},{3,2},{4,5},{5,4},{6,7},{7,6},{8,9},{9,8},{10,11... | collective-permute-start | bytes 49160 | tf_op jit(solution)/shard_map/ppermute | solution.py:381
  47.8 1.7 %backward1.1 = (f32[256,256]{1,0:T(8,128)S(1)}, f32[256,256]{1,0:T(8,128)S(1)}, f32[8,256]{1,0:T(8,128)S(1)}, f32[256,256]{1,0:T(8,128)S(1)}, f32[256,256]{1,0:T(8,128)}) custom-call(s32[1]{0:T(128)} %bitcast.refs_0_.parity_ref, f32[256,256]{1,0:T(8,128)S(1)} %get-tuple-element.93.refs_1_, f32[16,256]{1,0:T(8,128)S(1)} %collective-permute-done.10.refs_2_, ...), custom_call_target="tpu_custom_call" | custom-call | flops 200000000 | bytes 2000000 | tf_op jit(solution)/shard_map/backward1/pallas_call | solution.py:109
  49.5 1.4 %collective-permute-done.13.refs_3_ = f32[16,256]{1,0:T(8,128)S(1)} collective-permute-done((f32[16,256]{1,0:T(8,128)S(1)}, f32[16,256]{1,0:T(8,128)S(1)}, u32[]{:S(2)}, u32[]{:S(2)}) %collective-permute-start.13) | collective-permute-done | bytes 16416 | tf_op jit(solution)/shard_map/ppermute | solution.py:381
  51.0 0.9 backward0.1
  51.9 5.6 %collective-permute-start.14 = (f32[264,256]{1,0:T(8,128)S(1)}, f32[264,256]{1,0:T(8,128)S(1)}, u32[]{:S(2)}, u32[]{:S(2)}) collective-permute-start(f32[264,256]{1,0:T(8,128)S(1)} %get-tuple-element.110), channel_id=1, source_target_pairs={{0,1},{1,0},{2,3},{3,2},{4,5},{5,4},{6,7},{7,6},{8,9},{9,8},{10,11... | collective-permute-start | bytes 811016 | tf_op jit(solution)/shard_map/ppermute | solution.py:447
  57.5 1.2 %collective-permute-done.14.got_ref = f32[264,256]{1,0:T(8,128)S(1)} collective-permute-done((f32[264,256]{1,0:T(8,128)S(1)}, f32[264,256]{1,0:T(8,128)S(1)}, u32[]{:S(2)}, u32[]{:S(2)}) %collective-permute-start.14) | collective-permute-done | bytes 270368 | tf_op jit(solution)/shard_map/ppermute | solution.py:447
  58.7 11.9 %all_to_all.15.parts_ref = f32[16,24,256]{2,1,0:T(8,128)S(1)} all-to-all(f32[16,24,256]{2,1,0:T(8,128)S(1)} %chip_sum.1), channel_id=1, replica_groups=mesh['x'=4,'y'=4,'z'=8,'core'=2] {'x','y'}, dimensions={0} | all-to-all | bytes 786432 | tf_op jit(solution)/shard_map/all_to_all | solution.py:448
  70.7 10.8 %all_to_all.16.parts_ref = f32[8,24,256]{2,1,0:T(8,128)S(1)} all-to-all(f32[8,24,256]{2,1,0:T(8,128)S(1)} %plane_sum.1), channel_id=1, replica_groups=mesh['x'=4,'y'=4,'z'=8,'core'=2] {'z'}, dimensions={0} | all-to-all | bytes 393216 | tf_op jit(solution)/shard_map/all_to_all | solution.py:450
  81.5 11.0 %all_to_all.17 = f32[16,16,256]{2,1,0:T(8,128)S(1)} all-to-all(f32[16,16,256]{2,1,0:T(8,128)S(1)} %get-tuple-element.111), channel_id=1, replica_groups=mesh['x'=4,'y'=4,'z'=8,'core'=2] {'x','y'}, dimensions={0} | all-to-all | bytes 524288 | tf_op jit(solution)/shard_map/all_to_all | solution.py:452
  92.5 4.3 %collective-permute-start.15 = (f32[256,256]{1,0:T(8,128)S(1)}, f32[256,256]{1,0:T(8,128)S(1)}, u32[]{:S(2)}, u32[]{:S(2)}) collective-permute-start(f32[256,256]{1,0:T(8,128)S(1)} %bitcast.7), channel_id=1, source_target_pairs={{0,1},{1,0},{2,3},{3,2},{4,5},{5,4},{6,7},{7,6},{8,9},{9,8},{10,11... | collective-permute-start | bytes 786440 | tf_op jit(solution)/shard_map/ppermute | solution.py:453
  96.8 1.2 %collective-permute-done.15.other_ref = f32[256,256]{1,0:T(8,128)S(1)} collective-permute-done((f32[256,256]{1,0:T(8,128)S(1)}, f32[256,256]{1,0:T(8,128)S(1)}, u32[]{:S(2)}, u32[]{:S(2)}) %collective-permute-start.15) | collective-permute-done | bytes 262176 | tf_op jit(solution)/shard_map/ppermute | solution.py:453
  98.0 1.0 %scale.1 = (f32[256,256]{1,0:T(8,128)}, f32[1,256]{1,0:T(1,128)}, f32[256,256]{1,0:T(8,128)}, f32[1,256]{1,0:T(1,128)}, f32[1,1]{1,0:T(1,128)}) custom-call(s32[1]{0:T(128)} %bitcast.refs_0_.parity_ref, f32[256,256]{1,0:T(8,128)S(1)} %bitcast.8, f32[256,256]{1,0:T(8,128)S(1)} %collective-permute-done.15.other_ref, f32[8,256]{1,0:T(8,128)S(1)} %get-tuple-element.112.extra_ref), custom_call_target="tpu_custom_call" | custom-call | flops 200000000 | bytes 2000000 | tf_op jit(solution)/shard_map/scale/pallas_call | solution.py:109
  (34 shorter events, 0.2 us)
Async XLA Ops:
  0.6 0.7 copy-start.12
  1.3 0.9 copy-start.1
  2.3 3.4 %copy-start.9 = (f32[256,256]{1,0:T(8,128)S(1)}, f32[256,256]{1,0:T(8,128)}, u32[]{:S(2)}) copy-start(f32[256,256]{1,0:T(8,128)} %w_in_ref.1) | copy-start | bytes 786436
  2.3 3.4 %copy-start.10 = (f32[256,256]{1,0:T(8,128)S(1)}, f32[256,256]{1,0:T(8,128)}, u32[]{:S(2)}) copy-start(f32[256,256]{1,0:T(8,128)} %w_out_ref.1) | copy-start | bytes 786436
  2.3 3.4 %copy-start.11 = (s32[6,256]{1,0:T(8,128)S(1)}, s32[6,256]{1,0:T(8,128)}, u32[]{:S(2)}) copy-start(s32[6,256]{1,0:T(8,128)} %nbr_ref.1) | copy-start | bytes 18436
  2.3 14.9 %collective-permute-start = (f32[24,256]{1,0:T(8,128)S(1)}, f32[24,256]{1,0:T(8,128)S(1)}, u32[]{:S(2)}, u32[]{:S(2)}) collective-permute-start(f32[24,256]{1,0:T(8,128)S(1)} %get-tuple-element.66), channel_id=1, source_target_pairs={{0,1},{1,0},{2,3},{3,2},{4,5},{5,4},{6,7},{7,6},{8,9},{9,8},{10,11... | collective-permute-start | bytes 73736 | tf_op jit(solution)/shard_map/ppermute | solution.py:381
  5.6 11.6 %collective-permute-start.1 = (f32[24,256]{1,0:T(8,128)S(1)}, f32[24,256]{1,0:T(8,128)S(1)}, u32[]{:S(2)}, u32[]{:S(2)}) collective-permute-start(f32[24,256]{1,0:T(8,128)S(1)} %get-tuple-element.67), channel_id=1, source_target_pairs={{0,255},{1,2},{2,1},{3,4},{4,3},{5,6},{6,5},{7,8},{8,7},{9,10},{10... | collective-permute-start | bytes 73736 | tf_op jit(solution)/shard_map/ppermute | solution.py:381
  5.6 0.7 copy-start.13
  5.7 0.8 copy-start.14
  5.7 1.0 copy-start.2
  5.7 1.0 copy-start.4
  5.7 0.9 copy-start.6
  6.1 1.0 copy-start
  8.3 12.4 %collective-permute-start.2 = (f32[16,256]{1,0:T(8,128)S(1)}, f32[16,256]{1,0:T(8,128)S(1)}, u32[]{:S(2)}, u32[]{:S(2)}) collective-permute-start(f32[16,256]{1,0:T(8,128)S(1)} %get-tuple-element.70), channel_id=1, source_target_pairs={{0,1},{1,0},{2,3},{3,2},{4,5},{5,4},{6,7},{7,6},{8,9},{9,8},{10,11... | collective-permute-start | bytes 49160 | tf_op jit(solution)/shard_map/ppermute | solution.py:381
  17.2 3.5 %collective-permute-start.3 = (f32[16,256]{1,0:T(8,128)S(1)}, f32[16,256]{1,0:T(8,128)S(1)}, u32[]{:S(2)}, u32[]{:S(2)}) collective-permute-start(f32[16,256]{1,0:T(8,128)S(1)} %get-tuple-element.71), channel_id=1, source_target_pairs={{0,255},{1,2},{2,1},{3,4},{4,3},{5,6},{6,5},{7,8},{8,7},{9,10},{10... | collective-permute-start | bytes 49160 | tf_op jit(solution)/shard_map/ppermute | solution.py:381
  18.8 8.9 %collective-permute-start.4 = (f32[16,256]{1,0:T(8,128)S(1)}, f32[16,256]{1,0:T(8,128)S(1)}, u32[]{:S(2)}, u32[]{:S(2)}) collective-permute-start(f32[16,256]{1,0:T(8,128)S(1)} %get-tuple-element.75), channel_id=1, source_target_pairs={{0,1},{1,0},{2,3},{3,2},{4,5},{5,4},{6,7},{7,6},{8,9},{9,8},{10,11... | collective-permute-start | bytes 49160 | tf_op jit(solution)/shard_map/ppermute | solution.py:381
  20.0 7.7 %collective-permute-start.5 = (f32[16,256]{1,0:T(8,128)S(1)}, f32[16,256]{1,0:T(8,128)S(1)}, u32[]{:S(2)}, u32[]{:S(2)}) collective-permute-start(f32[16,256]{1,0:T(8,128)S(1)} %get-tuple-element.76), channel_id=1, source_target_pairs={{0,255},{1,2},{2,1},{3,4},{4,3},{5,6},{6,5},{7,8},{8,7},{9,10},{10... | collective-permute-start | bytes 49160 | tf_op jit(solution)/shard_map/ppermute | solution.py:381
  22.1 7.0 %collective-permute-start.6 = (f32[16,256]{1,0:T(8,128)S(1)}, f32[16,256]{1,0:T(8,128)S(1)}, u32[]{:S(2)}, u32[]{:S(2)}) collective-permute-start(f32[16,256]{1,0:T(8,128)S(1)} %get-tuple-element.78), channel_id=1, source_target_pairs={{0,1},{1,0},{2,3},{3,2},{4,5},{5,4},{6,7},{7,6},{8,9},{9,8},{10,11... | collective-permute-start | bytes 49160 | tf_op jit(solution)/shard_map/ppermute | solution.py:381
  27.7 3.2 %collective-permute-start.7 = (f32[16,256]{1,0:T(8,128)S(1)}, f32[16,256]{1,0:T(8,128)S(1)}, u32[]{:S(2)}, u32[]{:S(2)}) collective-permute-start(f32[16,256]{1,0:T(8,128)S(1)} %get-tuple-element.79), channel_id=1, source_target_pairs={{0,255},{1,2},{2,1},{3,4},{4,3},{5,6},{6,5},{7,8},{8,7},{9,10},{10... | collective-permute-start | bytes 49160 | tf_op jit(solution)/shard_map/ppermute | solution.py:381
  27.7 3.2 %copy-start.8 = (f32[256,256]{1,0:T(8,128)S(1)}, f32[256,256]{1,0:T(8,128)}, u32[]{:S(2)}) copy-start(f32[256,256]{1,0:T(8,128)} %target_ref.1) | copy-start | bytes 786436
  30.9 6.4 %copy-start.3 = (bf16[2,256,256]{2,1,0:T(8,128)(2,1)S(1)}, bf16[2,256,256]{2,1,0:T(8,128)(2,1)}, u32[]{:S(2)}) copy-start(bf16[2,256,256]{2,1,0:T(8,128)(2,1)} %constant.19.clone.refs_6_.refs_9_.refs_8_) | copy-start | bytes 786436
  30.9 6.4 %copy-start.5 = (bf16[256,64]{1,0:T(8,128)(2,1)S(1)}, bf16[256,64]{1,0:T(8,128)(2,1)}, u32[]{:S(2)}) copy-start(bf16[256,64]{1,0:T(8,128)(2,1)} %constant.20.clone.refs_7_.refs_10_.refs_9_) | copy-start | bytes 98308
  30.9 6.4 %copy-start.7 = (bf16[64,256]{1,0:T(8,128)(2,1)S(1)}, bf16[64,256]{1,0:T(8,128)(2,1)}, u32[]{:S(2)}) copy-start(bf16[64,256]{1,0:T(8,128)(2,1)} %constant.21.clone.refs_8_.refs_11_.refs_10_) | copy-start | bytes 98308
  31.7 9.1 %collective-permute-start.8 = (f32[16,256]{1,0:T(8,128)S(1)}, f32[16,256]{1,0:T(8,128)S(1)}, u32[]{:S(2)}, u32[]{:S(2)}) collective-permute-start(f32[16,256]{1,0:T(8,128)S(1)} %get-tuple-element.87), channel_id=1, source_target_pairs={{0,1},{1,0},{2,3},{3,2},{4,5},{5,4},{6,7},{7,6},{8,9},{9,8},{10,11... | collective-permute-start | bytes 49160 | tf_op jit(solution)/shard_map/ppermute | solution.py:381
  37.3 3.6 %collective-permute-start.9 = (f32[16,256]{1,0:T(8,128)S(1)}, f32[16,256]{1,0:T(8,128)S(1)}, u32[]{:S(2)}, u32[]{:S(2)}) collective-permute-start(f32[16,256]{1,0:T(8,128)S(1)} %get-tuple-element.88), channel_id=1, source_target_pairs={{0,255},{1,2},{2,1},{3,4},{4,3},{5,6},{6,5},{7,8},{8,7},{9,10},{10... | collective-permute-start | bytes 49160 | tf_op jit(solution)/shard_map/ppermute | solution.py:381
  38.7 9.1 %collective-permute-start.10 = (f32[16,256]{1,0:T(8,128)S(1)}, f32[16,256]{1,0:T(8,128)S(1)}, u32[]{:S(2)}, u32[]{:S(2)}) collective-permute-start(f32[16,256]{1,0:T(8,128)S(1)} %get-tuple-element.94), channel_id=1, source_target_pairs={{0,1},{1,0},{2,3},{3,2},{4,5},{5,4},{6,7},{7,6},{8,9},{9,8},{10,11... | collective-permute-start | bytes 49160 | tf_op jit(solution)/shard_map/ppermute | solution.py:381
  39.8 8.0 %collective-permute-start.11 = (f32[16,256]{1,0:T(8,128)S(1)}, f32[16,256]{1,0:T(8,128)S(1)}, u32[]{:S(2)}, u32[]{:S(2)}) collective-permute-start(f32[16,256]{1,0:T(8,128)S(1)} %get-tuple-element.95), channel_id=1, source_target_pairs={{0,255},{1,2},{2,1},{3,4},{4,3},{5,6},{6,5},{7,8},{8,7},{9,10},{10... | collective-permute-start | bytes 49160 | tf_op jit(solution)/shard_map/ppermute | solution.py:381
  42.3 7.3 %collective-permute-start.12 = (f32[16,256]{1,0:T(8,128)S(1)}, f32[16,256]{1,0:T(8,128)S(1)}, u32[]{:S(2)}, u32[]{:S(2)}) collective-permute-start(f32[16,256]{1,0:T(8,128)S(1)} %get-tuple-element.102), channel_id=1, source_target_pairs={{0,1},{1,0},{2,3},{3,2},{4,5},{5,4},{6,7},{7,6},{8,9},{9,8},{10,11... | collective-permute-start | bytes 49160 | tf_op jit(solution)/shard_map/ppermute | solution.py:381
  47.8 3.2 %collective-permute-start.13 = (f32[16,256]{1,0:T(8,128)S(1)}, f32[16,256]{1,0:T(8,128)S(1)}, u32[]{:S(2)}, u32[]{:S(2)}) collective-permute-start(f32[16,256]{1,0:T(8,128)S(1)} %get-tuple-element.103), channel_id=1, source_target_pairs={{0,255},{1,2},{2,1},{3,4},{4,3},{5,6},{6,5},{7,8},{8,7},{9,10},{10... | collective-permute-start | bytes 49160 | tf_op jit(solution)/shard_map/ppermute | solution.py:381
  51.9 6.8 %collective-permute-start.14 = (f32[264,256]{1,0:T(8,128)S(1)}, f32[264,256]{1,0:T(8,128)S(1)}, u32[]{:S(2)}, u32[]{:S(2)}) collective-permute-start(f32[264,256]{1,0:T(8,128)S(1)} %get-tuple-element.110), channel_id=1, source_target_pairs={{0,1},{1,0},{2,3},{3,2},{4,5},{5,4},{6,7},{7,6},{8,9},{9,8},{10,11... | collective-permute-start | bytes 811016 | tf_op jit(solution)/shard_map/ppermute | solution.py:447
  92.5 5.4 %collective-permute-start.15 = (f32[256,256]{1,0:T(8,128)S(1)}, f32[256,256]{1,0:T(8,128)S(1)}, u32[]{:S(2)}, u32[]{:S(2)}) collective-permute-start(f32[256,256]{1,0:T(8,128)S(1)} %bitcast.7), channel_id=1, source_target_pairs={{0,1},{1,0},{2,3},{3,2},{4,5},{5,4},{6,7},{7,6},{8,9},{9,8},{10,11... | collective-permute-start | bytes 786440 | tf_op jit(solution)/shard_map/ppermute | solution.py:453

commit v2 on v1

v2 whole, which is shorter than its diff:
```python
import jax
import jax.numpy as jnp
import ml_dtypes
import numpy as np
from jax import lax
from jax.experimental import pallas as pl
from jax.experimental.pallas import tpu as pltpu
from jax.sharding import Mesh, PartitionSpec as P

AXES = ("x", "y", "z", "core")
PLANE = ("x", "y")
SIZES = (4, 4, 8, 2)
DEVICES = 256
WIDTH = 256
COUNT = 16777216.0
PARAMS = 131584.0
TIME_STEP = 0.05
HALF_STEP = 0.025
TINY = 1e-20
F32 = jnp.float32
BF16 = jnp.bfloat16


def face_rows(face):
    layer = 0 if face % 2 == 0 else 3
    grid = np.arange(64).reshape(4, 4, 4)
    return np.take(grid, layer, axis=face // 2).reshape(16)


def operators():
    points = np.array([-1.0, -1.0 / np.sqrt(5.0), 1.0 / np.sqrt(5.0), 1.0])
    bary = np.array(
        [1.0 / np.prod([points[m] - points[n] for n in range(4) if n != m]) for m in range(4)]
    )
    deriv = np.zeros((4, 4))
    for m in range(4):
        for n in range(4):
            if m != n:
                deriv[m, n] = bary[n] / bary[m] / (points[m] - points[n])
        deriv[m, m] = -np.sum(deriv[m])
    eye = np.eye(4)
    tables = [
        np.kron(np.kron(deriv, eye), eye),
        np.kron(np.kron(eye, deriv), eye),
        np.kron(eye, np.kron(eye, deriv)),
    ]
    inner = np.zeros((256, 256))
    for a in range(3):
        inner[0:64, 64 * (a + 1) : 64 * (a + 2)] -= tables[a]
        inner[64 * (a + 1) : 64 * (a + 2), 0:64] -= tables[a]
    for face in range(6):
        sign = 2.0 * (face % 2) - 1.0
        for row in face_rows(face):
            speed = 64 * (face // 2 + 1) + row
            inner[row, row] -= 3.0
            inner[row, speed] += 3.0 * sign
            inner[speed, speed] -= 3.0
            inner[speed, row] += 3.0 * sign
    leave = np.zeros((64, 256))
    lift = np.zeros((256, 64))
    for face in range(2, 6):
        sign = 2.0 * (face % 2) - 1.0
        base = 16 * (face - 2)
        for n, row in enumerate(face_rows(face ^ 1)):
            leave[base + n, row] = 3.0
            leave[base + n, 64 * (face // 2 + 1) + row] = -3.0 * sign
        for n, row in enumerate(face_rows(face)):
            lift[row, base + n] = 1.0
            lift[64 * (face // 2 + 1) + row, base + n] = -sign
    return inner, leave, lift


def halves(values):
    high = values.astype(ml_dtypes.bfloat16)
    low = (values - high.astype(np.float64)).astype(ml_dtypes.bfloat16)
    return high, low


def split(values):
    high = values.astype(BF16)
    return high, (values - high.astype(F32)).astype(BF16)


def mm(left, right):
    return jnp.dot(left, right, preferred_element_type=F32)


def mm_nt(left, right):
    return lax.dot_general(left, right, (((1,), (1,)), ((), ())), preferred_element_type=F32)


def mm3(left, right, dot=mm):
    return dot(left[0], right[0]) + (dot(left[0], right[1]) + dot(left[1], right[0]))


def pair(ref):
    if len(ref.shape) == 2:
        return ref[0:256], ref[256:512]
    return ref[0], ref[1]


def call(body, outs, *args, name, micros, far=(), scratch=(), limit=24, reads=1000000):
    def space(n, value):
        if value.shape == (1,):
            return pltpu.SMEM
        return pltpu.HBM if n in far else pltpu.VMEM

    return list(pl.pallas_call(
        body,
        out_shape=[jax.ShapeDtypeStruct(s, t) for s, t in outs],
        in_specs=[pl.BlockSpec(memory_space=space(n, a)) for n, a in enumerate(args)],
        out_specs=[pl.BlockSpec(memory_space=pltpu.VMEM)] * len(outs),
        scratch_shapes=scratch,
        cost_estimate=pl.CostEstimate(flops=int(micros * 1.15e9), bytes_accessed=reads, transcendentals=0),
        compiler_params=pltpu.CompilerParams(vmem_limit_bytes=limit * 1024 * 1024),
        name=name,
    )(*args))


SQUARE = ((256, 256), F32)
PAIR = ((2, 256, 256), BF16)
EXTRA = ((8, 128), F32)
PACKED = ((16, 40, 128), F32)
COLUMN = ((256, 128), F32)


def edges(values):
    return values[0:16], values[48:64], values[64:80], values[112:128]


def leaving(values):
    p_low, p_high, u_low, u_high = edges(values)
    return 3.0 * (p_high + u_high), 3.0 * (p_low - u_low)


def put(parity, upward, downward, in_chip_ref, cross_ref, rows=0):
    even = parity == 0
    in_chip_ref[rows : rows + 16] = jnp.where(even, upward, downward)
    cross_ref[rows : rows + 16] = jnp.where(even, downward, upward)


def take(parity, in_chip, cross):
    even = parity == 0
    return jnp.where(even, cross, in_chip), jnp.where(even, in_chip, cross)


def pick(values, table, dot=mm):
    both = dot(jnp.concatenate(split(values), axis=0), table)
    return both[0:16] + both[16:32]


def add_edges(values_ref, first, second, third, fourth):
    values_ref[0:16] += first
    values_ref[48:64] += second
    values_ref[64:80] += third
    values_ref[112:128] += fourth


def one_hot(rows, column):
    return (rows == column).astype(F32).astype(BF16)


def first_kernel(
    parity_ref, state_far, w_in_far, nbr_far, fixed_far, b_in_far, w_out_far, b_out_far, send_far,
    next_ref, hidden_ref, in_chip_ref, cross_ref, w_in, b_in, w_out, b_out, near, state_ref, nbr_ref,
    inner, leave, lift, lift_t, w_in_ref, b_in_ref, w_out_ref, b_out_ref, send_ref, sems,
):
    pairs = (
        (state_far, state_ref), (w_in_far, w_in_ref), (b_in_far, b_in_ref), (fixed_far.at[512:576], leave),
        (nbr_far, nbr_ref), (fixed_far.at[0:512], inner), (fixed_far.at[576:640], lift_t), (w_out_far, w_out_ref),
        (b_out_far, b_out_ref), (send_far, send_ref),
    )
    copies = [pltpu.make_async_copy(s, t, sems.at[n]) for n, (s, t) in enumerate(pairs)]
    for copy in copies:
        copy.start()
    copies[0].wait()
    values = state_ref[...]
    parity = parity_ref[0]
    put(parity, *leaving(state_ref), in_chip_ref, cross_ref)
    copies[1].wait()
    w_in[0], w_in[1] = split(w_in_ref[...])
    for copy in copies[2:5]:
        copy.wait()
    rows = lax.broadcasted_iota(jnp.int32, (256, 256), 0)
    for face in range(2, 6):
        near[face - 2] = one_hot(rows + 256 * (face ^ 1), nbr_ref[face : face + 1])
    for copy in copies[5:]:
        copy.wait()
    lift[...] = flip(lift_t[...])
    w_out[0], w_out[1] = split(w_out_ref[...])
    for row_ref, ref in ((b_in_ref, b_in), (b_out_ref, b_out)):
        ref[...] = jnp.broadcast_to(row_ref[...], (128, 256)).T
    rates = local_rates(values, (w_in, b_in, w_out, b_out, inner, leave, lift, near), hidden_ref)
    next_ref[...] = values + TIME_STEP * rates
    put(parity, *leaving(next_ref), in_chip_ref, cross_ref, 16)
    down_index = send_ref[0:1].astype(F32)
    up_index = (send_ref[1:2] - 256).astype(F32)
    even = parity == 0
    in_chip_ref[32:40] = jnp.broadcast_to(jnp.where(even, up_index, down_index), (8, 256))
    cross_ref[32:40] = jnp.broadcast_to(jnp.where(even, down_index, up_index), (8, 256))


def flip(values):
    return values.astype(F32).T.astype(BF16)


def tables_kernel(
    w_in, w_out, inner, leave, nbr_ref, state_ref, after_ref, in_t_ref, out_t_ref, inner_t, leave_t, far_ref, copy_ref
):
    copy_ref[...] = state_ref[...]
    for part in range(2):
        in_t_ref[part] = flip(w_in[part])
        out_t_ref[part] = flip(w_out[part])
        inner_t[256 * part : 256 * part + 256] = flip(inner[256 * part : 256 * part + 256])
    leave_t[...] = flip(leave[...])
    rows = lax.broadcasted_iota(jnp.int32, (256, 256), 0)
    for face in range(2):
        far_ref[face] = one_hot(rows + (1536 + 256 * face), nbr_ref[face : face + 1])


def wide(column):
    return jnp.concatenate([column[...], column[...]], axis=1)


def local_rates(values, network, hidden_ref):
    w_in, b_in, w_out, b_out, inner, leave, lift, near = network
    parts = split(values)
    hidden = jnp.tanh(mm3(pair(w_in), parts) + wide(b_in))
    hidden_ref[...] = hidden
    rates = mm3(pair(inner), parts) + wide(b_out)
    high, low = split(mm(leave[...], parts[0]) + mm(leave[...], parts[1]))
    arrived = []
    for n in range(4):
        both = jnp.concatenate([high[16 * n : 16 * n + 16], low[16 * n : 16 * n + 16]], axis=0)
        arrived.append(mm(both, near[n]).astype(BF16))
    for part in range(2):
        rates += mm(lift[...], jnp.concatenate([a[16 * part : 16 * part + 16] for a in arrived], axis=0))
    return rates + mm3(pair(w_out), split(hidden))


def add_arrived(weight, base_ref, below, above, link, now_ref):
    low = weight * pick(below, link[0])
    high = weight * pick(above, link[1])
    now_ref[...] = base_ref[...]
    add_edges(now_ref, low, high, low, -high)
    return now_ref[...]


def middle_kernel(
    parity_ref, base_ref, state_ref, in_chip, cross, far_ref,
    w_in, b_in, w_out, b_out, inner, leave, lift, near,
    second_ref, third_ref, hidden_second, hidden_third, next_ref, link, in_chip_out, cross_out, between,
):
    network = (w_in, b_in, w_out, b_out, inner, leave, lift, near)
    parity = parity_ref[0]
    below, above = take(parity, in_chip[...], cross[...])
    rows = lax.broadcasted_iota(jnp.int32, (256, 256), 0).astype(F32)
    for side, received in enumerate((below, above)):
        link[side] = mm(one_hot(rows, received[32:33]), far_ref[side]).astype(BF16)
    values = add_arrived(TIME_STEP, base_ref, below[0:16], above[0:16], link, second_ref)
    between[...] = 0.5 * (state_ref[...] + values) + HALF_STEP * local_rates(values, network, hidden_second)
    put(parity, *leaving(between), in_chip_out, cross_out)
    values = add_arrived(HALF_STEP, between, below[16:32], above[16:32], link, third_ref)
    next_ref[...] = values + TIME_STEP * local_rates(values, network, hidden_third)
    put(parity, *leaving(next_ref), in_chip_out, cross_out, 16)


def sensitivities(values, link):
    p_low, p_high, u_low, u_high = edges(values)
    return pick(p_high - u_high, link[1], mm_nt), pick(p_low + u_low, link[0], mm_nt)


def through_closure(parts, hidden, w_out_t):
    return (1.0 - hidden * hidden) * mm3(w_out_t, parts)


def back_rates(parts, delta_parts, network):
    w_in_t, inner_t, leave_t, lift_t, near = network
    rates = mm3(pair(inner_t), parts) + mm3(pair(w_in_t), delta_parts)
    high, low = split(mm(lift_t[...], parts[0]) + mm(lift_t[...], parts[1]))
    arrived = []
    for n in range(4):
        both = jnp.concatenate([high[16 * n : 16 * n + 16], low[16 * n : 16 * n + 16]], axis=0)
        arrived.append(mm_nt(both, near[n]))
    high, low = split(jnp.concatenate([a[0:16] + a[16:32] for a in arrived], axis=0))
    return rates + (mm(leave_t[...], high) + mm(leave_t[...], low))


def turn_kernel(
    parity_ref, base_ref, third_ref, in_chip, cross, link, target_ref,
    w_in, b_in, w_out, b_out, inner, leave, lift, near, w_in_t, w_out_t, inner_t, leave_t, lift_t,
    final_ref, loss_ref, fourth_ref, hidden_ref, adjoint_ref, delta_ref, next_ref, in_chip_out, cross_out, between,
):
    network = (w_in, b_in, w_out, b_out, inner, leave, lift, near)
    parity = parity_ref[0]
    below, above = take(parity, in_chip[...], cross[...])
    values = add_arrived(TIME_STEP, base_ref, below[0:16], above[0:16], link, fourth_ref)
    between[...] = 0.5 * (third_ref[...] + values) + HALF_STEP * local_rates(values, network, hidden_ref)
    final = add_arrived(HALF_STEP, between, below[16:32], above[16:32], link, final_ref)
    mismatch = final - target_ref[...]
    adjoint = (HALF_STEP / COUNT) * mismatch
    adjoint_ref[...] = adjoint
    squares = jnp.sum(mismatch * mismatch, axis=0, keepdims=True)
    loss_ref[...] = jnp.broadcast_to(squares[:, 0:128] + squares[:, 128:256], (8, 128))
    put(parity, *sensitivities(adjoint_ref, link), in_chip_out, cross_out)
    parts = split(adjoint)
    delta = through_closure(parts, hidden_ref[...], pair(w_out_t))
    delta_ref[...] = delta
    next_ref[...] = adjoint + TIME_STEP * back_rates(parts, split(delta), (w_in_t, inner_t, leave_t, lift_t, near))
    put(parity, *sensitivities(next_ref, link), in_chip_out, cross_out, 16)


def gradients(parts, delta_parts, state, hidden):
    ones = jnp.ones((8, 256), BF16)
    rows = lax.broadcasted_iota(jnp.int32, (8, 128), 0)
    first = mm_nt(ones, delta_parts[0]) + mm_nt(ones, delta_parts[1])
    second = mm_nt(ones, parts[0]) + mm_nt(ones, parts[1])
    bias = jnp.where(rows == 0, first[:, 0:128], jnp.where(rows == 1, first[:, 128:256], 0.0))
    bias = jnp.where(rows == 2, second[:, 0:128], bias)
    if second.shape[1] == 256:
        bias = jnp.where(rows == 3, second[:, 128:256], bias)
    return mm3(delta_parts, split(state), mm_nt), mm3(parts, split(hidden), mm_nt), bias


def beside_kernel(
    adjoint_ref, delta_ref, state_ref, hidden_ref, in_chip, cross, w_in, b_in,
    grad_in, grad_out, extra, in_chip_hidden, cross_hidden,
):
    grad_in[...], grad_out[...], extra[...] = gradients(
        split(adjoint_ref[...]), split(delta_ref[...]), state_ref[...], hidden_ref[...]
    )
    for source, ref in ((in_chip, in_chip_hidden), (cross, cross_hidden)):
        ref[...] = jnp.tanh(mm3(pair(w_in), split(source[...])) + wide(b_in))


def back_kernel(
    parity_ref, base_ref, adjoint_ref, in_chip, cross, link,
    third_ref, hidden_third, second_ref, hidden_second, state_ref, hidden_first,
    in_chip_state, cross_state, in_chip_hidden, cross_hidden,
    near, w_in_t, w_out_t, inner_t, leave_t, lift_t, old_in, old_out, old_extra, loss_ref,
    keep_ref, send_ref, now_ref, between, sum_ref,
):
    network = (w_in_t, inner_t, leave_t, lift_t, near)
    parity = parity_ref[0]
    even = parity == 0
    below, above = take(parity, in_chip[...], cross[...])
    totals = [old_in[...], old_out[...], old_extra[...]]

    def arrive(source_ref, weight, low, high):
        now_ref[...] = source_ref[...]
        low, high = weight * low, weight * high
        add_edges(now_ref, low, high, -low, high)
        return now_ref[...]

    def gather(*args):
        for n, term in enumerate(gradients(*args)):
            totals[n] = totals[n] + term

    values = arrive(base_ref, 3.0 * TIME_STEP, below[0:16], above[0:16])
    parts = split(values)
    delta = split(through_closure(parts, hidden_third[...], pair(w_out_t)))
    between[...] = 0.5 * (adjoint_ref[...] + values) + HALF_STEP * back_rates(parts, delta, network)
    gather(parts, delta, third_ref[...], hidden_third[...])
    upward, downward = sensitivities(between, link)

    values = arrive(between, 3.0 * HALF_STEP, below[16:32], above[16:32])
    parts = split(values)
    delta = split(through_closure(parts, hidden_second[...], pair(w_out_t)))
    values = values + TIME_STEP * back_rates(parts, delta, network)
    gather(parts, delta, second_ref[...], hidden_second[...])

    parts = split(values)
    delta = split(through_closure(parts, hidden_first[...], pair(w_out_t)))
    gather(parts, delta, state_ref[...], hidden_first[...])

    states = take(parity, in_chip_state[...], cross_state[...])
    hiddens = take(parity, in_chip_hidden[...], cross_hidden[...])
    w_edge = w_out_t[0, :, 0:128], w_out_t[1, :, 0:128]
    weight = 3.0 * TIME_STEP
    none = jnp.zeros((48, 256), F32)
    low, high = weight * upward, weight * downward
    for values, state, hidden in (
        (jnp.concatenate([none, high, none, high], axis=0), states[0], hiddens[0]),
        (jnp.concatenate([low, none, -low, none], axis=0), states[1], hiddens[1]),
    ):
        parts = split(values)
        delta = split(through_closure(parts, hidden, w_edge))
        first, second, bias = gradients(parts, delta, state, hidden)
        totals[0] = totals[0] + first
        totals[2] = totals[2] + bias
        sum_ref[...] = totals[1]
        sum_ref[0:128] += second
        totals[1] = sum_ref[...]
    first, second, bias = totals
    rows = lax.broadcasted_iota(jnp.int32, (8, 128), 0)
    bias = jnp.where(rows == 4, loss_ref[...], bias)
    for ref, values in ((keep_ref, jnp.where(even, first, second)), (send_ref, jnp.where(even, second, first))):
        for n in range(16):
            ref[n, 0:16] = values[16 * n : 16 * n + 16, 0:128]
            ref[n, 16:32] = values[16 * n : 16 * n + 16, 128:256]
            ref[n, 32:40] = bias


def chip_kernel(keep_ref, got_ref, out_ref):
    out_ref[...] = keep_ref[...] + got_ref[...]


def plane_kernel(parts_ref, out_ref):
    total = jnp.sum(parts_ref[...], axis=0)
    for n in range(8):
        out_ref[n] = total


def line_kernel(parts_ref, out_ref, extra_ref):
    total = jnp.sum(parts_ref[...], axis=0)
    extra_ref[...] = total[32:40]
    for n in range(16):
        out_ref[n] = total[0:32]


def last_kernel(parity_ref, own_ref, other_ref, extra_ref, in_ref, b_in_ref, out_ref, b_out_ref, loss_ref):
    even = parity_ref[0] == 0
    own, other = own_ref[...], other_ref[...]
    first = jnp.where(even, own, other)
    second = jnp.where(even, other, own)
    bias = extra_ref[0:4]
    squares = jnp.sum(first * first + second * second, axis=0)
    total = jnp.sum(squares, keepdims=True) + jnp.sum(bias * bias, keepdims=True)
    scale = lax.rsqrt(total / PARAMS + TINY)
    for ref, values in ((in_ref, first * scale), (out_ref, second * scale)):
        for n in range(16):
            ref[16 * n : 16 * n + 16, 0:128] = values[n, 0:16]
            ref[16 * n : 16 * n + 16, 128:256] = values[n, 16:32]
    bias = bias * scale
    for row, ref in ((0, b_in_ref), (2, b_out_ref)):
        ref[:, 0:128] = bias[row : row + 1]
        ref[:, 128:256] = bias[row + 1 : row + 2]
    loss_ref[...] = jnp.sum(extra_ref[4:5], keepdims=True) * (0.5 / COUNT)


IN_CHIP = [(n, n ^ 1) for n in range(DEVICES)]
CROSS = [(n, (n - 1) % DEVICES if n % 2 == 0 else (n + 1) % DEVICES) for n in range(DEVICES)]


def exchange(in_chip, cross):
    return lax.ppermute(in_chip, AXES, IN_CHIP), lax.ppermute(cross, AXES, CROSS)


def local(state, target, w_in, b_in, w_out, b_out, nbr, send):
    parity = lax.axis_index("core").reshape(1)
    inner, leave, lift = operators()
    weights = [PAIR, COLUMN, PAIR, COLUMN]
    fixed = np.concatenate([*halves(inner), leave, lift.T], axis=0).astype(ml_dtypes.bfloat16)
    line = lambda values: values.reshape(1, 256)
    tall, flat, thin = ((512, 256), BF16), ((64, 256), BF16), ((256, 64), BF16)
    base, hidden_first, *edge, w_in2, b_in2, w_out2, b_out2, near, state, nbr, inner2, leave1, lift1, lift_t = call(
        first_kernel,
        [SQUARE, SQUARE, ((40, 256), F32), ((40, 256), F32)]
        + weights
        + [((4, 256, 256), BF16), SQUARE, ((6, 256), jnp.int32), tall, flat, thin, flat],
        parity, state, w_in, nbr, jnp.asarray(fixed), line(b_in), w_out, line(b_out), send,
        name="first", micros=1.5,
        far=range(1, 9),
        limit=52,
        scratch=[
            pltpu.VMEM((256, 256), F32), pltpu.VMEM((1, 256), F32), pltpu.VMEM((256, 256), F32),
            pltpu.VMEM((1, 256), F32), pltpu.VMEM((2, 256), jnp.int32), pltpu.SemaphoreType.DMA((10,)),
        ],
    )
    got = exchange(*edge)
    w_in_t, w_out_t, inner_t, leave_t, far, copy = call(
        tables_kernel,
        [PAIR, PAIR, tall, thin, PAIR, SQUARE],
        w_in2, w_out2, inner2, leave1, nbr, state, got[0],
        name="tables", micros=0.4,
    )
    beside = exchange(copy, copy)
    network = (w_in2, b_in2, w_out2, b_out2, inner2, leave1, lift1, near)
    back = (w_in_t, w_out_t, inner_t, leave_t, lift_t)
    edge_shapes = [((32, 256), F32)] * 2
    second, third, hidden_second, hidden_third, base, link, *edge, _ = call(
        middle_kernel,
        [SQUARE] * 5 + [PAIR] + edge_shapes + [SQUARE],
        parity, base, state, *got, far, *network, name="middle", micros=2.8,
    )
    got = exchange(*edge)
    final, loss, fourth, hidden_fourth, adjoint, delta, base, *edge, _ = call(
        turn_kernel,
        [SQUARE, EXTRA] + [SQUARE] * 5 + edge_shapes + [SQUARE],
        parity, base, third, *got, link, target, *network, *back, name="turn", micros=3,
    )
    got = exchange(*edge)
    *grads, in_chip_hidden, cross_hidden = call(
        beside_kernel,
        [SQUARE, SQUARE, EXTRA, SQUARE, SQUARE],
        adjoint, delta, fourth, hidden_fourth, *beside, w_in2, b_in2, name="beside", micros=0.8,
    )
    keep, give, *_ = call(
        back_kernel,
        [PACKED] * 2 + [SQUARE] * 3,
        parity, base, adjoint, *got, link, third, hidden_third, second, hidden_second, state, hidden_first,
        *beside, in_chip_hidden, cross_hidden, near, *back, *grads, loss, name="back", micros=4.5,
    )
    swap = [(0, 1), (1, 0)]
    (parts,) = call(chip_kernel, [PACKED], keep, lax.ppermute(give, "core", swap), name="chip_sum", micros=0.3)
    parts = lax.all_to_all(parts, PLANE, 0, 0, tiled=True)
    (parts,) = call(plane_kernel, [((8, 40, 128), F32)], parts, name="plane_sum", micros=0.3)
    parts = lax.all_to_all(parts, "z", 0, 0, tiled=True)
    parts, extra = call(line_kernel, [((16, 32, 128), F32), EXTRA], parts, name="line_sum", micros=0.3)
    own = lax.all_to_all(parts, PLANE, 0, 0, tiled=True)
    other = lax.ppermute(own, "core", swap)
    row = ((1, 256), F32)
    step_in, step_b_in, step_out, step_b_out, loss = call(
        last_kernel, [SQUARE, row, SQUARE, row, ((1, 1), F32)], parity, own, other, extra, name="scale", micros=1
    )
    return final, loss.reshape(()), step_in, step_b_in.reshape(256), step_out, step_b_out.reshape(256)


def solution(mesh):
    split_mesh = Mesh(mesh.devices.reshape(SIZES), AXES)
    whole = P(None, AXES)
    return jax.shard_map(
        local,
        mesh=split_mesh,
        in_specs=(whole, whole, P(), P(), P(), P(), whole, whole),
        out_specs=(whole, P(), P(), P(), P(), P()),
        check_vma=False,
    )
```

time: 99.3 us -> 91.9 us (0.925)
  starting transfers between devices: 42.9 us -> 28.8 us
  blocking collectives: 33.7 us -> 37.1 us
  Pallas kernels: 13.4 us -> 15.3 us
  waiting for transfers between devices: 5.54 us -> 7.39 us
    ppermute x7 -> x4, starting transfers between devices: 31.2 us -> 19.7 us  [exchange(): lax.ppermute(in_chip, AXES, IN_CHIP)]
    all_to_all x1, blocking collectives: 10.8 us -> 14.7 us  [local(): parts = lax.all_to_all(parts, 'z', 0, 0, tiled=True)]
    pallas_call x15 -> x10, Pallas kernels: 13.4 us -> 15.3 us  [call(): pl.pallas_call(body, out_shape=[jax.ShapeDtypeStruct(s, t) for s, t in ou...]
    ppermute x7 -> x4, starting transfers between devices: 1.74 us -> 0.01 us  [exchange(): lax.ppermute(cross, AXES, CROSS)]
    ppermute x7 -> x4, waiting for transfers between devices: 3.18 us -> 4.1 us  [exchange(): lax.ppermute(cross, AXES, CROSS)]
    unnamed x30 -> x16, local copies, waits for them, and re-layouts: 2.35 us -> 2.32 us
  transfers between devices with their start and end apart: 16 -> 10, of which waited for: 4 -> 6; matrix products, arithmetic and copies ran while one was open for 0% -> 0% of each run, Pallas kernels for 11% -> 5%
where the time goes in v2:
time: 91.9 us; the launch traced here: 91.6 us
  blocking collectives  37.1 us (40%)
  starting transfers between devices  28.8 us (31%)
  Pallas kernels  15.3 us (17%)
  waiting for transfers between devices  7.39 us (8%)
  local copies, waits for them, and re-layouts  2.32 us (3%)
    ppermute x4, starting transfers between devices, exchange(): lax.ppermute(in_chip, AXES, IN_CHIP)  19.7 us
    pallas_call x10, Pallas kernels, call(): pl.pallas_call(body, out_shape=[jax.ShapeDtypeStruct(s, t) for s, t in ou...  15.3 us
    all_to_all x1, blocking collectives, local(): parts = lax.all_to_all(parts, 'z', 0, 0, tiled=True)  14.7 us
    all_to_all x1, blocking collectives, local(): parts = lax.all_to_all(parts, PLANE, 0, 0, tiled=True)  11.2 us
    all_to_all x1, blocking collectives, local(): own = lax.all_to_all(parts, PLANE, 0, 0, tiled=True)  11.2 us
    ppermute x1, starting transfers between devices, local(): lax.ppermute(give, 'core', swap)  5.14 us
    ppermute x4, waiting for transfers between devices, exchange(): lax.ppermute(cross, AXES, CROSS)  4.1 us
    ppermute x1, starting transfers between devices, local(): other = lax.ppermute(own, 'core', swap)  4.01 us
  transfers between devices with their start and end apart: 10, of which 6 were waited for; matrix products, arithmetic and copies ran while one was open for 0% of the time, Pallas kernels for 5%

profile of v2, /device:TPU:1, one launch (start us, length us, event | category | flops | bytes accessed | tf_op | source)
XLA Modules:
  0.0 91.6 jit_solution(3284962312916901809)
XLA Ops:
  0.6 0.0 copy-start.1
  0.6 0.0 copy-start.2
  0.7 0.0 copy-start.3
  0.7 0.7 copy-done.1
  1.3 0.0 copy-done.2
  1.3 0.0 copy-done.3
  1.3 0.0 copy-start.4
  1.3 0.7 copy-done.4
  2.0 2.6 %first.1 = (f32[256,256]{1,0:T(8,128)S(1)}, f32[256,256]{1,0:T(8,128)S(1)}, f32[40,256]{1,0:T(8,128)S(1)}, f32[40,256]{1,0:T(8,128)S(1)}, bf16[2,256,256]{2,1,0:...) custom-call(s32[1]{0:T(128)} %bitcast.parity_ref, ...), custom_call_target="tpu_custom_call" | custom-call | flops 1724999936 | bytes 1000000 | tf_op jit(solution)/shard_map/first/pallas_call | solution.py:108
  4.6 3.3 %collective-permute-start = (f32[40,256]{1,0:T(8,128)S(1)}, f32[40,256]{1,0:T(8,128)S(1)}, u32[]{:S(2)}, u32[]{:S(2)}) collective-permute-start(f32[40,256]{1,0:T(8,128)S(1)} %get-tuple-element.60), channel_id=1, source_target_pairs={{0,1},{1,0},{2,3},{3,2},{4,5},{5,4},{6,7},{7,6},{8,9},{9,8},{10,11... | collective-permute-start | bytes 122888 | tf_op jit(solution)/shard_map/ppermute | solution.py:446
  7.9 0.0 collective-permute-start.1
  7.9 0.9 collective-permute-done.after_ref.in_chip
  8.8 0.0 copy-start.5
  8.8 0.9 %copy-done.5 = bf16[512,256]{1,0:T(8,128)(2,1)S(1)} copy-done((bf16[512,256]{1,0:T(8,128)(2,1)S(1)}, bf16[512,256]{1,0:T(8,128)(2,1)}, u32[]{:S(2)}) %copy-start.5) | copy-done | bytes 262168
  9.7 0.0 copy-start.6
  9.7 0.0 copy-start.7
  9.7 0.3 tables.1
  10.1 1.3 %collective-permute-done.1.cross = f32[40,256]{1,0:T(8,128)S(1)} collective-permute-done((f32[40,256]{1,0:T(8,128)S(1)}, f32[40,256]{1,0:T(8,128)S(1)}, u32[]{:S(2)}, u32[]{:S(2)}) %collective-permute-start.1) | collective-permute-done | bytes 40992 | tf_op jit(solution)/shard_map/ppermute | solution.py:446
  11.3 0.0 copy-done.6
  11.3 0.0 copy-done.7
  11.4 0.0 copy-start
  11.4 2.5 %middle.1 = (f32[256,256]{1,0:T(8,128)S(1)}, f32[256,256]{1,0:T(8,128)S(1)}, f32[256,256]{1,0:T(8,128)S(1)}, f32[256,256]{1,0:T(8,128)S(1)}, f32[256,256]{1,0:T(...) custom-call(s32[1]{0:T(128)} %bitcast.parity_ref, ...), custom_call_target="tpu_custom_call" | custom-call | flops 3220000000 | bytes 1000000 | tf_op jit(solution)/shard_map/middle/pallas_call | solution.py:108
  13.8 7.5 %collective-permute-start.2 = (f32[32,256]{1,0:T(8,128)S(1)}, f32[32,256]{1,0:T(8,128)S(1)}, u32[]{:S(2)}, u32[]{:S(2)}) collective-permute-start(f32[32,256]{1,0:T(8,128)S(1)} %get-tuple-element.74), channel_id=1, source_target_pairs={{0,1},{1,0},{2,3},{3,2},{4,5},{5,4},{6,7},{7,6},{8,9},{9,8},{10,11... | collective-permute-start | bytes 98312 | tf_op jit(solution)/shard_map/ppermute | solution.py:446
  21.3 0.0 collective-permute-start.3
  21.3 6.9 %collective-permute-start.6 = (f32[256,256]{1,0:T(8,128)S(1)}, f32[256,256]{1,0:T(8,128)S(1)}, u32[]{:S(2)}, u32[]{:S(2)}) collective-permute-start(f32[256,256]{1,0:T(8,128)S(1)} %get-tuple-element.91), channel_id=1, source_target_pairs={{0,1},{1,0},{2,3},{3,2},{4,5},{5,4},{6,7},{7,6},{8,9},{9,8},{10,11... | collective-permute-start | bytes 786440 | tf_op jit(solution)/shard_map/ppermute | solution.py:446
  28.2 0.0 collective-permute-start.7
  28.2 0.0 collective-permute-done.2.in_chip
  28.2 0.0 collective-permute-done.3.cross
  28.3 0.0 copy-done
  28.3 3.0 %turn.1 = (f32[256,256]{1,0:T(8,128)}, f32[8,128]{1,0:T(8,128)S(1)}, f32[256,256]{1,0:T(8,128)S(1)}, f32[256,256]{1,0:T(8,128)S(1)}, f32[256,256]{1,0:T(8,128)S(...) custom-call(s32[1]{0:T(128)} %bitcast.parity_ref, ...), custom_call_target="tpu_custom_call" | custom-call | flops 3449999872 | bytes 1000000 | tf_op jit(solution)/shard_map/turn/pallas_call | solution.py:108
  31.3 1.9 %collective-permute-start.4 = (f32[32,256]{1,0:T(8,128)S(1)}, f32[32,256]{1,0:T(8,128)S(1)}, u32[]{:S(2)}, u32[]{:S(2)}) collective-permute-start(f32[32,256]{1,0:T(8,128)S(1)} %get-tuple-element.85), channel_id=1, source_target_pairs={{0,1},{1,0},{2,3},{3,2},{4,5},{5,4},{6,7},{7,6},{8,9},{9,8},{10,11... | collective-permute-start | bytes 98312 | tf_op jit(solution)/shard_map/ppermute | solution.py:446
  33.2 0.0 collective-permute-start.5
  33.2 0.0 collective-permute-done.6.in_chip.in_chip_state
  33.2 0.8 collective-permute-done.7.cross.cross_state
  34.0 0.8 beside.1
  34.8 0.0 collective-permute-done.4.in_chip
  34.8 2.0 %collective-permute-done.5.cross = f32[32,256]{1,0:T(8,128)S(1)} collective-permute-done((f32[32,256]{1,0:T(8,128)S(1)}, f32[32,256]{1,0:T(8,128)S(1)}, u32[]{:S(2)}, u32[]{:S(2)}) %collective-permute-start.5) | collective-permute-done | bytes 32800 | tf_op jit(solution)/shard_map/ppermute | solution.py:446
  36.8 5.0 %back.1 = (f32[16,40,128]{2,1,0:T(8,128)S(1)}, f32[16,40,128]{2,1,0:T(8,128)S(1)}, f32[256,256]{1,0:T(8,128)}, f32[256,256]{1,0:T(8,128)}, f32[256,256]{1,0:T(8,128)}) custom-call(s32[1]{0:T(128)} %bitcast.parity_ref, f32[256,256]{1,0:T(8,128)S(1)} %get-tuple-element.83.base_ref, f32[256,256]{1,0:T(8,128)S(1)} %get-tuple-element.84.adjoint_ref, ...), custom_call_target="tpu_custom_call" | custom-call | flops 5175000064 | bytes 1000000 | tf_op jit(solution)/shard_map/back/pallas_call | solution.py:108
  41.8 5.1 %collective-permute-start.8 = (f32[16,40,128]{2,1,0:T(8,128)S(1)}, f32[16,40,128]{2,1,0:T(8,128)S(1)}, u32[]{:S(2)}, u32[]{:S(2)}) collective-permute-start(f32[16,40,128]{2,1,0:T(8,128)S(1)} %get-tuple-element.102), channel_id=1, source_target_pairs={{0,1},{1,0},{2,3},{3,2},{4,5},{5,4},{6,7},{7,6},{8,9},{9,8},{10,11... | collective-permute-start | bytes 983048 | tf_op jit(solution)/shard_map/ppermute | solution.py:505
  46.9 1.3 %collective-permute-done.8.got_ref = f32[16,40,128]{2,1,0:T(8,128)S(1)} collective-permute-done((f32[16,40,128]{2,1,0:T(8,128)S(1)}, f32[16,40,128]{2,1,0:T(8,128)S(1)}, u32[]{:S(2)}, u32[]{:S(2)}) %collective-permute-start.8) | collective-permute-done | bytes 327712 | tf_op jit(solution)/shard_map/ppermute | solution.py:505
  48.3 11.2 %all_to_all.15.parts_ref = f32[16,40,128]{2,1,0:T(8,128)S(1)} all-to-all(f32[16,40,128]{2,1,0:T(8,128)S(1)} %chip_sum.1), channel_id=1, replica_groups=mesh['x'=4,'y'=4,'z'=8,'core'=2] {'x','y'}, dimensions={0} | all-to-all | bytes 655360 | tf_op jit(solution)/shard_map/all_to_all | solution.py:506
  59.5 14.7 %all_to_all.16.parts_ref = f32[8,40,128]{2,1,0:T(8,128)S(1)} all-to-all(f32[8,40,128]{2,1,0:T(8,128)S(1)} %plane_sum.1), channel_id=1, replica_groups=mesh['x'=4,'y'=4,'z'=8,'core'=2] {'z'}, dimensions={0} | all-to-all | bytes 327680 | tf_op jit(solution)/shard_map/all_to_all | solution.py:508
  74.2 11.2 %all_to_all.17.own_ref = f32[16,32,128]{2,1,0:T(8,128)S(1)} all-to-all(f32[16,32,128]{2,1,0:T(8,128)S(1)} %get-tuple-element.103), channel_id=1, replica_groups=mesh['x'=4,'y'=4,'z'=8,'core'=2] {'x','y'}, dimensions={0} | all-to-all | bytes 524288 | tf_op jit(solution)/shard_map/all_to_all | solution.py:510
  85.4 4.0 %collective-permute-start.9 = (f32[16,32,128]{2,1,0:T(8,128)S(1)}, f32[16,32,128]{2,1,0:T(8,128)S(1)}, u32[]{:S(2)}, u32[]{:S(2)}) collective-permute-start(f32[16,32,128]{2,1,0:T(8,128)S(1)} %all_to_all.17.own_ref), channel_id=1, source_target_pairs={{0,1},{1,0},{2,3},{3,2},{4,5},{5,4},{6,7},{7,6},{8,9},{9,8},{10,11... | collective-permute-start | bytes 786440 | tf_op jit(solution)/shard_map/ppermute | solution.py:511
  89.4 1.2 %collective-permute-done.9.other_ref = f32[16,32,128]{2,1,0:T(8,128)S(1)} collective-permute-done((f32[16,32,128]{2,1,0:T(8,128)S(1)}, f32[16,32,128]{2,1,0:T(8,128)S(1)}, u32[]{:S(2)}, u32[]{:S(2)}) %collective-permute-start.9) | collective-permute-done | bytes 262176 | tf_op jit(solution)/shard_map/ppermute | solution.py:511
  90.6 1.0 %scale.1 = (f32[256,256]{1,0:T(8,128)}, f32[1,256]{1,0:T(1,128)}, f32[256,256]{1,0:T(8,128)}, f32[1,256]{1,0:T(1,128)}, f32[1,1]{1,0:T(1,128)}) custom-call(s32[1]{0:T(128)} %bitcast.parity_ref, f32[16,32,128]{2,1,0:T(8,128)S(1)} %all_to_all.17.own_ref, f32[16,32,128]{2,1,0:T(8,128)S(1)} %collective-permute-done.9.other_ref, ...), custom_call_target="tpu_custom_call" | custom-call | flops 1150000000 | bytes 1000000 | tf_op jit(solution)/shard_map/scale/pallas_call | solution.py:108
  (3 shorter events, 0.1 us)
Async XLA Ops:
  0.6 0.7 copy-start.1
  0.6 0.7 copy-start.2
  0.7 0.7 copy-start.3
  1.3 0.7 copy-start.4
  4.6 4.2 %collective-permute-start = (f32[40,256]{1,0:T(8,128)S(1)}, f32[40,256]{1,0:T(8,128)S(1)}, u32[]{:S(2)}, u32[]{:S(2)}) collective-permute-start(f32[40,256]{1,0:T(8,128)S(1)} %get-tuple-element.60), channel_id=1, source_target_pairs={{0,1},{1,0},{2,3},{3,2},{4,5},{5,4},{6,7},{7,6},{8,9},{9,8},{10,11... | collective-permute-start | bytes 122888 | tf_op jit(solution)/shard_map/ppermute | solution.py:446
  7.9 3.4 %collective-permute-start.1 = (f32[40,256]{1,0:T(8,128)S(1)}, f32[40,256]{1,0:T(8,128)S(1)}, u32[]{:S(2)}, u32[]{:S(2)}) collective-permute-start(f32[40,256]{1,0:T(8,128)S(1)} %get-tuple-element.61), channel_id=1, source_target_pairs={{0,255},{1,2},{2,1},{3,4},{4,3},{5,6},{6,5},{7,8},{8,7},{9,10},{10... | collective-permute-start | bytes 122888 | tf_op jit(solution)/shard_map/ppermute | solution.py:446
  8.8 0.9 %copy-start.5 = (bf16[512,256]{1,0:T(8,128)(2,1)S(1)}, bf16[512,256]{1,0:T(8,128)(2,1)}, u32[]{:S(2)}) copy-start(bf16[512,256]{1,0:T(8,128)(2,1)} %get-tuple-element.64.inner) | copy-start | bytes 786436
  9.7 1.6 %copy-start.6 = (bf16[512,256]{1,0:T(8,128)(2,1)S(1)}, bf16[512,256]{1,0:T(8,128)(2,1)}, u32[]{:S(2)}) copy-start(bf16[512,256]{1,0:T(8,128)(2,1)} %get-tuple-element.64.inner) | copy-start | bytes 786436
  9.7 1.6 %copy-start.7 = (bf16[4,256,256]{2,1,0:T(8,128)(2,1)S(1)}, bf16[4,256,256]{2,1,0:T(8,128)(2,1)}, u32[]{:S(2)}) copy-start(bf16[4,256,256]{2,1,0:T(8,128)(2,1)} %get-tuple-element.71.near) | copy-start | bytes 1572868
  11.4 16.9 %copy-start = (f32[256,256]{1,0:T(8,128)S(1)}, f32[256,256]{1,0:T(8,128)}, u32[]{:S(2)}) copy-start(f32[256,256]{1,0:T(8,128)} %target_ref.1) | copy-start | bytes 786436
  13.8 14.4 %collective-permute-start.2 = (f32[32,256]{1,0:T(8,128)S(1)}, f32[32,256]{1,0:T(8,128)S(1)}, u32[]{:S(2)}, u32[]{:S(2)}) collective-permute-start(f32[32,256]{1,0:T(8,128)S(1)} %get-tuple-element.74), channel_id=1, source_target_pairs={{0,1},{1,0},{2,3},{3,2},{4,5},{5,4},{6,7},{7,6},{8,9},{9,8},{10,11... | collective-permute-start | bytes 98312 | tf_op jit(solution)/shard_map/ppermute | solution.py:446
  21.3 6.9 %collective-permute-start.3 = (f32[32,256]{1,0:T(8,128)S(1)}, f32[32,256]{1,0:T(8,128)S(1)}, u32[]{:S(2)}, u32[]{:S(2)}) collective-permute-start(f32[32,256]{1,0:T(8,128)S(1)} %get-tuple-element.75), channel_id=1, source_target_pairs={{0,255},{1,2},{2,1},{3,4},{4,3},{5,6},{6,5},{7,8},{8,7},{9,10},{10... | collective-permute-start | bytes 98312 | tf_op jit(solution)/shard_map/ppermute | solution.py:446
  21.3 11.9 %collective-permute-start.6 = (f32[256,256]{1,0:T(8,128)S(1)}, f32[256,256]{1,0:T(8,128)S(1)}, u32[]{:S(2)}, u32[]{:S(2)}) collective-permute-start(f32[256,256]{1,0:T(8,128)S(1)} %get-tuple-element.91), channel_id=1, source_target_pairs={{0,1},{1,0},{2,3},{3,2},{4,5},{5,4},{6,7},{7,6},{8,9},{9,8},{10,11... | collective-permute-start | bytes 786440 | tf_op jit(solution)/shard_map/ppermute | solution.py:446
  28.2 5.8 %collective-permute-start.7 = (f32[256,256]{1,0:T(8,128)S(1)}, f32[256,256]{1,0:T(8,128)S(1)}, u32[]{:S(2)}, u32[]{:S(2)}) collective-permute-start(f32[256,256]{1,0:T(8,128)S(1)} %get-tuple-element.91), channel_id=1, source_target_pairs={{0,255},{1,2},{2,1},{3,4},{4,3},{5,6},{6,5},{7,8},{8,7},{9,10},{10... | collective-permute-start | bytes 786440 | tf_op jit(solution)/shard_map/ppermute | solution.py:446
  31.3 3.5 %collective-permute-start.4 = (f32[32,256]{1,0:T(8,128)S(1)}, f32[32,256]{1,0:T(8,128)S(1)}, u32[]{:S(2)}, u32[]{:S(2)}) collective-permute-start(f32[32,256]{1,0:T(8,128)S(1)} %get-tuple-element.85), channel_id=1, source_target_pairs={{0,1},{1,0},{2,3},{3,2},{4,5},{5,4},{6,7},{7,6},{8,9},{9,8},{10,11... | collective-permute-start | bytes 98312 | tf_op jit(solution)/shard_map/ppermute | solution.py:446
  33.2 3.6 %collective-permute-start.5 = (f32[32,256]{1,0:T(8,128)S(1)}, f32[32,256]{1,0:T(8,128)S(1)}, u32[]{:S(2)}, u32[]{:S(2)}) collective-permute-start(f32[32,256]{1,0:T(8,128)S(1)} %get-tuple-element.86), channel_id=1, source_target_pairs={{0,255},{1,2},{2,1},{3,4},{4,3},{5,6},{6,5},{7,8},{8,7},{9,10},{10... | collective-permute-start | bytes 98312 | tf_op jit(solution)/shard_map/ppermute | solution.py:446
  41.8 6.4 %collective-permute-start.8 = (f32[16,40,128]{2,1,0:T(8,128)S(1)}, f32[16,40,128]{2,1,0:T(8,128)S(1)}, u32[]{:S(2)}, u32[]{:S(2)}) collective-permute-start(f32[16,40,128]{2,1,0:T(8,128)S(1)} %get-tuple-element.102), channel_id=1, source_target_pairs={{0,1},{1,0},{2,3},{3,2},{4,5},{5,4},{6,7},{7,6},{8,9},{9,8},{10,11... | collective-permute-start | bytes 983048 | tf_op jit(solution)/shard_map/ppermute | solution.py:505
  85.4 5.2 %collective-permute-start.9 = (f32[16,32,128]{2,1,0:T(8,128)S(1)}, f32[16,32,128]{2,1,0:T(8,128)S(1)}, u32[]{:S(2)}, u32[]{:S(2)}) collective-permute-start(f32[16,32,128]{2,1,0:T(8,128)S(1)} %all_to_all.17.own_ref), channel_id=1, source_target_pairs={{0,1},{1,0},{2,3},{3,2},{4,5},{5,4},{6,7},{7,6},{8,9},{9,8},{10,11... | collective-permute-start | bytes 786440 | tf_op jit(solution)/shard_map/ppermute | solution.py:511

commit v3 on v2

--- a/solution.py
+++ b/solution.py
@@ -112,7 +112,7 @@
         out_specs=[pl.BlockSpec(memory_space=pltpu.VMEM)] * len(outs),
         scratch_shapes=scratch,
         cost_estimate=pl.CostEstimate(flops=int(micros * 1.15e9), bytes_accessed=reads, transcendentals=0),
-        compiler_params=pltpu.CompilerParams(vmem_limit_bytes=limit * 1024 * 1024),
+        compiler_params=pltpu.CompilerParams(vmem_limit_bytes=int(limit * 1048576)),
         name=name,
     )(*args))
 
@@ -121,16 +121,18 @@
 PAIR = ((2, 256, 256), BF16)
 EXTRA = ((8, 128), F32)
 PACKED = ((16, 40, 128), F32)
-COLUMN = ((256, 128), F32)
 
 
 def edges(values):
     return values[0:16], values[48:64], values[64:80], values[112:128]
 
 
-def leaving(values):
-    p_low, p_high, u_low, u_high = edges(values)
-    return 3.0 * (p_high + u_high), 3.0 * (p_low - u_low)
+def edge_rows(values):
+    return jnp.concatenate(edges(values), axis=0)
+
+
+def leaving(edge):
+    return 3.0 * (edge[16:32] + edge[48:64]), 3.0 * (edge[0:16] - edge[32:48])
 
 
 def put(parity, upward, downward, in_chip_ref, cross_ref, rows=0):
@@ -160,10 +162,16 @@
     return (rows == column).astype(F32).astype(BF16)
 
 
+def make_near(nbr_ref, near):
+    rows = lax.broadcasted_iota(jnp.int32, (256, 256), 0)
+    for face in range(2, 6):
+        near[face - 2] = one_hot(rows + 256 * (face ^ 1), nbr_ref[face : face + 1])
+
+
 def first_kernel(
     parity_ref, state_far, w_in_far, nbr_far, fixed_far, b_in_far, w_out_far, b_out_far, send_far,
-    next_ref, hidden_ref, in_chip_ref, cross_ref, w_in, b_in, w_out, b_out, near, state_ref, nbr_ref,
-    inner, leave, lift, lift_t, w_in_ref, b_in_ref, w_out_ref, b_out_ref, send_ref, sems,
+    arrived_ref, hidden_ref, in_chip_ref, cross_ref, w_in, w_out, state_ref, nbr_ref, inner, leave, lift, lift_t,
+    w_in_ref, b_in_ref, w_out_ref, b_out_ref, send_ref, near, sems,
 ):
     pairs = (
         (state_far, state_ref), (w_in_far, w_in_ref), (b_in_far, b_in_ref), (fixed_far.at[512:576], leave),
@@ -175,24 +183,24 @@
         copy.start()
     copies[0].wait()
     values = state_ref[...]
+    edge = edge_rows(values)
+    parts = split(values)
     parity = parity_ref[0]
-    put(parity, *leaving(state_ref), in_chip_ref, cross_ref)
+    put(parity, *leaving(edge), in_chip_ref, cross_ref)
     copies[1].wait()
     w_in[0], w_in[1] = split(w_in_ref[...])
     for copy in copies[2:5]:
         copy.wait()
-    rows = lax.broadcasted_iota(jnp.int32, (256, 256), 0)
-    for face in range(2, 6):
-        near[face - 2] = one_hot(rows + 256 * (face ^ 1), nbr_ref[face : face + 1])
+    make_near(nbr_ref, near)
+    arrive_near(parts, leave, near, arrived_ref)
+    hidden = jnp.tanh(mm3(pair(w_in), parts) + wide(b_in_ref))
+    hidden_ref[...] = hidden
     for copy in copies[5:]:
         copy.wait()
     lift[...] = flip(lift_t[...])
     w_out[0], w_out[1] = split(w_out_ref[...])
-    for row_ref, ref in ((b_in_ref, b_in), (b_out_ref, b_out)):
-        ref[...] = jnp.broadcast_to(row_ref[...], (128, 256)).T
-    rates = local_rates(values, (w_in, b_in, w_out, b_out, inner, leave, lift, near), hidden_ref)
-    next_ref[...] = values + TIME_STEP * rates
-    put(parity, *leaving(next_ref), in_chip_ref, cross_ref, 16)
+    rates = edge_rates(parts, split(hidden), (w_in, b_in_ref, w_out, b_out_ref, inner, leave, lift, near), arrived_ref)
+    put(parity, *leaving(edge + TIME_STEP * rates), in_chip_ref, cross_ref, 16)
     down_index = send_ref[0:1].astype(F32)
     up_index = (send_ref[1:2] - 256).astype(F32)
     even = parity == 0
@@ -205,37 +213,73 @@
 
 
 def tables_kernel(
-    w_in, w_out, inner, leave, nbr_ref, state_ref, after_ref, in_t_ref, out_t_ref, inner_t, leave_t, far_ref, copy_ref
+    w_in, b_in, w_out, b_out, inner, leave, lift, nbr_ref, state_ref, arrived_ref, hidden_ref, after_ref,
+    next_ref, in_t_ref, out_t_ref, inner_t, leave_t, near, far_ref, eff_ref, copy_ref, column_in, column_out,
 ):
-    copy_ref[...] = state_ref[...]
+    column_in[...] = column(b_in)
+    column_out[...] = column(b_out)
+    values = state_ref[...]
+    copy_ref[...] = values
+    network = (w_in, b_in, w_out, b_out, inner, leave, lift, near)
+    next_ref[...] = values + TIME_STEP * full_rates(split(values), split(hidden_ref[...]), network, arrived_ref)
+    make_near(nbr_ref, near)
+    rows = lax.broadcasted_iota(jnp.int32, (256, 256), 0)
+    for face in range(2):
+        far_ref[face] = one_hot(rows + (1536 + 256 * face), nbr_ref[face : face + 1])
     for part in range(2):
         in_t_ref[part] = flip(w_in[part])
         out_t_ref[part] = flip(w_out[part])
         inner_t[256 * part : 256 * part + 256] = flip(inner[256 * part : 256 * part + 256])
     leave_t[...] = flip(leave[...])
-    rows = lax.broadcasted_iota(jnp.int32, (256, 256), 0)
-    for face in range(2):
-        far_ref[face] = one_hot(rows + (1536 + 256 * face), nbr_ref[face : face + 1])
-
-
-def wide(column):
-    return jnp.concatenate([column[...], column[...]], axis=1)
-
-
-def local_rates(values, network, hidden_ref):
+    whole = w_out[0].astype(F32) + w_out[1].astype(F32)
+    for side, seen in enumerate((whole[48:64] + whole[112:128], whole[0:16] - whole[64:80])):
+        high, low = split(seen.T)
+        eff_ref[side] = jnp.concatenate([high, high, low], axis=1)
+
+
+def column(row):
+    return jnp.broadcast_to(row[...], (128, 256)).T
+
+
+def wide(bias):
+    values = column(bias) if bias.shape[0] == 1 else bias[...]
+    return jnp.concatenate([values, values], axis=1)
+
+
+def gather(high, low, near, dot):
+    for n in range(4):
+        both = jnp.concatenate([high[16 * n : 16 * n + 16], low[16 * n : 16 * n + 16]], axis=0)
+        yield dot(both, near[n])
+
+
+def arrive_near(parts, leave, near, arrived_ref):
+    high, low = split(mm(leave[...], parts[0]) + mm(leave[...], parts[1]))
+    for n, both in enumerate(gather(high, low, near, mm)):
+        both = both.astype(BF16)
+        arrived_ref[0, 16 * n : 16 * n + 16] = both[0:16]
+        arrived_ref[1, 16 * n : 16 * n + 16] = both[16:32]
+
+
+def edge_rates(parts, hidden_parts, network, arrived_ref):
     w_in, b_in, w_out, b_out, inner, leave, lift, near = network
-    parts = split(values)
+    rates = mm3([edge_rows(x) for x in pair(inner)], parts) + edge_rows(wide(b_out))
+    rates += mm(edge_rows(lift), arrived_ref[0]) + mm(edge_rows(lift), arrived_ref[1])
+    return rates + mm3([edge_rows(x) for x in pair(w_out)], hidden_parts)
+
+
+def full_rates(parts, hidden_parts, network, arrived_ref):
+    w_in, b_in, w_out, b_out, inner, leave, lift, near = network
+    rates = mm3(pair(inner), parts) + wide(b_out)
+    rates += mm(lift[...], arrived_ref[0]) + mm(lift[...], arrived_ref[1])
+    return rates + mm3(pair(w_out), hidden_parts)
+
+
+def activate(parts, network, hidden_ref, arrived_ref):
+    w_in, b_in, w_out, b_out, inner, leave, lift, near = network
     hidden = jnp.tanh(mm3(pair(w_in), parts) + wide(b_in))
     hidden_ref[...] = hidden
-    rates = mm3(pair(inner), parts) + wide(b_out)
-    high, low = split(mm(leave[...], parts[0]) + mm(leave[...], parts[1]))
-    arrived = []
-    for n in range(4):
-        both = jnp.concatenate([high[16 * n : 16 * n + 16], low[16 * n : 16 * n + 16]], axis=0)
-        arrived.append(mm(both, near[n]).astype(BF16))
-    for part in range(2):
-        rates += mm(lift[...], jnp.concatenate([a[16 * part : 16 * part + 16] for a in arrived], axis=0))
-    return rates + mm3(pair(w_out), split(hidden))
+    arrive_near(parts, leave, near, arrived_ref)
+    return split(hidden)
 
 
 def add_arrived(weight, base_ref, below, above, link, now_ref):
@@ -249,7 +293,7 @@
 def middle_kernel(
     parity_ref, base_ref, state_ref, in_chip, cross, far_ref,
     w_in, b_in, w_out, b_out, inner, leave, lift, near,
-    second_ref, third_ref, hidden_second, hidden_third, next_ref, link, in_chip_out, cross_out, between,
+    second_ref, third_ref, hidden_second, hidden_third, arrived_ref, link, in_chip_out, cross_out, between,
 ):
     network = (w_in, b_in, w_out, b_out, inner, leave, lift, near)
     parity = parity_ref[0]
@@ -258,77 +302,109 @@
     for side, received in enumerate((below, above)):
         link[side] = mm(one_hot(rows, received[32:33]), far_ref[side]).astype(BF16)
     values = add_arrived(TIME_STEP, base_ref, below[0:16], above[0:16], link, second_ref)
-    between[...] = 0.5 * (state_ref[...] + values) + HALF_STEP * local_rates(values, network, hidden_second)
-    put(parity, *leaving(between), in_chip_out, cross_out)
+    parts = split(values)
+    hidden_parts = activate(parts, network, hidden_second, arrived_ref)
+    rates = full_rates(parts, hidden_parts, network, arrived_ref)
+    between[...] = 0.5 * (state_ref[...] + values) + HALF_STEP * rates
+    put(parity, *leaving(edge_rows(between)), in_chip_out, cross_out)
     values = add_arrived(HALF_STEP, between, below[16:32], above[16:32], link, third_ref)
-    next_ref[...] = values + TIME_STEP * local_rates(values, network, hidden_third)
-    put(parity, *leaving(next_ref), in_chip_out, cross_out, 16)
-
-
-def sensitivities(values, link):
-    p_low, p_high, u_low, u_high = edges(values)
-    return pick(p_high - u_high, link[1], mm_nt), pick(p_low + u_low, link[0], mm_nt)
+    parts = split(values)
+    hidden_parts = activate(parts, network, hidden_third, arrived_ref)
+    rates = edge_rates(parts, hidden_parts, network, arrived_ref)
+    put(parity, *leaving(edge_rows(values) + TIME_STEP * rates), in_chip_out, cross_out, 16)
+
+
+def rest_kernel(
+    third_ref, hidden_ref, arrived_ref, w_in, b_in, w_out, b_out, inner, leave, lift, near, next_ref
+):
+    network = (w_in, b_in, w_out, b_out, inner, leave, lift, near)
+    values = third_ref[...]
+    next_ref[...] = values + TIME_STEP * full_rates(split(values), split(hidden_ref[...]), network, arrived_ref)
+
+
+def sensitivities(edge, link):
+    upward = pick(edge[16:32] - edge[48:64], link[1], mm_nt)
+    return upward, pick(edge[0:16] + edge[32:48], link[0], mm_nt)
 
 
 def through_closure(parts, hidden, w_out_t):
     return (1.0 - hidden * hidden) * mm3(w_out_t, parts)
 
 
-def back_rates(parts, delta_parts, network):
+def gather_back(parts, lift_t, near):
+    high, low = split(mm(lift_t[...], parts[0]) + mm(lift_t[...], parts[1]))
+    return split(jnp.concatenate([a[0:16] + a[16:32] for a in gather(high, low, near, mm_nt)], axis=0))
+
+
+def back_rates(parts, delta_parts, network, gathered, rows=lambda values: values[...]):
     w_in_t, inner_t, leave_t, lift_t, near = network
-    rates = mm3(pair(inner_t), parts) + mm3(pair(w_in_t), delta_parts)
-    high, low = split(mm(lift_t[...], parts[0]) + mm(lift_t[...], parts[1]))
-    arrived = []
-    for n in range(4):
-        both = jnp.concatenate([high[16 * n : 16 * n + 16], low[16 * n : 16 * n + 16]], axis=0)
-        arrived.append(mm_nt(both, near[n]))
-    high, low = split(jnp.concatenate([a[0:16] + a[16:32] for a in arrived], axis=0))
-    return rates + (mm(leave_t[...], high) + mm(leave_t[...], low))
+    rates = mm3([rows(x) for x in pair(inner_t)], parts) + mm3([rows(x) for x in pair(w_in_t)], delta_parts)
+    return rates + (mm(rows(leave_t), gathered[0]) + mm(rows(leave_t), gathered[1]))
 
 
 def turn_kernel(
     parity_ref, base_ref, third_ref, in_chip, cross, link, target_ref,
     w_in, b_in, w_out, b_out, inner, leave, lift, near, w_in_t, w_out_t, inner_t, leave_t, lift_t,
-    final_ref, loss_ref, fourth_ref, hidden_ref, adjoint_ref, delta_ref, next_ref, in_chip_out, cross_out, between,
+    final_ref, loss_ref, fourth_ref, hidden_ref, adjoint_ref, delta_ref, gathered_ref, in_chip_out, cross_out,
+    between, arrived_ref,
 ):
     network = (w_in, b_in, w_out, b_out, inner, leave, lift, near)
     parity = parity_ref[0]
     below, above = take(parity, in_chip[...], cross[...])
     values = add_arrived(TIME_STEP, base_ref, below[0:16], above[0:16], link, fourth_ref)
-    between[...] = 0.5 * (third_ref[...] + values) + HALF_STEP * local_rates(values, network, hidden_ref)
+    parts = split(values)
+    hidden_parts = activate(parts, network, hidden_ref, arrived_ref)
+    rates = full_rates(parts, hidden_parts, network, arrived_ref)
+    between[...] = 0.5 * (third_ref[...] + values) + HALF_STEP * rates
     final = add_arrived(HALF_STEP, between, below[16:32], above[16:32], link, final_ref)
     mismatch = final - target_ref[...]
     adjoint = (HALF_STEP / COUNT) * mismatch
     adjoint_ref[...] = adjoint
     squares = jnp.sum(mismatch * mismatch, axis=0, keepdims=True)
     loss_ref[...] = jnp.broadcast_to(squares[:, 0:128] + squares[:, 128:256], (8, 128))
-    put(parity, *sensitivities(adjoint_ref, link), in_chip_out, cross_out)
+    edge = edge_rows(adjoint)
+    put(parity, *sensitivities(edge, link), in_chip_out, cross_out)
     parts = split(adjoint)
     delta = through_closure(parts, hidden_ref[...], pair(w_out_t))
     delta_ref[...] = delta
-    next_ref[...] = adjoint + TIME_STEP * back_rates(parts, split(delta), (w_in_t, inner_t, leave_t, lift_t, near))
-    put(parity, *sensitivities(next_ref, link), in_chip_out, cross_out, 16)
-
-
-def gradients(parts, delta_parts, state, hidden):
-    ones = jnp.ones((8, 256), BF16)
+    gathered = gather_back(parts, lift_t, near)
+    gathered_ref[0], gathered_ref[1] = gathered
+    back = (w_in_t, inner_t, leave_t, lift_t, near)
+    rates = back_rates(parts, split(delta), back, gathered, edge_rows)
+    put(parity, *sensitivities(edge + TIME_STEP * rates, link), in_chip_out, cross_out, 16)
+
+
+def bias_rows(first, second):
     rows = lax.broadcasted_iota(jnp.int32, (8, 128), 0)
-    first = mm_nt(ones, delta_parts[0]) + mm_nt(ones, delta_parts[1])
-    second = mm_nt(ones, parts[0]) + mm_nt(ones, parts[1])
     bias = jnp.where(rows == 0, first[:, 0:128], jnp.where(rows == 1, first[:, 128:256], 0.0))
     bias = jnp.where(rows == 2, second[:, 0:128], bias)
     if second.shape[1] == 256:
         bias = jnp.where(rows == 3, second[:, 128:256], bias)
+    return bias
+
+
+def row_sums(parts):
+    ones = jnp.ones((8, 256), BF16)
+    return mm_nt(ones, parts[0]) + mm_nt(ones, parts[1])
+
+
+def gradients(parts, delta_parts, state, hidden):
+    bias = bias_rows(row_sums(delta_parts), row_sums(parts))
     return mm3(delta_parts, split(state), mm_nt), mm3(parts, split(hidden), mm_nt), bias
 
 
 def beside_kernel(
-    adjoint_ref, delta_ref, state_ref, hidden_ref, in_chip, cross, w_in, b_in,
-    grad_in, grad_out, extra, in_chip_hidden, cross_hidden,
+    adjoint_ref, delta_ref, gathered_ref, state_ref, hidden_ref, in_chip, cross, w_in, b_in,
+    w_in_t, inner_t, leave_t, lift_t, near,
+    next_ref, grad_in, grad_out, extra, in_chip_hidden, cross_hidden,
 ):
-    grad_in[...], grad_out[...], extra[...] = gradients(
-        split(adjoint_ref[...]), split(delta_ref[...]), state_ref[...], hidden_ref[...]
-    )
+    adjoint = adjoint_ref[...]
+    parts, delta_parts = split(adjoint), split(delta_ref[...])
+    gathered = gathered_ref[0], gathered_ref[1]
+    next_ref[...] = adjoint + TIME_STEP * back_rates(
+        parts, delta_parts, (w_in_t, inner_t, leave_t, lift_t, near), gathered
+    )
+    grad_in[...], grad_out[...], extra[...] = gradients(parts, delta_parts, state_ref[...], hidden_ref[...])
     for source, ref in ((in_chip, in_chip_hidden), (cross, cross_hidden)):
         ref[...] = jnp.tanh(mm3(pair(w_in), split(source[...])) + wide(b_in))
 
@@ -337,7 +413,7 @@
     parity_ref, base_ref, adjoint_ref, in_chip, cross, link,
     third_ref, hidden_third, second_ref, hidden_second, state_ref, hidden_first,
     in_chip_state, cross_state, in_chip_hidden, cross_hidden,
-    near, w_in_t, w_out_t, inner_t, leave_t, lift_t, old_in, old_out, old_extra, loss_ref,
+    near, w_in_t, w_out_t, inner_t, leave_t, lift_t, eff, old_in, old_out, old_extra, loss_ref,
     keep_ref, send_ref, now_ref, between, sum_ref,
 ):
     network = (w_in_t, inner_t, leave_t, lift_t, near)
@@ -352,46 +428,45 @@
         add_edges(now_ref, low, high, -low, high)
         return now_ref[...]
 
-    def gather(*args):
+    def collect(*args):
         for n, term in enumerate(gradients(*args)):
             totals[n] = totals[n] + term
 
     values = arrive(base_ref, 3.0 * TIME_STEP, below[0:16], above[0:16])
     parts = split(values)
     delta = split(through_closure(parts, hidden_third[...], pair(w_out_t)))
-    between[...] = 0.5 * (adjoint_ref[...] + values) + HALF_STEP * back_rates(parts, delta, network)
-    gather(parts, delta, third_ref[...], hidden_third[...])
-    upward, downward = sensitivities(between, link)
+    rates = back_rates(parts, delta, network, gather_back(parts, lift_t, near))
+    between[...] = 0.5 * (adjoint_ref[...] + values) + HALF_STEP * rates
+    collect(parts, delta, third_ref[...], hidden_third[...])
+    upward, downward = sensitivities(edge_rows(between), link)
 
     values = arrive(between, 3.0 * HALF_STEP, below[16:32], above[16:32])
     parts = split(values)
     delta = split(through_closure(parts, hidden_second[...], pair(w_out_t)))
-    values = values + TIME_STEP * back_rates(parts, delta, network)
-    gather(parts, delta, second_ref[...], hidden_second[...])
+    values = values + TIME_STEP * back_rates(parts, delta, network, gather_back(parts, lift_t, near))
+    collect(parts, delta, second_ref[...], hidden_second[...])
+
+    states = take(parity, in_chip_state[...], cross_state[...])
+    hiddens = take(parity, in_chip_hidden[...], cross_hidden[...])
+    weight = 3.0 * TIME_STEP
+    blocks = []
+    for side, received in enumerate((weight * downward, weight * upward)):
+        high, low = split(received)
+        hidden = hiddens[side]
+        seen = mm(eff[side], jnp.concatenate([high, low, high], axis=0))
+        delta = split((1.0 - hidden * hidden) * seen)
+        totals[0] = totals[0] + mm3(delta, split(states[side]), mm_nt)
+        blocks.append(mm3((high, low), split(hidden), mm_nt))
+        none = jnp.zeros((48, 256), F32)
+        spread = [none, received, none, received] if side == 0 else [received, none, -received, none]
+        totals[2] = totals[2] + bias_rows(row_sums(delta), row_sums(split(jnp.concatenate(spread, axis=0))))
 
     parts = split(values)
     delta = split(through_closure(parts, hidden_first[...], pair(w_out_t)))
-    gather(parts, delta, state_ref[...], hidden_first[...])
-
-    states = take(parity, in_chip_state[...], cross_state[...])
-    hiddens = take(parity, in_chip_hidden[...], cross_hidden[...])
-    w_edge = w_out_t[0, :, 0:128], w_out_t[1, :, 0:128]
-    weight = 3.0 * TIME_STEP
-    none = jnp.zeros((48, 256), F32)
-    low, high = weight * upward, weight * downward
-    for values, state, hidden in (
-        (jnp.concatenate([none, high, none, high], axis=0), states[0], hiddens[0]),
-        (jnp.concatenate([low, none, -low, none], axis=0), states[1], hiddens[1]),
-    ):
-        parts = split(values)
-        delta = split(through_closure(parts, hidden, w_edge))
-        first, second, bias = gradients(parts, delta, state, hidden)
-        totals[0] = totals[0] + first
-        totals[2] = totals[2] + bias
-        sum_ref[...] = totals[1]
-        sum_ref[0:128] += second
-        totals[1] = sum_ref[...]
-    first, second, bias = totals
+    collect(parts, delta, state_ref[...], hidden_first[...])
+    sum_ref[...] = totals[1]
+    add_edges(sum_ref, blocks[1], blocks[0], -blocks[1], blocks[0])
+    first, second, bias = totals[0], sum_ref[...], totals[2]
     rows = lax.broadcasted_iota(jnp.int32, (8, 128), 0)
     bias = jnp.where(rows == 4, loss_ref[...], bias)
     for ref, values in ((keep_ref, jnp.where(even, first, second)), (send_ref, jnp.where(even, second, first))):
@@ -449,57 +524,61 @@
 def local(state, target, w_in, b_in, w_out, b_out, nbr, send):
     parity = lax.axis_index("core").reshape(1)
     inner, leave, lift = operators()
-    weights = [PAIR, COLUMN, PAIR, COLUMN]
     fixed = np.concatenate([*halves(inner), leave, lift.T], axis=0).astype(ml_dtypes.bfloat16)
-    line = lambda values: values.reshape(1, 256)
+    b_in, b_out = b_in.reshape(1, 256), b_out.reshape(1, 256)
     tall, flat, thin = ((512, 256), BF16), ((64, 256), BF16), ((256, 64), BF16)
-    base, hidden_first, *edge, w_in2, b_in2, w_out2, b_out2, near, state, nbr, inner2, leave1, lift1, lift_t = call(
+    arrival = ((2, 64, 256), BF16)
+    arrived, hidden_first, *edge, w_in2, w_out2, state, nbr, inner2, leave1, lift1, lift_t = call(
         first_kernel,
-        [SQUARE, SQUARE, ((40, 256), F32), ((40, 256), F32)]
-        + weights
-        + [((4, 256, 256), BF16), SQUARE, ((6, 256), jnp.int32), tall, flat, thin, flat],
-        parity, state, w_in, nbr, jnp.asarray(fixed), line(b_in), w_out, line(b_out), send,
+        [arrival, SQUARE, ((40, 256), F32), ((40, 256), F32), PAIR, PAIR, SQUARE, ((6, 256), jnp.int32)]
+        + [tall, flat, thin, flat],
+        parity, state, w_in, nbr, jnp.asarray(fixed), b_in, w_out, b_out, send,
         name="first", micros=1.5,
         far=range(1, 9),
-        limit=52,
+        limit=52.25,
         scratch=[
             pltpu.VMEM((256, 256), F32), pltpu.VMEM((1, 256), F32), pltpu.VMEM((256, 256), F32),
-            pltpu.VMEM((1, 256), F32), pltpu.VMEM((2, 256), jnp.int32), pltpu.SemaphoreType.DMA((10,)),
+            pltpu.VMEM((1, 256), F32), pltpu.VMEM((2, 256), jnp.int32), pltpu.VMEM((4, 256, 256), BF16),
+            pltpu.SemaphoreType.DMA((10,)),
         ],
     )
     got = exchange(*edge)
-    w_in_t, w_out_t, inner_t, leave_t, far, copy = call(
+    base, w_in_t, w_out_t, inner_t, leave_t, near, far, eff, copy, b_in2, b_out2 = call(
         tables_kernel,
-        [PAIR, PAIR, tall, thin, PAIR, SQUARE],
-        w_in2, w_out2, inner2, leave1, nbr, state, got[0],
-        name="tables", micros=0.4,
+        [SQUARE, PAIR, PAIR, tall, thin, ((4, 256, 256), BF16), PAIR, ((2, 256, 48), BF16), SQUARE] + [((256, 128), F32)] * 2,
+        w_in2, b_in, w_out2, b_out, inner2, leave1, lift1, nbr, state, arrived, hidden_first, got[0],
+        name="tables", micros=1,
     )
     beside = exchange(copy, copy)
     network = (w_in2, b_in2, w_out2, b_out2, inner2, leave1, lift1, near)
-    back = (w_in_t, w_out_t, inner_t, leave_t, lift_t)
+    back = (w_in_t, inner_t, leave_t, lift_t)
     edge_shapes = [((32, 256), F32)] * 2
-    second, third, hidden_second, hidden_third, base, link, *edge, _ = call(
+    second, third, hidden_second, hidden_third, arrived, link, *edge, _ = call(
         middle_kernel,
-        [SQUARE] * 5 + [PAIR] + edge_shapes + [SQUARE],
-        parity, base, state, *got, far, *network, name="middle", micros=2.8,
+        [SQUARE] * 4 + [arrival, PAIR] + edge_shapes + [SQUARE],
+        parity, base, state, *got, far, *network, name="middle", micros=2.4,
     )
     got = exchange(*edge)
-    final, loss, fourth, hidden_fourth, adjoint, delta, base, *edge, _ = call(
+    (base,) = call(rest_kernel, [SQUARE], third, hidden_third, arrived, *network, name="rest", micros=0.6)
+    final, loss, fourth, hidden_fourth, adjoint, delta, gathered, *edge, _, _ = call(
         turn_kernel,
-        [SQUARE, EXTRA] + [SQUARE] * 5 + edge_shapes + [SQUARE],
-        parity, base, third, *got, link, target, *network, *back, name="turn", micros=3,
+        [SQUARE, EXTRA] + [SQUARE] * 4 + [arrival] + edge_shapes + [SQUARE, arrival],
+        parity, base, third, *got, link, target, *network, w_in_t, w_out_t, inner_t, leave_t, lift_t,
+        name="turn", micros=3,
     )
     got = exchange(*edge)
-    *grads, in_chip_hidden, cross_hidden = call(
+    base, *grads, in_chip_hidden, cross_hidden = call(
         beside_kernel,
-        [SQUARE, SQUARE, EXTRA, SQUARE, SQUARE],
-        adjoint, delta, fourth, hidden_fourth, *beside, w_in2, b_in2, name="beside", micros=0.8,
+        [SQUARE, SQUARE, SQUARE, EXTRA, SQUARE, SQUARE],
+        adjoint, delta, gathered, fourth, hidden_fourth, *beside, w_in2, b_in2, *back, near,
+        name="beside", micros=1.3,
     )
     keep, give, *_ = call(
         back_kernel,
         [PACKED] * 2 + [SQUARE] * 3,
         parity, base, adjoint, *got, link, third, hidden_third, second, hidden_second, state, hidden_first,
-        *beside, in_chip_hidden, cross_hidden, near, *back, *grads, loss, name="back", micros=4.5,
+        *beside, in_chip_hidden, cross_hidden, near, w_in_t, w_out_t, inner_t, leave_t, lift_t, eff, *grads, loss,
+        name="back", micros=4.5,
     )
     swap = [(0, 1), (1, 0)]
     (parts,) = call(chip_kernel, [PACKED], keep, lax.ppermute(give, "core", swap), name="chip_sum", micros=0.3)

time: 91.9 us -> 90.5 us (0.985)
  waiting for transfers between devices: 7.39 us -> 8.45 us
  starting transfers between devices: 28.8 us -> 27.8 us
  local copies, waits for them, and re-layouts: 2.32 us -> 1.37 us
    ppermute x4, starting transfers between devices: 19.7 us -> 17.3 us  [exchange(): lax.ppermute(in_chip, AXES, IN_CHIP)]
    ppermute x4, starting transfers between devices: 0.01 us -> 1.07 us  [exchange(): lax.ppermute(cross, AXES, CROSS)]
    unnamed x16 -> x10, local copies, waits for them, and re-layouts: 2.32 us -> 1.37 us
    pallas_call x10 -> x11, Pallas kernels: 15.3 us -> 14.9 us  [call(): pl.pallas_call(body, out_shape=[jax.ShapeDtypeStruct(s, t) for s, t in ou...]
  transfers between devices with their start and end apart: 10 -> 10, of which waited for: 6 -> 6; matrix products, arithmetic and copies ran while one was open for 0% -> 0% of each run, Pallas kernels for 5% -> 8%
where the time goes in v3:
time: 90.5 us; the launch traced here: 90.2 us
  blocking collectives  37 us (41%)
  starting transfers between devices  27.8 us (31%)
  Pallas kernels  14.9 us (16%)
  waiting for transfers between devices  8.45 us (9%)
  local copies, waits for them, and re-layouts  1.37 us (2%)
    ppermute x4, starting transfers between devices, exchange(): lax.ppermute(in_chip, AXES, IN_CHIP)  17.3 us
    pallas_call x11, Pallas kernels, call(): pl.pallas_call(body, out_shape=[jax.ShapeDtypeStruct(s, t) for s, t in ou...  14.9 us
    all_to_all x1, blocking collectives, local(): parts = lax.all_to_all(parts, 'z', 0, 0, tiled=True)  14.6 us
    all_to_all x1, blocking collectives, local(): parts = lax.all_to_all(parts, PLANE, 0, 0, tiled=True)  11.2 us
    all_to_all x1, blocking collectives, local(): own = lax.all_to_all(parts, PLANE, 0, 0, tiled=True)  11.2 us
    ppermute x1, starting transfers between devices, local(): lax.ppermute(give, 'core', swap)  5.43 us
    ppermute x4, waiting for transfers between devices, exchange(): lax.ppermute(cross, AXES, CROSS)  4.52 us
    ppermute x1, starting transfers between devices, local(): other = lax.ppermute(own, 'core', swap)  4.01 us
  transfers between devices with their start and end apart: 10, of which 6 were waited for; matrix products, arithmetic and copies ran while one was open for 0% of the time, Pallas kernels for 8%

profile of v3, /device:TPU:1, one launch (start us, length us, event | category | flops | bytes accessed | tf_op | source)
XLA Modules:
  0.0 90.2 jit_solution(9546962241162056891)
XLA Ops:
  0.6 0.0 copy-start.1
  0.6 0.0 copy-start.2
  0.7 0.0 copy-start.3
  0.7 0.7 copy-done.1
  1.3 0.0 copy-done.2
  1.3 0.0 copy-done.3
  1.3 0.0 copy-start.4
  1.3 0.7 copy-done.4
  2.0 2.1 %first.1 = (bf16[2,64,256]{2,1,0:T(8,128)(2,1)S(1)}, f32[256,256]{1,0:T(8,128)S(1)}, f32[40,256]{1,0:T(8,128)S(1)}, f32[40,256]{1,0:T(8,128)S(1)}, bf16[2,256,25...) custom-call(s32[1]{0:T(128)} %bitcast.parity_ref, ...), custom_call_target="tpu_custom_call" | custom-call | flops 1724999936 | bytes 1000000 | tf_op jit(solution)/shard_map/first/pallas_call | solution.py:108
  4.2 3.3 %collective-permute-start = (f32[40,256]{1,0:T(8,128)S(1)}, f32[40,256]{1,0:T(8,128)S(1)}, u32[]{:S(2)}, u32[]{:S(2)}) collective-permute-start(f32[40,256]{1,0:T(8,128)S(1)} %get-tuple-element.70), channel_id=1, source_target_pairs={{0,1},{1,0},{2,3},{3,2},{4,5},{5,4},{6,7},{7,6},{8,9},{9,8},{10,11... | collective-permute-start | bytes 122888 | tf_op jit(solution)/shard_map/ppermute | solution.py:521
  7.5 0.0 collective-permute-start.1
  7.5 0.9 collective-permute-done.after_ref.in_chip
  8.4 0.8 tables.1
  9.1 1.0 %collective-permute-start.5 = (f32[256,256]{1,0:T(8,128)S(1)}, f32[256,256]{1,0:T(8,128)S(1)}, u32[]{:S(2)}, u32[]{:S(2)}) collective-permute-start(f32[256,256]{1,0:T(8,128)S(1)} %get-tuple-element.94), channel_id=1, source_target_pairs={{0,255},{1,2},{2,1},{3,4},{4,3},{5,6},{6,5},{7,8},{8,7},{9,10},{10... | collective-permute-start | bytes 786440 | tf_op jit(solution)/shard_map/ppermute | solution.py:521
  10.1 8.0 %collective-permute-start.4 = (f32[256,256]{1,0:T(8,128)S(1)}, f32[256,256]{1,0:T(8,128)S(1)}, u32[]{:S(2)}, u32[]{:S(2)}) collective-permute-start(f32[256,256]{1,0:T(8,128)S(1)} %get-tuple-element.94), channel_id=1, source_target_pairs={{0,1},{1,0},{2,3},{3,2},{4,5},{5,4},{6,7},{7,6},{8,9},{9,8},{10,11... | collective-permute-start | bytes 786440 | tf_op jit(solution)/shard_map/ppermute | solution.py:521
  18.1 0.0 collective-permute-done.1.cross
  18.1 2.2 %middle.1 = (f32[256,256]{1,0:T(8,128)S(1)}, f32[256,256]{1,0:T(8,128)S(1)}, f32[256,256]{1,0:T(8,128)S(1)}, f32[256,256]{1,0:T(8,128)S(1)}, bf16[2,64,256]{2,1,...) custom-call(s32[1]{0:T(128)} %bitcast.parity_ref, ...), custom_call_target="tpu_custom_call" | custom-call | flops 2760000000 | bytes 1000000 | tf_op jit(solution)/shard_map/middle/pallas_call | solution.py:108
  20.3 0.1 collective-permute-start.2
  20.4 0.1 collective-permute-start.3
  20.5 0.0 copy-start
  20.5 0.4 rest.1.base_ref
  20.9 0.6 collective-permute-done.2.in_chip
  21.6 2.2 %collective-permute-done.3.cross = f32[32,256]{1,0:T(8,128)S(1)} collective-permute-done((f32[32,256]{1,0:T(8,128)S(1)}, f32[32,256]{1,0:T(8,128)S(1)}, u32[]{:S(2)}, u32[]{:S(2)}) %collective-permute-start.3) | collective-permute-done | bytes 32800 | tf_op jit(solution)/shard_map/ppermute | solution.py:521
  23.8 0.0 copy-done
  23.8 2.8 %turn.1 = (f32[256,256]{1,0:T(8,128)}, f32[8,128]{1,0:T(8,128)S(1)}, f32[256,256]{1,0:T(8,128)S(1)}, f32[256,256]{1,0:T(8,128)S(1)}, f32[256,256]{1,0:T(8,128)S(...) custom-call(s32[1]{0:T(128)} %bitcast.parity_ref, ...), custom_call_target="tpu_custom_call" | custom-call | flops 3449999872 | bytes 1000000 | tf_op jit(solution)/shard_map/turn/pallas_call | solution.py:108
  26.6 5.8 %collective-permute-start.6 = (f32[32,256]{1,0:T(8,128)S(1)}, f32[32,256]{1,0:T(8,128)S(1)}, u32[]{:S(2)}, u32[]{:S(2)}) collective-permute-start(f32[32,256]{1,0:T(8,128)S(1)} %get-tuple-element.96), channel_id=1, source_target_pairs={{0,1},{1,0},{2,3},{3,2},{4,5},{5,4},{6,7},{7,6},{8,9},{9,8},{10,11... | collective-permute-start | bytes 98312 | tf_op jit(solution)/shard_map/ppermute | solution.py:521
  32.4 0.0 collective-permute-start.7
  32.4 0.0 collective-permute-done.5.cross.cross_state
  32.4 0.0 collective-permute-done.4.in_chip.in_chip_state
  32.4 1.0 %beside.1 = (f32[256,256]{1,0:T(8,128)S(1)}, f32[256,256]{1,0:T(8,128)S(1)}, f32[256,256]{1,0:T(8,128)S(1)}, f32[8,128]{1,0:T(8,128)S(1)}, f32[256,256]{1,0:T(8,128)S(1)}, /*index=5*/f32[256,256]{1,0:T(8,128)S(1)}) custom-call(f32[256,256]{1,0:T(8,128)S(1)} %get-tuple-element.89.adjoint_ref, f32[256,256]{1,0:T(8,128)S(1)} %get-tuple-element.90.delta_ref, ...), custom_call_target="tpu_custom_call" | custom-call | flops 1495000064 | bytes 1000000 | tf_op jit(solution)/shard_map/beside/pallas_call | solution.py:108
  33.5 0.0 collective-permute-done.6.in_chip
  33.5 2.3 %collective-permute-done.7.cross = f32[32,256]{1,0:T(8,128)S(1)} collective-permute-done((f32[32,256]{1,0:T(8,128)S(1)}, f32[32,256]{1,0:T(8,128)S(1)}, u32[]{:S(2)}, u32[]{:S(2)}) %collective-permute-start.7) | collective-permute-done | bytes 32800 | tf_op jit(solution)/shard_map/ppermute | solution.py:521
  35.8 4.4 %back.1 = (f32[16,40,128]{2,1,0:T(8,128)S(1)}, f32[16,40,128]{2,1,0:T(8,128)S(1)}, f32[256,256]{1,0:T(8,128)}, f32[256,256]{1,0:T(8,128)}, f32[256,256]{1,0:T(8,128)}) custom-call(s32[1]{0:T(128)} %bitcast.parity_ref, f32[256,256]{1,0:T(8,128)S(1)} %get-tuple-element.95.base_ref, f32[256,256]{1,0:T(8,128)S(1)} %get-tuple-element.89.adjoint_ref, ...), custom_call_target="tpu_custom_call" | custom-call | flops 5175000064 | bytes 1000000 | tf_op jit(solution)/shard_map/back/pallas_call | solution.py:108
  40.2 5.4 %collective-permute-start.8 = (f32[16,40,128]{2,1,0:T(8,128)S(1)}, f32[16,40,128]{2,1,0:T(8,128)S(1)}, u32[]{:S(2)}, u32[]{:S(2)}) collective-permute-start(f32[16,40,128]{2,1,0:T(8,128)S(1)} %get-tuple-element.108), channel_id=1, source_target_pairs={{0,1},{1,0},{2,3},{3,2},{4,5},{5,4},{6,7},{7,6},{8,9},{9,8},{10,11... | collective-permute-start | bytes 983048 | tf_op jit(solution)/shard_map/ppermute | solution.py:584
  45.6 1.3 %collective-permute-done.8.got_ref = f32[16,40,128]{2,1,0:T(8,128)S(1)} collective-permute-done((f32[16,40,128]{2,1,0:T(8,128)S(1)}, f32[16,40,128]{2,1,0:T(8,128)S(1)}, u32[]{:S(2)}, u32[]{:S(2)}) %collective-permute-start.8) | collective-permute-done | bytes 327712 | tf_op jit(solution)/shard_map/ppermute | solution.py:584
  46.9 11.2 %all_to_all.15.parts_ref = f32[16,40,128]{2,1,0:T(8,128)S(1)} all-to-all(f32[16,40,128]{2,1,0:T(8,128)S(1)} %chip_sum.1), channel_id=1, replica_groups=mesh['x'=4,'y'=4,'z'=8,'core'=2] {'x','y'}, dimensions={0} | all-to-all | bytes 655360 | tf_op jit(solution)/shard_map/all_to_all | solution.py:585
  58.2 14.6 %all_to_all.16.parts_ref = f32[8,40,128]{2,1,0:T(8,128)S(1)} all-to-all(f32[8,40,128]{2,1,0:T(8,128)S(1)} %plane_sum.1), channel_id=1, replica_groups=mesh['x'=4,'y'=4,'z'=8,'core'=2] {'z'}, dimensions={0} | all-to-all | bytes 327680 | tf_op jit(solution)/shard_map/all_to_all | solution.py:587
  72.8 11.2 %all_to_all.17.own_ref = f32[16,32,128]{2,1,0:T(8,128)S(1)} all-to-all(f32[16,32,128]{2,1,0:T(8,128)S(1)} %get-tuple-element.109), channel_id=1, replica_groups=mesh['x'=4,'y'=4,'z'=8,'core'=2] {'x','y'}, dimensions={0} | all-to-all | bytes 524288 | tf_op jit(solution)/shard_map/all_to_all | solution.py:589
  84.0 4.0 %collective-permute-start.9 = (f32[16,32,128]{2,1,0:T(8,128)S(1)}, f32[16,32,128]{2,1,0:T(8,128)S(1)}, u32[]{:S(2)}, u32[]{:S(2)}) collective-permute-start(f32[16,32,128]{2,1,0:T(8,128)S(1)} %all_to_all.17.own_ref), channel_id=1, source_target_pairs={{0,1},{1,0},{2,3},{3,2},{4,5},{5,4},{6,7},{7,6},{8,9},{9,8},{10,11... | collective-permute-start | bytes 786440 | tf_op jit(solution)/shard_map/ppermute | solution.py:590
  88.0 1.2 %collective-permute-done.9.other_ref = f32[16,32,128]{2,1,0:T(8,128)S(1)} collective-permute-done((f32[16,32,128]{2,1,0:T(8,128)S(1)}, f32[16,32,128]{2,1,0:T(8,128)S(1)}, u32[]{:S(2)}, u32[]{:S(2)}) %collective-permute-start.9) | collective-permute-done | bytes 262176 | tf_op jit(solution)/shard_map/ppermute | solution.py:590
  89.2 1.0 %scale.1 = (f32[256,256]{1,0:T(8,128)}, f32[1,256]{1,0:T(1,128)}, f32[256,256]{1,0:T(8,128)}, f32[1,256]{1,0:T(1,128)}, f32[1,1]{1,0:T(1,128)}) custom-call(s32[1]{0:T(128)} %bitcast.parity_ref, f32[16,32,128]{2,1,0:T(8,128)S(1)} %all_to_all.17.own_ref, f32[16,32,128]{2,1,0:T(8,128)S(1)} %collective-permute-done.9.other_ref, ...), custom_call_target="tpu_custom_call" | custom-call | flops 1150000000 | bytes 1000000 | tf_op jit(solution)/shard_map/scale/pallas_call | solution.py:108
  (3 shorter events, 0.1 us)
Async XLA Ops:
  0.6 0.7 copy-start.1
  0.6 0.7 copy-start.2
  0.7 0.7 copy-start.3
  1.3 0.7 copy-start.4
  4.2 4.2 %collective-permute-start = (f32[40,256]{1,0:T(8,128)S(1)}, f32[40,256]{1,0:T(8,128)S(1)}, u32[]{:S(2)}, u32[]{:S(2)}) collective-permute-start(f32[40,256]{1,0:T(8,128)S(1)} %get-tuple-element.70), channel_id=1, source_target_pairs={{0,1},{1,0},{2,3},{3,2},{4,5},{5,4},{6,7},{7,6},{8,9},{9,8},{10,11... | collective-permute-start | bytes 122888 | tf_op jit(solution)/shard_map/ppermute | solution.py:521
  7.5 10.6 %collective-permute-start.1 = (f32[40,256]{1,0:T(8,128)S(1)}, f32[40,256]{1,0:T(8,128)S(1)}, u32[]{:S(2)}, u32[]{:S(2)}) collective-permute-start(f32[40,256]{1,0:T(8,128)S(1)} %get-tuple-element.72), channel_id=1, source_target_pairs={{0,255},{1,2},{2,1},{3,4},{4,3},{5,6},{6,5},{7,8},{8,7},{9,10},{10... | collective-permute-start | bytes 122888 | tf_op jit(solution)/shard_map/ppermute | solution.py:521
  9.1 23.3 %collective-permute-start.5 = (f32[256,256]{1,0:T(8,128)S(1)}, f32[256,256]{1,0:T(8,128)S(1)}, u32[]{:S(2)}, u32[]{:S(2)}) collective-permute-start(f32[256,256]{1,0:T(8,128)S(1)} %get-tuple-element.94), channel_id=1, source_target_pairs={{0,255},{1,2},{2,1},{3,4},{4,3},{5,6},{6,5},{7,8},{8,7},{9,10},{10... | collective-permute-start | bytes 786440 | tf_op jit(solution)/shard_map/ppermute | solution.py:521
  10.1 22.3 %collective-permute-start.4 = (f32[256,256]{1,0:T(8,128)S(1)}, f32[256,256]{1,0:T(8,128)S(1)}, u32[]{:S(2)}, u32[]{:S(2)}) collective-permute-start(f32[256,256]{1,0:T(8,128)S(1)} %get-tuple-element.94), channel_id=1, source_target_pairs={{0,1},{1,0},{2,3},{3,2},{4,5},{5,4},{6,7},{7,6},{8,9},{9,8},{10,11... | collective-permute-start | bytes 786440 | tf_op jit(solution)/shard_map/ppermute | solution.py:521
  20.3 1.3 %collective-permute-start.2 = (f32[32,256]{1,0:T(8,128)S(1)}, f32[32,256]{1,0:T(8,128)S(1)}, u32[]{:S(2)}, u32[]{:S(2)}) collective-permute-start(f32[32,256]{1,0:T(8,128)S(1)} %get-tuple-element.80), channel_id=1, source_target_pairs={{0,1},{1,0},{2,3},{3,2},{4,5},{5,4},{6,7},{7,6},{8,9},{9,8},{10,11... | collective-permute-start | bytes 98312 | tf_op jit(solution)/shard_map/ppermute | solution.py:521
  20.4 3.4 %collective-permute-start.3 = (f32[32,256]{1,0:T(8,128)S(1)}, f32[32,256]{1,0:T(8,128)S(1)}, u32[]{:S(2)}, u32[]{:S(2)}) collective-permute-start(f32[32,256]{1,0:T(8,128)S(1)} %get-tuple-element.81), channel_id=1, source_target_pairs={{0,255},{1,2},{2,1},{3,4},{4,3},{5,6},{6,5},{7,8},{8,7},{9,10},{10... | collective-permute-start | bytes 98312 | tf_op jit(solution)/shard_map/ppermute | solution.py:521
  20.5 3.3 %copy-start = (f32[256,256]{1,0:T(8,128)S(1)}, f32[256,256]{1,0:T(8,128)}, u32[]{:S(2)}) copy-start(f32[256,256]{1,0:T(8,128)} %target_ref.1) | copy-start | bytes 786436
  26.6 6.9 %collective-permute-start.6 = (f32[32,256]{1,0:T(8,128)S(1)}, f32[32,256]{1,0:T(8,128)S(1)}, u32[]{:S(2)}, u32[]{:S(2)}) collective-permute-start(f32[32,256]{1,0:T(8,128)S(1)} %get-tuple-element.96), channel_id=1, source_target_pairs={{0,1},{1,0},{2,3},{3,2},{4,5},{5,4},{6,7},{7,6},{8,9},{9,8},{10,11... | collective-permute-start | bytes 98312 | tf_op jit(solution)/shard_map/ppermute | solution.py:521
  32.4 3.3 %collective-permute-start.7 = (f32[32,256]{1,0:T(8,128)S(1)}, f32[32,256]{1,0:T(8,128)S(1)}, u32[]{:S(2)}, u32[]{:S(2)}) collective-permute-start(f32[32,256]{1,0:T(8,128)S(1)} %get-tuple-element.97), channel_id=1, source_target_pairs={{0,255},{1,2},{2,1},{3,4},{4,3},{5,6},{6,5},{7,8},{8,7},{9,10},{10... | collective-permute-start | bytes 98312 | tf_op jit(solution)/shard_map/ppermute | solution.py:521
  40.2 6.7 %collective-permute-start.8 = (f32[16,40,128]{2,1,0:T(8,128)S(1)}, f32[16,40,128]{2,1,0:T(8,128)S(1)}, u32[]{:S(2)}, u32[]{:S(2)}) collective-permute-start(f32[16,40,128]{2,1,0:T(8,128)S(1)} %get-tuple-element.108), channel_id=1, source_target_pairs={{0,1},{1,0},{2,3},{3,2},{4,5},{5,4},{6,7},{7,6},{8,9},{9,8},{10,11... | collective-permute-start | bytes 983048 | tf_op jit(solution)/shard_map/ppermute | solution.py:584
  84.0 5.2 %collective-permute-start.9 = (f32[16,32,128]{2,1,0:T(8,128)S(1)}, f32[16,32,128]{2,1,0:T(8,128)S(1)}, u32[]{:S(2)}, u32[]{:S(2)}) collective-permute-start(f32[16,32,128]{2,1,0:T(8,128)S(1)} %all_to_all.17.own_ref), channel_id=1, source_target_pairs={{0,1},{1,0},{2,3},{3,2},{4,5},{5,4},{6,7},{7,6},{8,9},{9,8},{10,11... | collective-permute-start | bytes 786440 | tf_op jit(solution)/shard_map/ppermute | solution.py:590

commit v4 on v3

--- a/solution.py
+++ b/solution.py
@@ -162,25 +162,26 @@
     return (rows == column).astype(F32).astype(BF16)
 
 
-def make_near(nbr_ref, near):
-    rows = lax.broadcasted_iota(jnp.int32, (256, 256), 0)
+def make_near(small_ref, near):
+    rows = lax.broadcasted_iota(jnp.int32, (256, 256), 0).astype(F32)
     for face in range(2, 6):
-        near[face - 2] = one_hot(rows + 256 * (face ^ 1), nbr_ref[face : face + 1])
+        near[face - 2] = one_hot(rows, small_ref[face : face + 1] - 256.0 * (face ^ 1))
 
 
 def first_kernel(
-    parity_ref, state_far, w_in_far, nbr_far, fixed_far, b_in_far, w_out_far, b_out_far, send_far,
-    arrived_ref, hidden_ref, in_chip_ref, cross_ref, w_in, w_out, state_ref, nbr_ref, inner, leave, lift, lift_t,
-    w_in_ref, b_in_ref, w_out_ref, b_out_ref, send_ref, near, sems,
+    parity_ref, state_far, w_in_far, fixed_far, w_out_far, small_ref,
+    arrived_ref, hidden_ref, in_chip_ref, cross_ref, w_in, state_ref,
+    w_in_ref, w_out_ref, fixed, near, sems,
 ):
     pairs = (
-        (state_far, state_ref), (w_in_far, w_in_ref), (b_in_far, b_in_ref), (fixed_far.at[512:576], leave),
-        (nbr_far, nbr_ref), (fixed_far.at[0:512], inner), (fixed_far.at[576:640], lift_t), (w_out_far, w_out_ref),
-        (b_out_far, b_out_ref), (send_far, send_ref),
+        (state_far, state_ref), (w_in_far, w_in_ref), (fixed_far.at[0:256], fixed), (w_out_far.at[0:16], w_out_ref.at[0:16]),
+        (w_out_far.at[48:80], w_out_ref.at[16:48]), (w_out_far.at[112:128], w_out_ref.at[48:64]),
     )
     copies = [pltpu.make_async_copy(s, t, sems.at[n]) for n, (s, t) in enumerate(pairs)]
     for copy in copies:
         copy.start()
+    make_near(small_ref, near)
+    bias = wide(small_ref.at[8:9])
     copies[0].wait()
     values = state_ref[...]
     edge = edge_rows(values)
@@ -189,20 +190,17 @@
     put(parity, *leaving(edge), in_chip_ref, cross_ref)
     copies[1].wait()
     w_in[0], w_in[1] = split(w_in_ref[...])
-    for copy in copies[2:5]:
+    hidden = jnp.tanh(mm3(pair(w_in), parts) + bias)
+    hidden_ref[...] = hidden
+    for copy in copies[2:]:
         copy.wait()
-    make_near(nbr_ref, near)
-    arrive_near(parts, leave, near, arrived_ref)
-    hidden = jnp.tanh(mm3(pair(w_in), parts) + wide(b_in_ref))
-    hidden_ref[...] = hidden
-    for copy in copies[5:]:
-        copy.wait()
-    lift[...] = flip(lift_t[...])
-    w_out[0], w_out[1] = split(w_out_ref[...])
-    rates = edge_rates(parts, split(hidden), (w_in, b_in_ref, w_out, b_out_ref, inner, leave, lift, near), arrived_ref)
+    arrive_near(mm(fixed[128:192], parts[0]) + mm(fixed[128:192], parts[1]), near, arrived_ref)
+    rates = mm3((fixed[0:64], fixed[64:128]), parts) + mm3(split(w_out_ref[...]), split(hidden))
+    lift = fixed[192:256, 0:64]
+    rates += mm(lift, arrived_ref[0]) + mm(lift, arrived_ref[1])
     put(parity, *leaving(edge + TIME_STEP * rates), in_chip_ref, cross_ref, 16)
-    down_index = send_ref[0:1].astype(F32)
-    up_index = (send_ref[1:2] - 256).astype(F32)
+    down_index = small_ref[6:7]
+    up_index = small_ref[7:8] - 256.0
     even = parity == 0
     in_chip_ref[32:40] = jnp.broadcast_to(jnp.where(even, up_index, down_index), (8, 256))
     cross_ref[32:40] = jnp.broadcast_to(jnp.where(even, down_index, up_index), (8, 256))
@@ -212,29 +210,56 @@
     return values.astype(F32).T.astype(BF16)
 
 
+def forward_pairs(turned):
+    return jnp.concatenate([turned[0:16] + turned[64:80], turned[48:64] - turned[112:128]], axis=0)
+
+
+def backward_pairs(turned):
+    return jnp.concatenate([turned[0:16] - turned[64:80], turned[48:64] + turned[112:128]], axis=0)
+
+
+def deep(rows):
+    high, low = split(rows.T)
+    return jnp.concatenate([high, high, low], axis=1)
+
+
 def tables_kernel(
-    w_in, b_in, w_out, b_out, inner, leave, lift, nbr_ref, state_ref, arrived_ref, hidden_ref, after_ref,
-    next_ref, in_t_ref, out_t_ref, inner_t, leave_t, near, far_ref, eff_ref, copy_ref, column_in, column_out,
+    w_in, w_out_ref, inner, leave, lift_t, small_ref, state_ref, arrived_ref, hidden_ref, after_ref,
+    next_ref, sum_ref, linear_ref, out_ref, w_out, in_t_ref, out_t_ref, inner_t, leave_t, lift,
+    near, far_ref, column_in, column_out, in_deep, inner_deep, leave_deep, out_deep, inner_t_deep, lift_t_deep, eff_ref,
 ):
+    b_in, b_out = small_ref.at[8:9], small_ref.at[9:10]
     column_in[...] = column(b_in)
     column_out[...] = column(b_out)
+    second = w_out_ref[...]
+    w_out[0], w_out[1] = split(second)
+    lift[...] = flip(lift_t[...])
+    leave_t[...] = flip(leave[...])
     values = state_ref[...]
-    copy_ref[...] = values
-    network = (w_in, b_in, w_out, b_out, inner, leave, lift, near)
-    next_ref[...] = values + TIME_STEP * full_rates(split(values), split(hidden_ref[...]), network, arrived_ref)
-    make_near(nbr_ref, near)
-    rows = lax.broadcasted_iota(jnp.int32, (256, 256), 0)
+    network = (w_in, column_in, w_out, column_out, inner, leave, lift, near)
+    rates = full_rates(split(values), split(hidden_ref[...]), network, arrived_ref)
+    base = values + TIME_STEP * rates
+    next_ref[...] = base
+    sum_ref[...], linear_ref[...], out_ref[...] = prepare(split(base), network)
+    make_near(small_ref, near)
+    rows = lax.broadcasted_iota(jnp.int32, (256, 256), 0).astype(F32)
     for face in range(2):
-        far_ref[face] = one_hot(rows + (1536 + 256 * face), nbr_ref[face : face + 1])
+        far_ref[face] = one_hot(rows, small_ref[face : face + 1] - (1536.0 + 256.0 * face))
     for part in range(2):
         in_t_ref[part] = flip(w_in[part])
         out_t_ref[part] = flip(w_out[part])
         inner_t[256 * part : 256 * part + 256] = flip(inner[256 * part : 256 * part + 256])
-    leave_t[...] = flip(leave[...])
-    whole = w_out[0].astype(F32) + w_out[1].astype(F32)
-    for side, seen in enumerate((whole[48:64] + whole[112:128], whole[0:16] - whole[64:80])):
-        high, low = split(seen.T)
-        eff_ref[side] = jnp.concatenate([high, high, low], axis=1)
+    whole = lambda values: values[0].astype(F32) + values[1].astype(F32)
+    in_deep[...] = deep(TIME_STEP * forward_pairs(whole(pair(in_t_ref))))
+    inner_deep[...] = deep(TIME_STEP * forward_pairs(whole(pair(inner_t))))
+    leave_deep[...] = deep(TIME_STEP * forward_pairs(leave_t[...].astype(F32)))
+    weight = 3.0 * TIME_STEP
+    out_deep[...] = deep(weight * backward_pairs(second))
+    inner_t_deep[...] = deep(weight * backward_pairs(whole(pair(inner))))
+    lift_t_deep[...] = deep(weight * backward_pairs(lift[...].astype(F32)))
+    seen = backward_pairs(second)
+    eff_ref[0] = deep(seen[16:32])
+    eff_ref[1] = deep(seen[0:16])
 
 
 def column(row):
@@ -252,12 +277,25 @@
         yield dot(both, near[n])
 
 
-def arrive_near(parts, leave, near, arrived_ref):
-    high, low = split(mm(leave[...], parts[0]) + mm(leave[...], parts[1]))
+def arrive_near(out, near, arrived_ref):
+    high, low = split(out)
     for n, both in enumerate(gather(high, low, near, mm)):
         both = both.astype(BF16)
         arrived_ref[0, 16 * n : 16 * n + 16] = both[0:16]
         arrived_ref[1, 16 * n : 16 * n + 16] = both[16:32]
+
+
+def prepare(parts, network):
+    w_in, b_in, w_out, b_out, inner, leave, lift, near = network
+    out = mm(leave[...], parts[0]) + mm(leave[...], parts[1])
+    return mm3(pair(w_in), parts) + wide(b_in), mm3(pair(inner), parts) + wide(b_out), out
+
+
+def full_rates(parts, hidden_parts, network, arrived_ref):
+    w_in, b_in, w_out, b_out, inner, leave, lift, near = network
+    rates = mm3(pair(inner), parts) + wide(b_out)
+    rates += mm(lift[...], arrived_ref[0]) + mm(lift[...], arrived_ref[1])
+    return rates + mm3(pair(w_out), hidden_parts)
 
 
 def edge_rates(parts, hidden_parts, network, arrived_ref):
@@ -267,31 +305,38 @@
     return rates + mm3([edge_rows(x) for x in pair(w_out)], hidden_parts)
 
 
-def full_rates(parts, hidden_parts, network, arrived_ref):
-    w_in, b_in, w_out, b_out, inner, leave, lift, near = network
-    rates = mm3(pair(inner), parts) + wide(b_out)
-    rates += mm(lift[...], arrived_ref[0]) + mm(lift[...], arrived_ref[1])
-    return rates + mm3(pair(w_out), hidden_parts)
-
-
-def activate(parts, network, hidden_ref, arrived_ref):
-    w_in, b_in, w_out, b_out, inner, leave, lift, near = network
-    hidden = jnp.tanh(mm3(pair(w_in), parts) + wide(b_in))
-    hidden_ref[...] = hidden
-    arrive_near(parts, leave, near, arrived_ref)
-    return split(hidden)
-
-
-def add_arrived(weight, base_ref, below, above, link, now_ref):
-    low = weight * pick(below, link[0])
-    high = weight * pick(above, link[1])
+def pick_parts(below, above, link):
+    low = mm(jnp.concatenate(split(below), axis=0), link[0])
+    high = mm(jnp.concatenate(split(above), axis=0), link[1])
+    return low, high
+
+
+def stack(low, high):
+    top = jnp.concatenate([low[0:16], high[0:16]], axis=0).astype(BF16)
+    rest = jnp.concatenate([low[16:32], high[16:32]], axis=0).astype(BF16)
+    return jnp.concatenate([top, rest, top], axis=0)
+
+
+def add_arrived(weight, base_ref, low, high, now_ref):
+    low = weight * (low[0:16] + low[16:32])
+    high = weight * (high[0:16] + high[16:32])
     now_ref[...] = base_ref[...]
     add_edges(now_ref, low, high, low, -high)
     return now_ref[...]
 
 
+def prepared_rates(stacked, prepared, deeps, network, hidden_ref, arrived_ref):
+    total, linear, out = (ref[...] + mm(d[...], stacked) for ref, d in zip(prepared, deeps))
+    hidden = jnp.tanh(total)
+    hidden_ref[...] = hidden
+    lift, near, w_out = network[6], network[7], network[2]
+    arrive_near(out, near, arrived_ref)
+    linear += mm(lift[...], arrived_ref[0]) + mm(lift[...], arrived_ref[1])
+    return linear + mm3(pair(w_out), split(hidden))
+
+
 def middle_kernel(
-    parity_ref, base_ref, state_ref, in_chip, cross, far_ref,
+    parity_ref, base_ref, state_ref, in_chip, cross, far_ref, sum_ref, linear_ref, out_ref, in_deep, inner_deep, leave_deep,
     w_in, b_in, w_out, b_out, inner, leave, lift, near,
     second_ref, third_ref, hidden_second, hidden_third, arrived_ref, link, in_chip_out, cross_out, between,
 ):
@@ -301,25 +346,35 @@
     rows = lax.broadcasted_iota(jnp.int32, (256, 256), 0).astype(F32)
     for side, received in enumerate((below, above)):
         link[side] = mm(one_hot(rows, received[32:33]), far_ref[side]).astype(BF16)
-    values = add_arrived(TIME_STEP, base_ref, below[0:16], above[0:16], link, second_ref)
-    parts = split(values)
-    hidden_parts = activate(parts, network, hidden_second, arrived_ref)
-    rates = full_rates(parts, hidden_parts, network, arrived_ref)
+    low, high = pick_parts(below[0:16], above[0:16], link)
+    rates = prepared_rates(
+        stack(low, high), (sum_ref, linear_ref, out_ref), (in_deep, inner_deep, leave_deep),
+        network, hidden_second, arrived_ref,
+    )
+    values = add_arrived(TIME_STEP, base_ref, low, high, second_ref)
     between[...] = 0.5 * (state_ref[...] + values) + HALF_STEP * rates
     put(parity, *leaving(edge_rows(between)), in_chip_out, cross_out)
-    values = add_arrived(HALF_STEP, between, below[16:32], above[16:32], link, third_ref)
+    up_bias, down_bias = leaving(TIME_STEP * edge_rows(wide(b_out)))
+    low, high = pick_parts(below[16:32] + up_bias, above[16:32] + down_bias, link)
+    values = add_arrived(HALF_STEP, between, low, high, third_ref)
     parts = split(values)
-    hidden_parts = activate(parts, network, hidden_third, arrived_ref)
-    rates = edge_rates(parts, hidden_parts, network, arrived_ref)
+    hidden = jnp.tanh(mm3(pair(w_in), parts) + wide(b_in))
+    hidden_third[...] = hidden
+    arrive_near(mm(leave[...], parts[0]) + mm(leave[...], parts[1]), near, arrived_ref)
+    rates = edge_rates(parts, split(hidden), network, arrived_ref)
     put(parity, *leaving(edge_rows(values) + TIME_STEP * rates), in_chip_out, cross_out, 16)
 
 
 def rest_kernel(
-    third_ref, hidden_ref, arrived_ref, w_in, b_in, w_out, b_out, inner, leave, lift, near, next_ref
+    third_ref, hidden_ref, arrived_ref, state_ref, w_in, b_in, w_out, b_out, inner, leave, lift, near,
+    next_ref, sum_ref, linear_ref, out_ref, copy_ref,
 ):
+    copy_ref[...] = state_ref[...]
     network = (w_in, b_in, w_out, b_out, inner, leave, lift, near)
     values = third_ref[...]
-    next_ref[...] = values + TIME_STEP * full_rates(split(values), split(hidden_ref[...]), network, arrived_ref)
+    base = values + TIME_STEP * full_rates(split(values), split(hidden_ref[...]), network, arrived_ref)
+    next_ref[...] = base
+    sum_ref[...], linear_ref[...], out_ref[...] = prepare(split(base), network)
 
 
 def sensitivities(edge, link):
@@ -344,6 +399,7 @@
 
 def turn_kernel(
     parity_ref, base_ref, third_ref, in_chip, cross, link, target_ref,
+    sum_ref, linear_ref, out_ref, in_deep, inner_deep, leave_deep,
     w_in, b_in, w_out, b_out, inner, leave, lift, near, w_in_t, w_out_t, inner_t, leave_t, lift_t,
     final_ref, loss_ref, fourth_ref, hidden_ref, adjoint_ref, delta_ref, gathered_ref, in_chip_out, cross_out,
     between, arrived_ref,
@@ -351,12 +407,15 @@
     network = (w_in, b_in, w_out, b_out, inner, leave, lift, near)
     parity = parity_ref[0]
     below, above = take(parity, in_chip[...], cross[...])
-    values = add_arrived(TIME_STEP, base_ref, below[0:16], above[0:16], link, fourth_ref)
-    parts = split(values)
-    hidden_parts = activate(parts, network, hidden_ref, arrived_ref)
-    rates = full_rates(parts, hidden_parts, network, arrived_ref)
+    low, high = pick_parts(below[0:16], above[0:16], link)
+    rates = prepared_rates(
+        stack(low, high), (sum_ref, linear_ref, out_ref), (in_deep, inner_deep, leave_deep),
+        network, hidden_ref, arrived_ref,
+    )
+    values = add_arrived(TIME_STEP, base_ref, low, high, fourth_ref)
     between[...] = 0.5 * (third_ref[...] + values) + HALF_STEP * rates
-    final = add_arrived(HALF_STEP, between, below[16:32], above[16:32], link, final_ref)
+    low, high = pick_parts(below[16:32], above[16:32], link)
+    final = add_arrived(HALF_STEP, between, low, high, final_ref)
     mismatch = final - target_ref[...]
     adjoint = (HALF_STEP / COUNT) * mismatch
     adjoint_ref[...] = adjoint
@@ -395,16 +454,22 @@
 
 def beside_kernel(
     adjoint_ref, delta_ref, gathered_ref, state_ref, hidden_ref, in_chip, cross, w_in, b_in,
-    w_in_t, inner_t, leave_t, lift_t, near,
-    next_ref, grad_in, grad_out, extra, in_chip_hidden, cross_hidden,
+    w_in_t, inner_t, leave_t, lift_t, near, w_out_t, hidden_third,
+    next_ref, grad_in, grad_out, extra, in_chip_hidden, cross_hidden, back_ref, linear_ref, out_ref,
 ):
     adjoint = adjoint_ref[...]
     parts, delta_parts = split(adjoint), split(delta_ref[...])
     gathered = gathered_ref[0], gathered_ref[1]
-    next_ref[...] = adjoint + TIME_STEP * back_rates(
-        parts, delta_parts, (w_in_t, inner_t, leave_t, lift_t, near), gathered
-    )
-    grad_in[...], grad_out[...], extra[...] = gradients(parts, delta_parts, state_ref[...], hidden_ref[...])
+    base = adjoint + TIME_STEP * back_rates(parts, delta_parts, (w_in_t, inner_t, leave_t, lift_t, near), gathered)
+    next_ref[...] = base
+    base_parts = split(base)
+    back_ref[...] = mm3(pair(w_out_t), base_parts)
+    linear_ref[...] = mm3(pair(inner_t), base_parts)
+    out_ref[...] = mm(lift_t[...], base_parts[0]) + mm(lift_t[...], base_parts[1])
+    first, second, bias = gradients(parts, delta_parts, state_ref[...], hidden_ref[...])
+    grad_in[...] = first
+    grad_out[...] = second + mm3(base_parts, split(hidden_third[...]), mm_nt)
+    extra[...] = bias
     for source, ref in ((in_chip, in_chip_hidden), (cross, cross_hidden)):
         ref[...] = jnp.tanh(mm3(pair(w_in), split(source[...])) + wide(b_in))
 
@@ -413,7 +478,8 @@
     parity_ref, base_ref, adjoint_ref, in_chip, cross, link,
     third_ref, hidden_third, second_ref, hidden_second, state_ref, hidden_first,
     in_chip_state, cross_state, in_chip_hidden, cross_hidden,
-    near, w_in_t, w_out_t, inner_t, leave_t, lift_t, eff, old_in, old_out, old_extra, loss_ref,
+    near, w_in_t, w_out_t, inner_t, leave_t, lift_t, eff, back_ref, linear_ref, out_ref, out_deep, inner_t_deep, lift_t_deep,
+    old_in, old_out, old_extra, loss_ref,
     keep_ref, send_ref, now_ref, between, sum_ref,
 ):
     network = (w_in_t, inner_t, leave_t, lift_t, near)
@@ -432,12 +498,24 @@
         for n, term in enumerate(gradients(*args)):
             totals[n] = totals[n] + term
 
-    values = arrive(base_ref, 3.0 * TIME_STEP, below[0:16], above[0:16])
-    parts = split(values)
-    delta = split(through_closure(parts, hidden_third[...], pair(w_out_t)))
-    rates = back_rates(parts, delta, network, gather_back(parts, lift_t, near))
+    received = below[0:16], above[0:16]
+    high_parts, low_parts = zip(*(split(x) for x in received))
+    top, rest = jnp.concatenate(high_parts, axis=0), jnp.concatenate(low_parts, axis=0)
+    stacked = jnp.concatenate([top, rest, top], axis=0)
+    hidden = hidden_third[...]
+    delta_full = (1.0 - hidden * hidden) * (back_ref[...] + mm(out_deep[...], stacked))
+    delta = split(delta_full)
+    high, low = split(out_ref[...] + mm(lift_t_deep[...], stacked))
+    gathered = split(jnp.concatenate([a[0:16] + a[16:32] for a in gather(high, low, near, mm_nt)], axis=0))
+    rates = linear_ref[...] + mm(inner_t_deep[...], stacked) + mm3(pair(w_in_t), delta)
+    rates += mm(leave_t[...], gathered[0]) + mm(leave_t[...], gathered[1])
+    values = arrive(base_ref, 3.0 * TIME_STEP, *received)
     between[...] = 0.5 * (adjoint_ref[...] + values) + HALF_STEP * rates
-    collect(parts, delta, third_ref[...], hidden_third[...])
+    totals[0] = totals[0] + mm3(delta, split(third_ref[...]), mm_nt)
+    totals[2] = totals[2] + bias_rows(row_sums(delta), row_sums(split(values)))
+    weight = 3.0 * TIME_STEP
+    hidden_parts = split(hidden)
+    early = [weight * mm3((h, l), hidden_parts, mm_nt) for h, l in zip(high_parts, low_parts)]
     upward, downward = sensitivities(edge_rows(between), link)
 
     values = arrive(between, 3.0 * HALF_STEP, below[16:32], above[16:32])
@@ -448,7 +526,6 @@
 
     states = take(parity, in_chip_state[...], cross_state[...])
     hiddens = take(parity, in_chip_hidden[...], cross_hidden[...])
-    weight = 3.0 * TIME_STEP
     blocks = []
     for side, received in enumerate((weight * downward, weight * upward)):
         high, low = split(received)
@@ -465,7 +542,8 @@
     delta = split(through_closure(parts, hidden_first[...], pair(w_out_t)))
     collect(parts, delta, state_ref[...], hidden_first[...])
     sum_ref[...] = totals[1]
-    add_edges(sum_ref, blocks[1], blocks[0], -blocks[1], blocks[0])
+    low, high = blocks[1] + early[0], blocks[0] + early[1]
+    add_edges(sum_ref, low, high, -low, high)
     first, second, bias = totals[0], sum_ref[...], totals[2]
     rows = lax.broadcasted_iota(jnp.int32, (8, 128), 0)
     bias = jnp.where(rows == 4, loss_ref[...], bias)
@@ -518,67 +596,85 @@
 
 
 def exchange(in_chip, cross):
-    return lax.ppermute(in_chip, AXES, IN_CHIP), lax.ppermute(cross, AXES, CROSS)
+    crossed = lax.ppermute(cross, AXES, CROSS)
+    return lax.ppermute(in_chip, AXES, IN_CHIP), crossed
 
 
 def local(state, target, w_in, b_in, w_out, b_out, nbr, send):
     parity = lax.axis_index("core").reshape(1)
     inner, leave, lift = operators()
-    fixed = np.concatenate([*halves(inner), leave, lift.T], axis=0).astype(ml_dtypes.bfloat16)
-    b_in, b_out = b_in.reshape(1, 256), b_out.reshape(1, 256)
+    edge = np.concatenate([np.arange(0, 16), np.arange(48, 80), np.arange(112, 128)])
+    fixed = np.zeros((768, 256))
+    fixed[0:64], fixed[64:128] = (x[edge].astype(np.float64) for x in halves(inner))
+    fixed[128:192], fixed[192:256, 0:64] = leave, lift[edge]
+    to_bf16 = lambda values: jnp.asarray(values.astype(ml_dtypes.bfloat16))
+    fixed, inner2, leave1, lift_t = (to_bf16(x) for x in (fixed, np.concatenate(halves(inner)), leave, lift.T))
+    rows = ((0, nbr), (6, send), (8, b_in.reshape(1, 256)), (9, b_out.reshape(1, 256)))
+    small = sum(jnp.pad(x.astype(F32), ((at, 16 - at - x.shape[0]), (0, 0))) for at, x in rows)
     tall, flat, thin = ((512, 256), BF16), ((64, 256), BF16), ((256, 64), BF16)
     arrival = ((2, 64, 256), BF16)
-    arrived, hidden_first, *edge, w_in2, w_out2, state, nbr, inner2, leave1, lift1, lift_t = call(
+    arrived, hidden_first, *edge, w_in2, state = call(
         first_kernel,
-        [arrival, SQUARE, ((40, 256), F32), ((40, 256), F32), PAIR, PAIR, SQUARE, ((6, 256), jnp.int32)]
-        + [tall, flat, thin, flat],
-        parity, state, w_in, nbr, jnp.asarray(fixed), b_in, w_out, b_out, send,
+        [arrival, SQUARE, ((40, 256), F32), ((40, 256), F32), PAIR, SQUARE],
+        parity, state, w_in, fixed, w_out, small,
         name="first", micros=1.5,
-        far=range(1, 9),
-        limit=52.25,
+        far=range(1, 5),
+        limit=53,
         scratch=[
-            pltpu.VMEM((256, 256), F32), pltpu.VMEM((1, 256), F32), pltpu.VMEM((256, 256), F32),
-            pltpu.VMEM((1, 256), F32), pltpu.VMEM((2, 256), jnp.int32), pltpu.VMEM((4, 256, 256), BF16),
-            pltpu.SemaphoreType.DMA((10,)),
+            pltpu.VMEM((256, 256), F32), pltpu.VMEM((64, 256), F32), pltpu.VMEM((256, 256), BF16),
+            pltpu.VMEM((4, 256, 256), BF16), pltpu.SemaphoreType.DMA((6,)),
         ],
     )
     got = exchange(*edge)
-    base, w_in_t, w_out_t, inner_t, leave_t, near, far, eff, copy, b_in2, b_out2 = call(
+    middle = [SQUARE, SQUARE, ((64, 256), F32)]
+    depth, shallow = ((256, 96), BF16), ((64, 96), BF16)
+    made = call(
         tables_kernel,
-        [SQUARE, PAIR, PAIR, tall, thin, ((4, 256, 256), BF16), PAIR, ((2, 256, 48), BF16), SQUARE] + [((256, 128), F32)] * 2,
-        w_in2, b_in, w_out2, b_out, inner2, leave1, lift1, nbr, state, arrived, hidden_first, got[0],
-        name="tables", micros=1,
-    )
-    beside = exchange(copy, copy)
+        [SQUARE, *middle, PAIR, PAIR, PAIR, tall, thin, thin, ((4, 256, 256), BF16), PAIR]
+        + [((256, 128), F32)] * 2
+        + [depth, depth, shallow] * 2
+        + [((2, 256, 48), BF16)],
+        w_in2, w_out, inner2, leave1, lift_t, small, state, arrived, hidden_first, edge[0],
+        name="tables", micros=1.5,
+    )
+    base, prepared, deeps, eff = made[0], made[1:4], made[14:20], made[20]
+    w_out2, w_in_t, w_out_t, inner_t, leave_t, lift1, near, far, b_in2, b_out2 = made[4:14]
+    forward_deeps, backward_deeps = deeps[:3], deeps[3:]
     network = (w_in2, b_in2, w_out2, b_out2, inner2, leave1, lift1, near)
     back = (w_in_t, inner_t, leave_t, lift_t)
     edge_shapes = [((32, 256), F32)] * 2
-    second, third, hidden_second, hidden_third, arrived, link, *edge, _ = call(
+    square = pltpu.VMEM((256, 256), F32)
+    second, third, hidden_second, hidden_third, arrived, link, *edge = call(
         middle_kernel,
-        [SQUARE] * 4 + [arrival, PAIR] + edge_shapes + [SQUARE],
-        parity, base, state, *got, far, *network, name="middle", micros=2.4,
+        [SQUARE] * 4 + [arrival, PAIR] + edge_shapes,
+        parity, base, state, *got, far, *prepared, *forward_deeps, *network, name="middle", micros=2.1, scratch=[square],
     )
     got = exchange(*edge)
-    (base,) = call(rest_kernel, [SQUARE], third, hidden_third, arrived, *network, name="rest", micros=0.6)
-    final, loss, fourth, hidden_fourth, adjoint, delta, gathered, *edge, _, _ = call(
+    base, *prepared, copy = call(
+        rest_kernel, [SQUARE, *middle, SQUARE], third, hidden_third, arrived, state, *network, name="rest", micros=0.9
+    )
+    beside = exchange(copy, copy)
+    final, loss, fourth, hidden_fourth, adjoint, delta, gathered, *edge = call(
         turn_kernel,
-        [SQUARE, EXTRA] + [SQUARE] * 4 + [arrival] + edge_shapes + [SQUARE, arrival],
-        parity, base, third, *got, link, target, *network, w_in_t, w_out_t, inner_t, leave_t, lift_t,
-        name="turn", micros=3,
+        [SQUARE, EXTRA] + [SQUARE] * 4 + [arrival] + edge_shapes,
+        parity, base, third, *got, link, target, *prepared, *forward_deeps, *network,
+        w_in_t, w_out_t, inner_t, leave_t, lift_t,
+        name="turn", micros=2.5, scratch=[square, pltpu.VMEM((2, 64, 256), BF16)],
     )
     got = exchange(*edge)
-    base, *grads, in_chip_hidden, cross_hidden = call(
+    base, *grads, in_chip_hidden, cross_hidden, back_product, linear, out = call(
         beside_kernel,
-        [SQUARE, SQUARE, SQUARE, EXTRA, SQUARE, SQUARE],
-        adjoint, delta, gathered, fourth, hidden_fourth, *beside, w_in2, b_in2, *back, near,
-        name="beside", micros=1.3,
-    )
-    keep, give, *_ = call(
+        [SQUARE, SQUARE, SQUARE, EXTRA, SQUARE, SQUARE, *middle],
+        adjoint, delta, gathered, fourth, hidden_fourth, *beside, w_in2, b_in2, *back, near, w_out_t, hidden_third,
+        name="beside", micros=2,
+    )
+    keep, give = call(
         back_kernel,
-        [PACKED] * 2 + [SQUARE] * 3,
+        [PACKED] * 2,
         parity, base, adjoint, *got, link, third, hidden_third, second, hidden_second, state, hidden_first,
-        *beside, in_chip_hidden, cross_hidden, near, w_in_t, w_out_t, inner_t, leave_t, lift_t, eff, *grads, loss,
-        name="back", micros=4.5,
+        *beside, in_chip_hidden, cross_hidden, near, w_in_t, w_out_t, inner_t, leave_t, lift_t, eff,
+        back_product, linear, out, *backward_deeps, *grads, loss,
+        name="back", micros=4, scratch=[square] * 3,
     )
     swap = [(0, 1), (1, 0)]
     (parts,) = call(chip_kernel, [PACKED], keep, lax.ppermute(give, "core", swap), name="chip_sum", micros=0.3)

time: 90.5 us -> 88.6 us (0.979)
  waiting for transfers between devices: 8.45 us -> 3.72 us
  starting transfers between devices: 27.8 us -> 30.8 us
  blocking collectives: 37 us -> 35.9 us
    ppermute x8, waiting for transfers between devices: 6.03 us -> 1.3 us  [the longest x4 1.29 us: exchange(): crossed = lax.ppermute(cross, AXES, CROSS)]
    ppermute x1, starting transfers between devices: 5.43 us -> 7.2 us  [local(): lax.ppermute(give, 'core', swap)]
    ppermute x8, starting transfers between devices: 18.3 us -> 19.6 us  [the longest x4 14.6 us: exchange(): return (lax.ppermute(in_chip, AXES, IN_CHIP), crossed)]
    all_to_all x1, blocking collectives: 14.6 us -> 13.5 us  [local(): parts = lax.all_to_all(parts, 'z', 0, 0, tiled=True)]
    pallas_call x11, Pallas kernels: 14.9 us -> 15.8 us  [call(): pl.pallas_call(body, out_shape=[jax.ShapeDtypeStruct(s, t) for s, t in ou...]
  transfers between devices with their start and end apart: 10 -> 10, of which waited for: 6 -> 3; matrix products, arithmetic and copies ran while one was open for 0% -> 0% of each run, Pallas kernels for 8% -> 8%
where the time goes in v4:
time: 88.6 us; the launch traced here: 88.3 us
  blocking collectives  35.9 us (41%)
  starting transfers between devices  30.8 us (35%)
  Pallas kernels  15.8 us (18%)
  waiting for transfers between devices  3.72 us (4%)
    pallas_call x11, Pallas kernels, call(): pl.pallas_call(body, out_shape=[jax.ShapeDtypeStruct(s, t) for s, t in ou...  15.8 us
    ppermute x4, starting transfers between devices, exchange(): return (lax.ppermute(in_chip, AXES, IN_CHIP), crossed)  14.6 us
    all_to_all x1, blocking collectives, local(): parts = lax.all_to_all(parts, 'z', 0, 0, tiled=True)  13.5 us
    all_to_all x1, blocking collectives, local(): parts = lax.all_to_all(parts, PLANE, 0, 0, tiled=True)  11.2 us
    all_to_all x1, blocking collectives, local(): own = lax.all_to_all(parts, PLANE, 0, 0, tiled=True)  11.2 us
    ppermute x1, starting transfers between devices, local(): lax.ppermute(give, 'core', swap)  7.2 us
    ppermute x4, starting transfers between devices, exchange(): crossed = lax.ppermute(cross, AXES, CROSS)  4.95 us
    ppermute x1, starting transfers between devices, local(): other = lax.ppermute(own, 'core', swap)  4.01 us
  transfers between devices with their start and end apart: 10, of which 3 were waited for; matrix products, arithmetic and copies ran while one was open for 0% of the time, Pallas kernels for 8%

profile of v4, /device:TPU:1, one launch (start us, length us, event | category | flops | bytes accessed | tf_op | source)
XLA Modules:
  0.0 88.3 jit_solution(12672012623226926872)
XLA Ops:
  0.6 0.0 copy-start.5
  0.6 0.7 convert_element_type.15
  1.3 0.0 copy-done.5
  1.3 0.0 copy-start.7
  1.3 0.0 copy-start.6
  1.4 0.7 copy-done.7
  2.0 0.0 copy-done.6
  2.0 0.0 copy-start
  2.1 0.0 copy-start.2
  2.1 0.0 copy-start.3
  2.1 0.0 copy-start.4
  2.1 2.0 %first.1 = (bf16[2,64,256]{2,1,0:T(8,128)(2,1)S(1)}, f32[256,256]{1,0:T(8,128)S(1)}, f32[40,256]{1,0:T(8,128)S(1)}, f32[40,256]{1,0:T(8,128)S(1)}, bf16[2,256,25...) custom-call(s32[1]{0:T(128)} %bitcast.parity_ref, f32[256,256]{1,0:T(8,128)} %state_far.1, f32[256,256]{1,0:T(8,128)} %w_in_far.1, ...), custom_call_target="tpu_custom_call" | custom-call | flops 1724999936 | bytes 1000000 | tf_op jit(solution)/shard_map/first/pallas_call | solution.py:108
  4.1 3.1 %collective-permute-start.1 = (f32[40,256]{1,0:T(8,128)S(1)}, f32[40,256]{1,0:T(8,128)S(1)}, u32[]{:S(2)}, u32[]{:S(2)}) collective-permute-start(f32[40,256]{1,0:T(8,128)S(1)} %get-tuple-element.79), channel_id=1, source_target_pairs={{0,255},{1,2},{2,1},{3,4},{4,3},{5,6},{6,5},{7,8},{8,7},{9,10},{10... | collective-permute-start | bytes 122888 | tf_op jit(solution)/shard_map/ppermute | solution.py:599
  7.3 8.4 %collective-permute-start = (f32[40,256]{1,0:T(8,128)S(1)}, f32[40,256]{1,0:T(8,128)S(1)}, u32[]{:S(2)}, u32[]{:S(2)}) collective-permute-start(f32[40,256]{1,0:T(8,128)S(1)} %get-tuple-element.77.after_ref), channel_id=1, source_target_pairs={{0,1},{1,0},{2,3},{3,2},{4,5},{5,4},{6,7},{7,6},{8,9},{9,8},{10,11... | collective-permute-start | bytes 122888 | tf_op jit(solution)/shard_map/ppermute | solution.py:600
  15.7 0.0 copy-done
  15.7 0.0 copy-done.2
  15.7 0.0 copy-done.3
  15.7 0.0 copy-done.4
  15.7 1.5 %tables.1 = (f32[256,256]{1,0:T(8,128)S(1)}, f32[256,256]{1,0:T(8,128)S(1)}, f32[256,256]{1,0:T(8,128)S(1)}, f32[64,256]{1,0:T(8,128)S(1)}, bf16[2,256,256]{2,1,...) custom-call(bf16[2,256,256]{2,1,0:T(8,128)(2,1)S(1)} %get-tuple-elem, ...), custom_call_target="tpu_custom_call" | custom-call | flops 1724999936 | bytes 1000000 | tf_op jit(solution)/shard_map/tables/pallas_call | solution.py:108
  17.2 0.0 collective-permute-done.1.cross
  17.2 0.0 collective-permute-done.in_chip
  17.2 2.0 %middle.1 = (f32[256,256]{1,0:T(8,128)S(1)}, f32[256,256]{1,0:T(8,128)S(1)}, f32[256,256]{1,0:T(8,128)S(1)}, f32[256,256]{1,0:T(8,128)S(1)}, bf16[2,64,256]{2,1,...) custom-call(s32[1]{0:T(128)} %bitcast.parity_ref, ...), custom_call_target="tpu_custom_call" | custom-call | flops 2415000064 | bytes 1000000 | tf_op jit(solution)/shard_map/middle/pallas_call | solution.py:108
  19.2 0.3 collective-permute-start.2
  19.5 0.0 collective-permute-start.3
  19.5 0.0 copy-start.1
  19.5 1.3 %rest.1 = (f32[256,256]{1,0:T(8,128)S(1)}, f32[256,256]{1,0:T(8,128)S(1)}, f32[256,256]{1,0:T(8,128)S(1)}, f32[64,256]{1,0:T(8,128)S(1)}, f32[256,256]{1,0:T(8,128)S(1)}) custom-call(f32[256,256]{1,0:T(8,128)S(1)} %get-tuple-element.92.third_ref, f32[256,256]{1,0:T(8,128)S(1)} %get-tuple-element.93.hidden_ref.hidden_third, ...), custom_call_target="tpu_custom_call" | custom-call | flops 1035000000 | bytes 1000000 | tf_op jit(solution)/shard_map/rest/pallas_call | solution.py:108
  20.8 1.8 %collective-permute-start.5 = (f32[256,256]{1,0:T(8,128)S(1)}, f32[256,256]{1,0:T(8,128)S(1)}, u32[]{:S(2)}, u32[]{:S(2)}) collective-permute-start(f32[256,256]{1,0:T(8,128)S(1)} %get-tuple-element.112), channel_id=1, source_target_pairs={{0,255},{1,2},{2,1},{3,4},{4,3},{5,6},{6,5},{7,8},{8,7},{9,10},{10... | collective-permute-start | bytes 786440 | tf_op jit(solution)/shard_map/ppermute | solution.py:599
  22.6 5.8 %collective-permute-start.4 = (f32[256,256]{1,0:T(8,128)S(1)}, f32[256,256]{1,0:T(8,128)S(1)}, u32[]{:S(2)}, u32[]{:S(2)}) collective-permute-start(f32[256,256]{1,0:T(8,128)S(1)} %get-tuple-element.112), channel_id=1, source_target_pairs={{0,1},{1,0},{2,3},{3,2},{4,5},{5,4},{6,7},{7,6},{8,9},{9,8},{10,11... | collective-permute-start | bytes 786440 | tf_op jit(solution)/shard_map/ppermute | solution.py:600
  28.4 0.0 collective-permute-done.2.in_chip
  28.4 0.0 collective-permute-done.3.cross
  28.4 0.0 copy-done.1
  28.4 2.4 %turn.1 = (f32[256,256]{1,0:T(8,128)}, f32[8,128]{1,0:T(8,128)S(1)}, f32[256,256]{1,0:T(8,128)S(1)}, f32[256,256]{1,0:T(8,128)S(1)}, f32[256,256]{1,0:T(8,128)S(...) custom-call(s32[1]{0:T(128)} %bitcast.parity_ref, ...), custom_call_target="tpu_custom_call" | custom-call | flops 2875000064 | bytes 1000000 | tf_op jit(solution)/shard_map/turn/pallas_call | solution.py:108
  30.8 0.2 collective-permute-start.6
  31.0 0.0 collective-permute-start.7
  31.0 0.0 collective-permute-done.5.cross.cross_state
  31.0 0.0 collective-permute-done.4.in_chip.in_chip_state
  31.0 2.0 %beside.1 = (f32[256,256]{1,0:T(8,128)S(1)}, f32[256,256]{1,0:T(8,128)S(1)}, f32[256,256]{1,0:T(8,128)S(1)}, f32[8,128]{1,0:T(8,128)S(1)}, f32[256,256]{1,0:T(8,...) custom-call(f32[256,256]{1,0:T(8,128)S(1)} %get-tuple-element.107.ad, ...), custom_call_target="tpu_custom_call" | custom-call | flops 2300000000 | bytes 1000000 | tf_op jit(solution)/shard_map/beside/pallas_call | solution.py:108
  33.0 0.0 collective-permute-done.6.in_chip
  33.0 1.3 %collective-permute-done.7.cross = f32[32,256]{1,0:T(8,128)S(1)} collective-permute-done((f32[32,256]{1,0:T(8,128)S(1)}, f32[32,256]{1,0:T(8,128)S(1)}, u32[]{:S(2)}, u32[]{:S(2)}) %collective-permute-start.7) | collective-permute-done | bytes 32800 | tf_op jit(solution)/shard_map/ppermute | solution.py:599
  34.3 3.4 %back.1 = (f32[16,40,128]{2,1,0:T(8,128)S(1)}, f32[16,40,128]{2,1,0:T(8,128)S(1)}) custom-call(s32[1]{0:T(128)} %bitcast.parity_ref, f32[256,256]{1,0:T(8,128)S(1)} %get-tuple-element.113.base_ref, f32[256,256]{1,0:T(8,128)S(1)} %get-tuple-element.107.adjoint_ref, f32[32,256]{1,0:T(8,128)S(1)} %collective-permute-done.6.in_chip, ...), custom_call_target="tpu_custom_call" | custom-call | flops 4600000000 | bytes 1000000 | tf_op jit(solution)/shard_map/back/pallas_call | solution.py:108
  37.7 7.2 %collective-permute-start.8 = (f32[16,40,128]{2,1,0:T(8,128)S(1)}, f32[16,40,128]{2,1,0:T(8,128)S(1)}, u32[]{:S(2)}, u32[]{:S(2)}) collective-permute-start(f32[16,40,128]{2,1,0:T(8,128)S(1)} %get-tuple-element.132), channel_id=1, source_target_pairs={{0,1},{1,0},{2,3},{3,2},{4,5},{5,4},{6,7},{7,6},{8,9},{9,8},{10,11... | collective-permute-start | bytes 983048 | tf_op jit(solution)/shard_map/ppermute | solution.py:680
  44.9 1.3 %collective-permute-done.8.got_ref = f32[16,40,128]{2,1,0:T(8,128)S(1)} collective-permute-done((f32[16,40,128]{2,1,0:T(8,128)S(1)}, f32[16,40,128]{2,1,0:T(8,128)S(1)}, u32[]{:S(2)}, u32[]{:S(2)}) %collective-permute-start.8) | collective-permute-done | bytes 327712 | tf_op jit(solution)/shard_map/ppermute | solution.py:680
  46.2 11.2 %all_to_all.15.parts_ref = f32[16,40,128]{2,1,0:T(8,128)S(1)} all-to-all(f32[16,40,128]{2,1,0:T(8,128)S(1)} %chip_sum.1), channel_id=1, replica_groups=mesh['x'=4,'y'=4,'z'=8,'core'=2] {'x','y'}, dimensions={0} | all-to-all | bytes 655360 | tf_op jit(solution)/shard_map/all_to_all | solution.py:681
  57.4 13.5 %all_to_all.16.parts_ref = f32[8,40,128]{2,1,0:T(8,128)S(1)} all-to-all(f32[8,40,128]{2,1,0:T(8,128)S(1)} %plane_sum.1), channel_id=1, replica_groups=mesh['x'=4,'y'=4,'z'=8,'core'=2] {'z'}, dimensions={0} | all-to-all | bytes 327680 | tf_op jit(solution)/shard_map/all_to_all | solution.py:683
  70.9 11.2 %all_to_all.17.own_ref = f32[16,32,128]{2,1,0:T(8,128)S(1)} all-to-all(f32[16,32,128]{2,1,0:T(8,128)S(1)} %get-tuple-element.133), channel_id=1, replica_groups=mesh['x'=4,'y'=4,'z'=8,'core'=2] {'x','y'}, dimensions={0} | all-to-all | bytes 524288 | tf_op jit(solution)/shard_map/all_to_all | solution.py:685
  82.1 4.0 %collective-permute-start.9 = (f32[16,32,128]{2,1,0:T(8,128)S(1)}, f32[16,32,128]{2,1,0:T(8,128)S(1)}, u32[]{:S(2)}, u32[]{:S(2)}) collective-permute-start(f32[16,32,128]{2,1,0:T(8,128)S(1)} %all_to_all.17.own_ref), channel_id=1, source_target_pairs={{0,1},{1,0},{2,3},{3,2},{4,5},{5,4},{6,7},{7,6},{8,9},{9,8},{10,11... | collective-permute-start | bytes 786440 | tf_op jit(solution)/shard_map/ppermute | solution.py:686
  86.1 1.2 %collective-permute-done.9.other_ref = f32[16,32,128]{2,1,0:T(8,128)S(1)} collective-permute-done((f32[16,32,128]{2,1,0:T(8,128)S(1)}, f32[16,32,128]{2,1,0:T(8,128)S(1)}, u32[]{:S(2)}, u32[]{:S(2)}) %collective-permute-start.9) | collective-permute-done | bytes 262176 | tf_op jit(solution)/shard_map/ppermute | solution.py:686
  87.3 1.0 %scale.1 = (f32[256,256]{1,0:T(8,128)}, f32[1,256]{1,0:T(1,128)}, f32[256,256]{1,0:T(8,128)}, f32[1,256]{1,0:T(1,128)}, f32[1,1]{1,0:T(1,128)}) custom-call(s32[1]{0:T(128)} %bitcast.parity_ref, f32[16,32,128]{2,1,0:T(8,128)S(1)} %all_to_all.17.own_ref, f32[16,32,128]{2,1,0:T(8,128)S(1)} %collective-permute-done.9.other_ref, ...), custom_call_target="tpu_custom_call" | custom-call | flops 1150000000 | bytes 1000000 | tf_op jit(solution)/shard_map/scale/pallas_call | solution.py:108
  (5 shorter events, 0.1 us)
Async XLA Ops:
  0.6 0.7 copy-start.5
  1.3 0.7 copy-start.7
  1.3 0.7 copy-start.6
  2.0 13.6 %copy-start = (f32[256,256]{1,0:T(8,128)S(1)}, f32[256,256]{1,0:T(8,128)}, u32[]{:S(2)}) copy-start(f32[256,256]{1,0:T(8,128)} %w_out_ref.1) | copy-start | bytes 786436
  2.1 13.6 %copy-start.2 = (bf16[512,256]{1,0:T(8,128)(2,1)S(1)}, bf16[512,256]{1,0:T(8,128)(2,1)}, u32[]{:S(2)}) copy-start(bf16[512,256]{1,0:T(8,128)(2,1)} %constant.16.clone.inner) | copy-start | bytes 786436
  2.1 13.6 %copy-start.3 = (bf16[64,256]{1,0:T(8,128)(2,1)S(1)}, bf16[64,256]{1,0:T(8,128)(2,1)}, u32[]{:S(2)}) copy-start(bf16[64,256]{1,0:T(8,128)(2,1)} %constant.18.clone.lift_t) | copy-start | bytes 98308
  2.1 13.6 %copy-start.4 = (bf16[64,256]{1,0:T(8,128)(2,1)S(1)}, bf16[64,256]{1,0:T(8,128)(2,1)}, u32[]{:S(2)}) copy-start(bf16[64,256]{1,0:T(8,128)(2,1)} %constant.17.clone.leave) | copy-start | bytes 98308
  4.1 13.0 %collective-permute-start.1 = (f32[40,256]{1,0:T(8,128)S(1)}, f32[40,256]{1,0:T(8,128)S(1)}, u32[]{:S(2)}, u32[]{:S(2)}) collective-permute-start(f32[40,256]{1,0:T(8,128)S(1)} %get-tuple-element.79), channel_id=1, source_target_pairs={{0,255},{1,2},{2,1},{3,4},{4,3},{5,6},{6,5},{7,8},{8,7},{9,10},{10... | collective-permute-start | bytes 122888 | tf_op jit(solution)/shard_map/ppermute | solution.py:599
  7.3 9.9 %collective-permute-start = (f32[40,256]{1,0:T(8,128)S(1)}, f32[40,256]{1,0:T(8,128)S(1)}, u32[]{:S(2)}, u32[]{:S(2)}) collective-permute-start(f32[40,256]{1,0:T(8,128)S(1)} %get-tuple-element.77.after_ref), channel_id=1, source_target_pairs={{0,1},{1,0},{2,3},{3,2},{4,5},{5,4},{6,7},{7,6},{8,9},{9,8},{10,11... | collective-permute-start | bytes 122888 | tf_op jit(solution)/shard_map/ppermute | solution.py:600
  19.2 9.1 %collective-permute-start.2 = (f32[32,256]{1,0:T(8,128)S(1)}, f32[32,256]{1,0:T(8,128)S(1)}, u32[]{:S(2)}, u32[]{:S(2)}) collective-permute-start(f32[32,256]{1,0:T(8,128)S(1)} %get-tuple-element.96), channel_id=1, source_target_pairs={{0,1},{1,0},{2,3},{3,2},{4,5},{5,4},{6,7},{7,6},{8,9},{9,8},{10,11... | collective-permute-start | bytes 98312 | tf_op jit(solution)/shard_map/ppermute | solution.py:600
  19.5 8.9 %collective-permute-start.3 = (f32[32,256]{1,0:T(8,128)S(1)}, f32[32,256]{1,0:T(8,128)S(1)}, u32[]{:S(2)}, u32[]{:S(2)}) collective-permute-start(f32[32,256]{1,0:T(8,128)S(1)} %get-tuple-element.97), channel_id=1, source_target_pairs={{0,255},{1,2},{2,1},{3,4},{4,3},{5,6},{6,5},{7,8},{8,7},{9,10},{10... | collective-permute-start | bytes 98312 | tf_op jit(solution)/shard_map/ppermute | solution.py:599
  19.5 8.9 %copy-start.1 = (f32[256,256]{1,0:T(8,128)S(1)}, f32[256,256]{1,0:T(8,128)}, u32[]{:S(2)}) copy-start(f32[256,256]{1,0:T(8,128)} %target_ref.1) | copy-start | bytes 786436
  20.8 10.2 %collective-permute-start.5 = (f32[256,256]{1,0:T(8,128)S(1)}, f32[256,256]{1,0:T(8,128)S(1)}, u32[]{:S(2)}, u32[]{:S(2)}) collective-permute-start(f32[256,256]{1,0:T(8,128)S(1)} %get-tuple-element.112), channel_id=1, source_target_pairs={{0,255},{1,2},{2,1},{3,4},{4,3},{5,6},{6,5},{7,8},{8,7},{9,10},{10... | collective-permute-start | bytes 786440 | tf_op jit(solution)/shard_map/ppermute | solution.py:599
  22.6 8.4 %collective-permute-start.4 = (f32[256,256]{1,0:T(8,128)S(1)}, f32[256,256]{1,0:T(8,128)S(1)}, u32[]{:S(2)}, u32[]{:S(2)}) collective-permute-start(f32[256,256]{1,0:T(8,128)S(1)} %get-tuple-element.112), channel_id=1, source_target_pairs={{0,1},{1,0},{2,3},{3,2},{4,5},{5,4},{6,7},{7,6},{8,9},{9,8},{10,11... | collective-permute-start | bytes 786440 | tf_op jit(solution)/shard_map/ppermute | solution.py:600
  30.8 2.2 %collective-permute-start.6 = (f32[32,256]{1,0:T(8,128)S(1)}, f32[32,256]{1,0:T(8,128)S(1)}, u32[]{:S(2)}, u32[]{:S(2)}) collective-permute-start(f32[32,256]{1,0:T(8,128)S(1)} %get-tuple-element.114), channel_id=1, source_target_pairs={{0,1},{1,0},{2,3},{3,2},{4,5},{5,4},{6,7},{7,6},{8,9},{9,8},{10,11... | collective-permute-start | bytes 98312 | tf_op jit(solution)/shard_map/ppermute | solution.py:600
  31.0 3.3 %collective-permute-start.7 = (f32[32,256]{1,0:T(8,128)S(1)}, f32[32,256]{1,0:T(8,128)S(1)}, u32[]{:S(2)}, u32[]{:S(2)}) collective-permute-start(f32[32,256]{1,0:T(8,128)S(1)} %get-tuple-element.115), channel_id=1, source_target_pairs={{0,255},{1,2},{2,1},{3,4},{4,3},{5,6},{6,5},{7,8},{8,7},{9,10},{10... | collective-permute-start | bytes 98312 | tf_op jit(solution)/shard_map/ppermute | solution.py:599
  37.7 8.5 %collective-permute-start.8 = (f32[16,40,128]{2,1,0:T(8,128)S(1)}, f32[16,40,128]{2,1,0:T(8,128)S(1)}, u32[]{:S(2)}, u32[]{:S(2)}) collective-permute-start(f32[16,40,128]{2,1,0:T(8,128)S(1)} %get-tuple-element.132), channel_id=1, source_target_pairs={{0,1},{1,0},{2,3},{3,2},{4,5},{5,4},{6,7},{7,6},{8,9},{9,8},{10,11... | collective-permute-start | bytes 983048 | tf_op jit(solution)/shard_map/ppermute | solution.py:680
  82.1 5.2 %collective-permute-start.9 = (f32[16,32,128]{2,1,0:T(8,128)S(1)}, f32[16,32,128]{2,1,0:T(8,128)S(1)}, u32[]{:S(2)}, u32[]{:S(2)}) collective-permute-start(f32[16,32,128]{2,1,0:T(8,128)S(1)} %all_to_all.17.own_ref), channel_id=1, source_target_pairs={{0,1},{1,0},{2,3},{3,2},{4,5},{5,4},{6,7},{7,6},{8,9},{9,8},{10,11... | collective-permute-start | bytes 786440 | tf_op jit(solution)/shard_map/ppermute | solution.py:686

commit v5 on v4

--- a/solution.py
+++ b/solution.py
@@ -162,26 +162,25 @@
     return (rows == column).astype(F32).astype(BF16)
 
 
-def make_near(small_ref, near):
-    rows = lax.broadcasted_iota(jnp.int32, (256, 256), 0).astype(F32)
+def make_near(index_ref, near):
+    rows = lax.broadcasted_iota(jnp.int32, (256, 256), 0)
     for face in range(2, 6):
-        near[face - 2] = one_hot(rows, small_ref[face : face + 1] - 256.0 * (face ^ 1))
+        near[face - 2] = one_hot(rows, index_ref[face : face + 1] - 256 * (face ^ 1))
 
 
 def first_kernel(
-    parity_ref, state_far, w_in_far, fixed_far, w_out_far, small_ref,
+    parity_ref, state_far, w_in_far, fixed_far, w_out_far, nbr_far, send_far, b_in_far,
     arrived_ref, hidden_ref, in_chip_ref, cross_ref, w_in, state_ref,
-    w_in_ref, w_out_ref, fixed, near, sems,
+    w_in_ref, w_out_ref, fixed, near, nbr_ref, send_ref, b_in, sems,
 ):
     pairs = (
         (state_far, state_ref), (w_in_far, w_in_ref), (fixed_far.at[0:256], fixed), (w_out_far.at[0:16], w_out_ref.at[0:16]),
         (w_out_far.at[48:80], w_out_ref.at[16:48]), (w_out_far.at[112:128], w_out_ref.at[48:64]),
+        (nbr_far, nbr_ref), (send_far, send_ref), (b_in_far, b_in),
     )
     copies = [pltpu.make_async_copy(s, t, sems.at[n]) for n, (s, t) in enumerate(pairs)]
     for copy in copies:
         copy.start()
-    make_near(small_ref, near)
-    bias = wide(small_ref.at[8:9])
     copies[0].wait()
     values = state_ref[...]
     edge = edge_rows(values)
@@ -190,17 +189,20 @@
     put(parity, *leaving(edge), in_chip_ref, cross_ref)
     copies[1].wait()
     w_in[0], w_in[1] = split(w_in_ref[...])
+    copies[8].wait()
+    bias = wide(b_in)
     hidden = jnp.tanh(mm3(pair(w_in), parts) + bias)
     hidden_ref[...] = hidden
-    for copy in copies[2:]:
+    for copy in copies[2:8]:
         copy.wait()
+    make_near(nbr_ref, near)
     arrive_near(mm(fixed[128:192], parts[0]) + mm(fixed[128:192], parts[1]), near, arrived_ref)
     rates = mm3((fixed[0:64], fixed[64:128]), parts) + mm3(split(w_out_ref[...]), split(hidden))
     lift = fixed[192:256, 0:64]
     rates += mm(lift, arrived_ref[0]) + mm(lift, arrived_ref[1])
     put(parity, *leaving(edge + TIME_STEP * rates), in_chip_ref, cross_ref, 16)
-    down_index = small_ref[6:7]
-    up_index = small_ref[7:8] - 256.0
+    down_index = send_ref[0:1].astype(F32)
+    up_index = (send_ref[1:2] - 256).astype(F32)
     even = parity == 0
     in_chip_ref[32:40] = jnp.broadcast_to(jnp.where(even, up_index, down_index), (8, 256))
     cross_ref[32:40] = jnp.broadcast_to(jnp.where(even, down_index, up_index), (8, 256))
@@ -224,11 +226,10 @@
 
 
 def tables_kernel(
-    w_in, w_out_ref, inner, leave, lift_t, small_ref, state_ref, arrived_ref, hidden_ref, after_ref,
+    w_in, w_out_ref, inner, leave, lift_t, nbr_ref, b_in, b_out, state_ref, arrived_ref, hidden_ref, after_ref,
     next_ref, sum_ref, linear_ref, out_ref, w_out, in_t_ref, out_t_ref, inner_t, leave_t, lift,
     near, far_ref, column_in, column_out, in_deep, inner_deep, leave_deep, out_deep, inner_t_deep, lift_t_deep, eff_ref,
 ):
-    b_in, b_out = small_ref.at[8:9], small_ref.at[9:10]
     column_in[...] = column(b_in)
     column_out[...] = column(b_out)
     second = w_out_ref[...]
@@ -241,10 +242,10 @@
     base = values + TIME_STEP * rates
     next_ref[...] = base
     sum_ref[...], linear_ref[...], out_ref[...] = prepare(split(base), network)
-    make_near(small_ref, near)
-    rows = lax.broadcasted_iota(jnp.int32, (256, 256), 0).astype(F32)
+    make_near(nbr_ref, near)
+    rows = lax.broadcasted_iota(jnp.int32, (256, 256), 0)
     for face in range(2):
-        far_ref[face] = one_hot(rows, small_ref[face : face + 1] - (1536.0 + 256.0 * face))
+        far_ref[face] = one_hot(rows, nbr_ref[face : face + 1] - (1536 + 256 * face))
     for part in range(2):
         in_t_ref[part] = flip(w_in[part])
         out_t_ref[part] = flip(w_out[part])
@@ -336,7 +337,7 @@
 
 
 def middle_kernel(
-    parity_ref, base_ref, state_ref, in_chip, cross, far_ref, sum_ref, linear_ref, out_ref, in_deep, inner_deep, leave_deep,
+    parity_ref, base_ref, state_ref, cross, in_chip, far_ref, sum_ref, linear_ref, out_ref, in_deep, inner_deep, leave_deep,
     w_in, b_in, w_out, b_out, inner, leave, lift, near,
     second_ref, third_ref, hidden_second, hidden_third, arrived_ref, link, in_chip_out, cross_out, between,
 ):
@@ -398,7 +399,7 @@
 
 
 def turn_kernel(
-    parity_ref, base_ref, third_ref, in_chip, cross, link, target_ref,
+    parity_ref, base_ref, third_ref, cross, in_chip, link, target_ref,
     sum_ref, linear_ref, out_ref, in_deep, inner_deep, leave_deep,
     w_in, b_in, w_out, b_out, inner, leave, lift, near, w_in_t, w_out_t, inner_t, leave_t, lift_t,
     final_ref, loss_ref, fourth_ref, hidden_ref, adjoint_ref, delta_ref, gathered_ref, in_chip_out, cross_out,
@@ -453,9 +454,9 @@
 
 
 def beside_kernel(
-    adjoint_ref, delta_ref, gathered_ref, state_ref, hidden_ref, in_chip, cross, w_in, b_in,
+    adjoint_ref, delta_ref, gathered_ref, state_ref, hidden_ref,
     w_in_t, inner_t, leave_t, lift_t, near, w_out_t, hidden_third,
-    next_ref, grad_in, grad_out, extra, in_chip_hidden, cross_hidden, back_ref, linear_ref, out_ref,
+    next_ref, grad_in, grad_out, extra, back_ref, linear_ref, out_ref,
 ):
     adjoint = adjoint_ref[...]
     parts, delta_parts = split(adjoint), split(delta_ref[...])
@@ -470,14 +471,17 @@
     grad_in[...] = first
     grad_out[...] = second + mm3(base_parts, split(hidden_third[...]), mm_nt)
     extra[...] = bias
-    for source, ref in ((in_chip, in_chip_hidden), (cross, cross_hidden)):
+
+
+def hidden_kernel(cross, in_chip, w_in, b_in, cross_hidden, in_chip_hidden):
+    for source, ref in ((cross, cross_hidden), (in_chip, in_chip_hidden)):
         ref[...] = jnp.tanh(mm3(pair(w_in), split(source[...])) + wide(b_in))
 
 
 def back_kernel(
-    parity_ref, base_ref, adjoint_ref, in_chip, cross, link,
+    parity_ref, base_ref, adjoint_ref, cross, in_chip, link,
     third_ref, hidden_third, second_ref, hidden_second, state_ref, hidden_first,
-    in_chip_state, cross_state, in_chip_hidden, cross_hidden,
+    cross_state, in_chip_state, cross_hidden, in_chip_hidden,
     near, w_in_t, w_out_t, inner_t, leave_t, lift_t, eff, back_ref, linear_ref, out_ref, out_deep, inner_t_deep, lift_t_deep,
     old_in, old_out, old_extra, loss_ref,
     keep_ref, send_ref, now_ref, between, sum_ref,
@@ -596,8 +600,7 @@
 
 
 def exchange(in_chip, cross):
-    crossed = lax.ppermute(cross, AXES, CROSS)
-    return lax.ppermute(in_chip, AXES, IN_CHIP), crossed
+    return lax.ppermute(cross, AXES, CROSS), lax.ppermute(in_chip, AXES, IN_CHIP)
 
 
 def local(state, target, w_in, b_in, w_out, b_out, nbr, send):
@@ -609,20 +612,20 @@
     fixed[128:192], fixed[192:256, 0:64] = leave, lift[edge]
     to_bf16 = lambda values: jnp.asarray(values.astype(ml_dtypes.bfloat16))
     fixed, inner2, leave1, lift_t = (to_bf16(x) for x in (fixed, np.concatenate(halves(inner)), leave, lift.T))
-    rows = ((0, nbr), (6, send), (8, b_in.reshape(1, 256)), (9, b_out.reshape(1, 256)))
-    small = sum(jnp.pad(x.astype(F32), ((at, 16 - at - x.shape[0]), (0, 0))) for at, x in rows)
+    b_in, b_out = b_in.reshape(1, 256), b_out.reshape(1, 256)
     tall, flat, thin = ((512, 256), BF16), ((64, 256), BF16), ((256, 64), BF16)
     arrival = ((2, 64, 256), BF16)
     arrived, hidden_first, *edge, w_in2, state = call(
         first_kernel,
         [arrival, SQUARE, ((40, 256), F32), ((40, 256), F32), PAIR, SQUARE],
-        parity, state, w_in, fixed, w_out, small,
+        parity, state, w_in, fixed, w_out, nbr, send, b_in,
         name="first", micros=1.5,
-        far=range(1, 5),
+        far=range(1, 8),
         limit=53,
         scratch=[
             pltpu.VMEM((256, 256), F32), pltpu.VMEM((64, 256), F32), pltpu.VMEM((256, 256), BF16),
-            pltpu.VMEM((4, 256, 256), BF16), pltpu.SemaphoreType.DMA((6,)),
+            pltpu.VMEM((4, 256, 256), BF16), pltpu.VMEM((6, 256), jnp.int32), pltpu.VMEM((2, 256), jnp.int32),
+            pltpu.VMEM((1, 256), F32), pltpu.SemaphoreType.DMA((9,)),
         ],
     )
     got = exchange(*edge)
@@ -634,7 +637,7 @@
         + [((256, 128), F32)] * 2
         + [depth, depth, shallow] * 2
         + [((2, 256, 48), BF16)],
-        w_in2, w_out, inner2, leave1, lift_t, small, state, arrived, hidden_first, edge[0],
+        w_in2, w_out, inner2, leave1, lift_t, nbr, b_in, b_out, state, arrived, hidden_first, edge[0],
         name="tables", micros=1.5,
     )
     base, prepared, deeps, eff = made[0], made[1:4], made[14:20], made[20]
@@ -662,17 +665,18 @@
         name="turn", micros=2.5, scratch=[square, pltpu.VMEM((2, 64, 256), BF16)],
     )
     got = exchange(*edge)
-    base, *grads, in_chip_hidden, cross_hidden, back_product, linear, out = call(
+    base, *grads, back_product, linear, out = call(
         beside_kernel,
-        [SQUARE, SQUARE, SQUARE, EXTRA, SQUARE, SQUARE, *middle],
-        adjoint, delta, gathered, fourth, hidden_fourth, *beside, w_in2, b_in2, *back, near, w_out_t, hidden_third,
-        name="beside", micros=2,
-    )
+        [SQUARE, SQUARE, SQUARE, EXTRA, *middle],
+        adjoint, delta, gathered, fourth, hidden_fourth, *back, near, w_out_t, hidden_third,
+        name="beside", micros=1.4,
+    )
+    beside_hidden = call(hidden_kernel, [SQUARE] * 2, *beside, w_in2, b_in2, name="hidden", micros=0.6)
     keep, give = call(
         back_kernel,
         [PACKED] * 2,
         parity, base, adjoint, *got, link, third, hidden_third, second, hidden_second, state, hidden_first,
-        *beside, in_chip_hidden, cross_hidden, near, w_in_t, w_out_t, inner_t, leave_t, lift_t, eff,
+        *beside, *beside_hidden, near, w_in_t, w_out_t, inner_t, leave_t, lift_t, eff,
         back_product, linear, out, *backward_deeps, *grads, loss,
         name="back", micros=4, scratch=[square] * 3,
     )

time: 88.6 us -> 88.2 us (level)
  local copies, waits for them, and re-layouts: 0.72 us -> 2.04 us
  waiting for transfers between devices: 3.72 us -> 2.7 us
  starting transfers between devices: 30.8 us -> 29.9 us
    ppermute x1, starting transfers between devices: 7.2 us -> 0.2 us  [local(): lax.ppermute(give, 'core', swap)]
    ppermute x8, starting transfers between devices: 19.6 us -> 25.7 us  [the longest x4 21.2 us: exchange(): lax.ppermute(in_chip, AXES, IN_CHIP)]
    unnamed x16 -> x18, local copies, waits for them, and re-layouts: 0.72 us -> 2.04 us
    ppermute x8, waiting for transfers between devices: 1.3 us -> 0.02 us  [the longest x4 0.01 us: exchange(): lax.ppermute(in_chip, AXES, IN_CHIP)]
    pallas_call x11 -> x12, Pallas kernels: 15.8 us -> 15.9 us  [call(): pl.pallas_call(body, out_shape=[jax.ShapeDtypeStruct(s, t) for s, t in ou...]
  transfers between devices with their start and end apart: 10 -> 10, of which waited for: 3 -> 2; matrix products, arithmetic and copies ran while one was open for 0% -> 0% of each run, Pallas kernels for 8% -> 8%
where the time goes in v5:
time: 88.2 us; the launch traced here: 87.9 us
  blocking collectives  36.6 us (41%)
  starting transfers between devices  29.9 us (34%)
  Pallas kernels  15.9 us (18%)
  waiting for transfers between devices  2.7 us (3%)
  local copies, waits for them, and re-layouts  2.04 us (2%)
    ppermute x4, starting transfers between devices, exchange(): lax.ppermute(in_chip, AXES, IN_CHIP)  21.2 us
    pallas_call x12, Pallas kernels, call(): pl.pallas_call(body, out_shape=[jax.ShapeDtypeStruct(s, t) for s, t in ou...  15.9 us
    all_to_all x1, blocking collectives, local(): parts = lax.all_to_all(parts, 'z', 0, 0, tiled=True)  14.3 us
    all_to_all x1, blocking collectives, local(): own = lax.all_to_all(parts, PLANE, 0, 0, tiled=True)  11.2 us
    all_to_all x1, blocking collectives, local(): parts = lax.all_to_all(parts, PLANE, 0, 0, tiled=True)  11.1 us
    ppermute x4, starting transfers between devices, exchange(): lax.ppermute(cross, AXES, CROSS)  4.48 us
    ppermute x1, starting transfers between devices, local(): other = lax.ppermute(own, 'core', swap)  4.01 us
    unnamed x18, local copies, waits for them, and re-layouts  2.04 us
  transfers between devices with their start and end apart: 10, of which 2 were waited for; matrix products, arithmetic and copies ran while one was open for 0% of the time, Pallas kernels for 8%

profile of v5, /device:TPU:1, one launch (start us, length us, event | category | flops | bytes accessed | tf_op | source)
XLA Modules:
  0.0 87.9 jit_solution(4120023028915434487)
XLA Ops:
  0.6 0.0 copy-start.2
  0.6 0.0 copy-start.4
  0.7 0.7 copy-done.2
  1.3 0.0 copy-done.4
  1.3 0.0 copy-start.3
  1.3 0.7 copy-done.3
  2.0 0.0 copy-start
  2.0 0.0 copy-start.6
  2.0 0.0 copy-start.7
  2.0 0.0 copy-start.8
  2.0 2.1 %first.1 = (bf16[2,64,256]{2,1,0:T(8,128)(2,1)S(1)}, f32[256,256]{1,0:T(8,128)S(1)}, f32[40,256]{1,0:T(8,128)S(1)}, f32[40,256]{1,0:T(8,128)S(1)}, bf16[2,256,25...) custom-call(s32[1]{0:T(128)} %bitcast.parity_ref, f32[256,256]{1,0:T(8,128)} %state_far.1, f32[256,256]{1,0:T(8,128)} %w_in_far.1, ...), custom_call_target="tpu_custom_call" | custom-call | flops 1724999936 | bytes 1000000 | tf_op jit(solution)/shard_map/first/pallas_call | solution.py:108
  4.2 3.1 %collective-permute-start = (f32[40,256]{1,0:T(8,128)S(1)}, f32[40,256]{1,0:T(8,128)S(1)}, u32[]{:S(2)}, u32[]{:S(2)}) collective-permute-start(f32[40,256]{1,0:T(8,128)S(1)} %get-tuple-element.79), channel_id=1, source_target_pairs={{0,255},{1,2},{2,1},{3,4},{4,3},{5,6},{6,5},{7,8},{8,7},{9,10},{10... | collective-permute-start | bytes 122888 | tf_op jit(solution)/shard_map/ppermute | solution.py:603
  7.3 8.4 %collective-permute-start.1 = (f32[40,256]{1,0:T(8,128)S(1)}, f32[40,256]{1,0:T(8,128)S(1)}, u32[]{:S(2)}, u32[]{:S(2)}) collective-permute-start(f32[40,256]{1,0:T(8,128)S(1)} %get-tuple-element.77.after_ref), channel_id=1, source_target_pairs={{0,1},{1,0},{2,3},{3,2},{4,5},{5,4},{6,7},{7,6},{8,9},{9,8},{10,11... | collective-permute-start | bytes 122888 | tf_op jit(solution)/shard_map/ppermute | solution.py:603
  15.7 0.0 copy-done
  15.7 0.0 copy-done.6
  15.7 0.0 copy-done.7
  15.7 0.0 copy-done.8
  15.7 0.7 copy-done.5
  16.4 1.5 %tables.1 = (f32[256,256]{1,0:T(8,128)S(1)}, f32[256,256]{1,0:T(8,128)S(1)}, f32[256,256]{1,0:T(8,128)S(1)}, f32[64,256]{1,0:T(8,128)S(1)}, bf16[2,256,256]{2,1,...) custom-call(bf16[2,256,256]{2,1,0:T(8,128)(2,1)S(1)} %get-tuple-elem, ...), custom_call_target="tpu_custom_call" | custom-call | flops 1724999936 | bytes 1000000 | tf_op jit(solution)/shard_map/tables/pallas_call | solution.py:108
  17.9 0.0 collective-permute-done.cross
  17.9 0.0 collective-permute-done.1.in_chip
  17.9 2.0 %middle.1 = (f32[256,256]{1,0:T(8,128)S(1)}, f32[256,256]{1,0:T(8,128)S(1)}, f32[256,256]{1,0:T(8,128)S(1)}, f32[256,256]{1,0:T(8,128)S(1)}, bf16[2,64,256]{2,1,...) custom-call(s32[1]{0:T(128)} %bitcast.parity_ref, ...), custom_call_target="tpu_custom_call" | custom-call | flops 2415000064 | bytes 1000000 | tf_op jit(solution)/shard_map/middle/pallas_call | solution.py:108
  20.0 0.1 collective-permute-start.2
  20.1 6.6 %collective-permute-start.3 = (f32[32,256]{1,0:T(8,128)S(1)}, f32[32,256]{1,0:T(8,128)S(1)}, u32[]{:S(2)}, u32[]{:S(2)}) collective-permute-start(f32[32,256]{1,0:T(8,128)S(1)} %get-tuple-element.97), channel_id=1, source_target_pairs={{0,1},{1,0},{2,3},{3,2},{4,5},{5,4},{6,7},{7,6},{8,9},{9,8},{10,11... | collective-permute-start | bytes 98312 | tf_op jit(solution)/shard_map/ppermute | solution.py:603
  26.7 1.3 %rest.1 = (f32[256,256]{1,0:T(8,128)S(1)}, f32[256,256]{1,0:T(8,128)S(1)}, f32[256,256]{1,0:T(8,128)S(1)}, f32[64,256]{1,0:T(8,128)S(1)}, f32[256,256]{1,0:T(8,128)S(1)}) custom-call(f32[256,256]{1,0:T(8,128)S(1)} %get-tuple-element.92.third_ref, f32[256,256]{1,0:T(8,128)S(1)} %get-tuple-element.93.hidden_ref.hidden_third, ...), custom_call_target="tpu_custom_call" | custom-call | flops 1035000000 | bytes 1000000 | tf_op jit(solution)/shard_map/rest/pallas_call | solution.py:108
  27.9 0.1 collective-permute-start.6
  28.0 0.6 collective-permute-start.7
  28.6 0.0 collective-permute-done.2.cross
  28.6 0.0 collective-permute-done.3.in_chip
  28.6 0.0 copy-done.1
  28.6 2.4 %turn.1 = (f32[256,256]{1,0:T(8,128)}, f32[8,128]{1,0:T(8,128)S(1)}, f32[256,256]{1,0:T(8,128)S(1)}, f32[256,256]{1,0:T(8,128)S(1)}, f32[256,256]{1,0:T(8,128)S(...) custom-call(s32[1]{0:T(128)} %bitcast.parity_ref, ...), custom_call_target="tpu_custom_call" | custom-call | flops 2875000064 | bytes 1000000 | tf_op jit(solution)/shard_map/turn/pallas_call | solution.py:108
  31.0 1.2 %collective-permute-start.4 = (f32[32,256]{1,0:T(8,128)S(1)}, f32[32,256]{1,0:T(8,128)S(1)}, u32[]{:S(2)}, u32[]{:S(2)}) collective-permute-start(f32[32,256]{1,0:T(8,128)S(1)} %get-tuple-element.113), channel_id=1, source_target_pairs={{0,255},{1,2},{2,1},{3,4},{4,3},{5,6},{6,5},{7,8},{8,7},{9,10},{10... | collective-permute-start | bytes 98312 | tf_op jit(solution)/shard_map/ppermute | solution.py:603
  32.2 5.6 %collective-permute-start.5 = (f32[32,256]{1,0:T(8,128)S(1)}, f32[32,256]{1,0:T(8,128)S(1)}, u32[]{:S(2)}, u32[]{:S(2)}) collective-permute-start(f32[32,256]{1,0:T(8,128)S(1)} %get-tuple-element.114), channel_id=1, source_target_pairs={{0,1},{1,0},{2,3},{3,2},{4,5},{5,4},{6,7},{7,6},{8,9},{9,8},{10,11... | collective-permute-start | bytes 98312 | tf_op jit(solution)/shard_map/ppermute | solution.py:603
  37.8 1.6 %beside.1 = (f32[256,256]{1,0:T(8,128)S(1)}, f32[256,256]{1,0:T(8,128)S(1)}, f32[256,256]{1,0:T(8,128)S(1)}, f32[8,128]{1,0:T(8,128)S(1)}, f32[256,256]{1,0:T(8,...) custom-call(f32[256,256]{1,0:T(8,128)S(1)} %get-tuple-element.107.adjoint_ref, ...), custom_call_target="tpu_custom_call" | custom-call | flops 1610000000 | bytes 1000000 | tf_op jit(solution)/shard_map/beside/pallas_call | solution.py:108
  39.4 0.0 collective-permute-done.6.cross.cross_state
  39.4 0.0 collective-permute-done.7.in_chip.in_chip_state
  39.4 0.4 hidden.1
  39.8 0.0 collective-permute-done.4.cross
  39.8 0.0 collective-permute-done.5.in_chip
  39.8 3.4 %back.1 = (f32[16,40,128]{2,1,0:T(8,128)S(1)}, f32[16,40,128]{2,1,0:T(8,128)S(1)}) custom-call(s32[1]{0:T(128)} %bitcast.parity_ref, f32[256,256]{1,0:T(8,128)S(1)} %get-tuple-element.112.base_ref, f32[256,256]{1,0:T(8,128)S(1)} %get-tuple-element.107.adjoint_ref, f32[32,256]{1,0:T(8,128)S(1)} %collective-permute-done.4.cross, ...), custom_call_target="tpu_custom_call" | custom-call | flops 4600000000 | bytes 1000000 | tf_op jit(solution)/shard_map/back/pallas_call | solution.py:108
  43.2 0.2 collective-permute-start.8
  43.4 1.5 %collective-permute-done.8.got_ref = f32[16,40,128]{2,1,0:T(8,128)S(1)} collective-permute-done((f32[16,40,128]{2,1,0:T(8,128)S(1)}, f32[16,40,128]{2,1,0:T(8,128)S(1)}, u32[]{:S(2)}, u32[]{:S(2)}) %collective-permute-start.8) | collective-permute-done | bytes 327712 | tf_op jit(solution)/shard_map/ppermute | solution.py:684
  45.0 11.1 %all_to_all.15.parts_ref = f32[16,40,128]{2,1,0:T(8,128)S(1)} all-to-all(f32[16,40,128]{2,1,0:T(8,128)S(1)} %chip_sum.1), channel_id=1, replica_groups=mesh['x'=4,'y'=4,'z'=8,'core'=2] {'x','y'}, dimensions={0} | all-to-all | bytes 655360 | tf_op jit(solution)/shard_map/all_to_all | solution.py:685
  56.2 14.3 %all_to_all.16.parts_ref = f32[8,40,128]{2,1,0:T(8,128)S(1)} all-to-all(f32[8,40,128]{2,1,0:T(8,128)S(1)} %plane_sum.1), channel_id=1, replica_groups=mesh['x'=4,'y'=4,'z'=8,'core'=2] {'z'}, dimensions={0} | all-to-all | bytes 327680 | tf_op jit(solution)/shard_map/all_to_all | solution.py:687
  70.5 11.2 %all_to_all.17.own_ref = f32[16,32,128]{2,1,0:T(8,128)S(1)} all-to-all(f32[16,32,128]{2,1,0:T(8,128)S(1)} %get-tuple-element.133), channel_id=1, replica_groups=mesh['x'=4,'y'=4,'z'=8,'core'=2] {'x','y'}, dimensions={0} | all-to-all | bytes 524288 | tf_op jit(solution)/shard_map/all_to_all | solution.py:689
  81.7 4.0 %collective-permute-start.9 = (f32[16,32,128]{2,1,0:T(8,128)S(1)}, f32[16,32,128]{2,1,0:T(8,128)S(1)}, u32[]{:S(2)}, u32[]{:S(2)}) collective-permute-start(f32[16,32,128]{2,1,0:T(8,128)S(1)} %all_to_all.17.own_ref), channel_id=1, source_target_pairs={{0,1},{1,0},{2,3},{3,2},{4,5},{5,4},{6,7},{7,6},{8,9},{9,8},{10,11... | collective-permute-start | bytes 786440 | tf_op jit(solution)/shard_map/ppermute | solution.py:690
  85.7 1.2 %collective-permute-done.9.other_ref = f32[16,32,128]{2,1,0:T(8,128)S(1)} collective-permute-done((f32[16,32,128]{2,1,0:T(8,128)S(1)}, f32[16,32,128]{2,1,0:T(8,128)S(1)}, u32[]{:S(2)}, u32[]{:S(2)}) %collective-permute-start.9) | collective-permute-done | bytes 262176 | tf_op jit(solution)/shard_map/ppermute | solution.py:690
  86.9 1.0 %scale.1 = (f32[256,256]{1,0:T(8,128)}, f32[1,256]{1,0:T(1,128)}, f32[256,256]{1,0:T(8,128)}, f32[1,256]{1,0:T(1,128)}, f32[1,1]{1,0:T(1,128)}) custom-call(s32[1]{0:T(128)} %bitcast.parity_ref, f32[16,32,128]{2,1,0:T(8,128)S(1)} %all_to_all.17.own_ref, f32[16,32,128]{2,1,0:T(8,128)S(1)} %collective-permute-done.9.other_ref, ...), custom_call_target="tpu_custom_call" | custom-call | flops 1150000000 | bytes 1000000 | tf_op jit(solution)/shard_map/scale/pallas_call | solution.py:108
  (5 shorter events, 0.1 us)
Async XLA Ops:
  0.6 0.7 copy-start.2
  0.6 0.7 copy-start.4
  1.3 0.7 copy-start.3
  2.0 13.7 %copy-start = (f32[256,256]{1,0:T(8,128)S(1)}, f32[256,256]{1,0:T(8,128)}, u32[]{:S(2)}) copy-start(f32[256,256]{1,0:T(8,128)} %w_out_ref.1) | copy-start | bytes 786436
  2.0 13.7 %copy-start.6 = (bf16[512,256]{1,0:T(8,128)(2,1)S(1)}, bf16[512,256]{1,0:T(8,128)(2,1)}, u32[]{:S(2)}) copy-start(bf16[512,256]{1,0:T(8,128)(2,1)} %constant.13.clone.inner) | copy-start | bytes 786436
  2.0 13.7 %copy-start.7 = (bf16[64,256]{1,0:T(8,128)(2,1)S(1)}, bf16[64,256]{1,0:T(8,128)(2,1)}, u32[]{:S(2)}) copy-start(bf16[64,256]{1,0:T(8,128)(2,1)} %constant.15.clone.lift_t) | copy-start | bytes 98308
  2.0 13.7 %copy-start.8 = (bf16[64,256]{1,0:T(8,128)(2,1)S(1)}, bf16[64,256]{1,0:T(8,128)(2,1)}, u32[]{:S(2)}) copy-start(bf16[64,256]{1,0:T(8,128)(2,1)} %constant.14.clone.leave) | copy-start | bytes 98308
  4.2 13.8 %collective-permute-start = (f32[40,256]{1,0:T(8,128)S(1)}, f32[40,256]{1,0:T(8,128)S(1)}, u32[]{:S(2)}, u32[]{:S(2)}) collective-permute-start(f32[40,256]{1,0:T(8,128)S(1)} %get-tuple-element.79), channel_id=1, source_target_pairs={{0,255},{1,2},{2,1},{3,4},{4,3},{5,6},{6,5},{7,8},{8,7},{9,10},{10... | collective-permute-start | bytes 122888 | tf_op jit(solution)/shard_map/ppermute | solution.py:603
  7.3 10.7 %collective-permute-start.1 = (f32[40,256]{1,0:T(8,128)S(1)}, f32[40,256]{1,0:T(8,128)S(1)}, u32[]{:S(2)}, u32[]{:S(2)}) collective-permute-start(f32[40,256]{1,0:T(8,128)S(1)} %get-tuple-element.77.after_ref), channel_id=1, source_target_pairs={{0,1},{1,0},{2,3},{3,2},{4,5},{5,4},{6,7},{7,6},{8,9},{9,8},{10,11... | collective-permute-start | bytes 122888 | tf_op jit(solution)/shard_map/ppermute | solution.py:603
  15.7 0.7 copy-start.5
  20.0 8.6 %collective-permute-start.2 = (f32[32,256]{1,0:T(8,128)S(1)}, f32[32,256]{1,0:T(8,128)S(1)}, u32[]{:S(2)}, u32[]{:S(2)}) collective-permute-start(f32[32,256]{1,0:T(8,128)S(1)} %get-tuple-element.96), channel_id=1, source_target_pairs={{0,255},{1,2},{2,1},{3,4},{4,3},{5,6},{6,5},{7,8},{8,7},{9,10},{10... | collective-permute-start | bytes 98312 | tf_op jit(solution)/shard_map/ppermute | solution.py:603
  20.1 8.5 %collective-permute-start.3 = (f32[32,256]{1,0:T(8,128)S(1)}, f32[32,256]{1,0:T(8,128)S(1)}, u32[]{:S(2)}, u32[]{:S(2)}) collective-permute-start(f32[32,256]{1,0:T(8,128)S(1)} %get-tuple-element.97), channel_id=1, source_target_pairs={{0,1},{1,0},{2,3},{3,2},{4,5},{5,4},{6,7},{7,6},{8,9},{9,8},{10,11... | collective-permute-start | bytes 98312 | tf_op jit(solution)/shard_map/ppermute | solution.py:603
  26.7 1.9 %copy-start.1 = (f32[256,256]{1,0:T(8,128)S(1)}, f32[256,256]{1,0:T(8,128)}, u32[]{:S(2)}) copy-start(f32[256,256]{1,0:T(8,128)} %target_ref.1) | copy-start | bytes 786436
  27.9 11.5 %collective-permute-start.6 = (f32[256,256]{1,0:T(8,128)S(1)}, f32[256,256]{1,0:T(8,128)S(1)}, u32[]{:S(2)}, u32[]{:S(2)}) collective-permute-start(f32[256,256]{1,0:T(8,128)S(1)} %get-tuple-element.117), channel_id=1, source_target_pairs={{0,255},{1,2},{2,1},{3,4},{4,3},{5,6},{6,5},{7,8},{8,7},{9,10},{10... | collective-permute-start | bytes 786440 | tf_op jit(solution)/shard_map/ppermute | solution.py:603
  28.0 11.4 %collective-permute-start.7 = (f32[256,256]{1,0:T(8,128)S(1)}, f32[256,256]{1,0:T(8,128)S(1)}, u32[]{:S(2)}, u32[]{:S(2)}) collective-permute-start(f32[256,256]{1,0:T(8,128)S(1)} %get-tuple-element.117), channel_id=1, source_target_pairs={{0,1},{1,0},{2,3},{3,2},{4,5},{5,4},{6,7},{7,6},{8,9},{9,8},{10,11... | collective-permute-start | bytes 786440 | tf_op jit(solution)/shard_map/ppermute | solution.py:603
  31.0 8.8 %collective-permute-start.4 = (f32[32,256]{1,0:T(8,128)S(1)}, f32[32,256]{1,0:T(8,128)S(1)}, u32[]{:S(2)}, u32[]{:S(2)}) collective-permute-start(f32[32,256]{1,0:T(8,128)S(1)} %get-tuple-element.113), channel_id=1, source_target_pairs={{0,255},{1,2},{2,1},{3,4},{4,3},{5,6},{6,5},{7,8},{8,7},{9,10},{10... | collective-permute-start | bytes 98312 | tf_op jit(solution)/shard_map/ppermute | solution.py:603
  32.2 7.6 %collective-permute-start.5 = (f32[32,256]{1,0:T(8,128)S(1)}, f32[32,256]{1,0:T(8,128)S(1)}, u32[]{:S(2)}, u32[]{:S(2)}) collective-permute-start(f32[32,256]{1,0:T(8,128)S(1)} %get-tuple-element.114), channel_id=1, source_target_pairs={{0,1},{1,0},{2,3},{3,2},{4,5},{5,4},{6,7},{7,6},{8,9},{9,8},{10,11... | collective-permute-start | bytes 98312 | tf_op jit(solution)/shard_map/ppermute | solution.py:603
  43.2 1.7 %collective-permute-start.8 = (f32[16,40,128]{2,1,0:T(8,128)S(1)}, f32[16,40,128]{2,1,0:T(8,128)S(1)}, u32[]{:S(2)}, u32[]{:S(2)}) collective-permute-start(f32[16,40,128]{2,1,0:T(8,128)S(1)} %get-tuple-element.132), channel_id=1, source_target_pairs={{0,1},{1,0},{2,3},{3,2},{4,5},{5,4},{6,7},{7,6},{8,9},{9,8},{10,11... | collective-permute-start | bytes 983048 | tf_op jit(solution)/shard_map/ppermute | solution.py:684
  81.7 5.2 %collective-permute-start.9 = (f32[16,32,128]{2,1,0:T(8,128)S(1)}, f32[16,32,128]{2,1,0:T(8,128)S(1)}, u32[]{:S(2)}, u32[]{:S(2)}) collective-permute-start(f32[16,32,128]{2,1,0:T(8,128)S(1)} %all_to_all.17.own_ref), channel_id=1, source_target_pairs={{0,1},{1,0},{2,3},{3,2},{4,5},{5,4},{6,7},{7,6},{8,9},{9,8},{10,11... | collective-permute-start | bytes 786440 | tf_op jit(solution)/shard_map/ppermute | solution.py:690

commit v6 on v5

--- a/solution.py
+++ b/solution.py
@@ -473,6 +473,10 @@
     extra[...] = bias
 
 
+def final_kernel(final_ref, out_ref):
+    out_ref[...] = final_ref[...]
+
+
 def hidden_kernel(cross, in_chip, w_in, b_in, cross_hidden, in_chip_hidden):
     for source, ref in ((cross, cross_hidden), (in_chip, in_chip_hidden)):
         ref[...] = jnp.tanh(mm3(pair(w_in), split(source[...])) + wide(b_in))
@@ -672,6 +676,7 @@
         name="beside", micros=1.4,
     )
     beside_hidden = call(hidden_kernel, [SQUARE] * 2, *beside, w_in2, b_in2, name="hidden", micros=0.6)
+    (final,) = call(final_kernel, [SQUARE], final, name="final", micros=0.4)
     keep, give = call(
         back_kernel,
         [PACKED] * 2,

time: 88.2 us -> 87.7 us (level)
  waiting for transfers between devices: 2.7 us -> 1.72 us
    pallas_call x12 -> x13, Pallas kernels: 15.9 us -> 16 us  [call(): pl.pallas_call(body, out_shape=[jax.ShapeDtypeStruct(s, t) for s, t in ou...]
where the time goes in v6:
time: 87.7 us; the launch traced here: 87.4 us
  blocking collectives  36.6 us (42%)
  starting transfers between devices  30.2 us (34%)
  Pallas kernels  16 us (18%)
  local copies, waits for them, and re-layouts  2.04 us (2%)
  waiting for transfers between devices  1.72 us (2%)
    ppermute x4, starting transfers between devices, exchange(): lax.ppermute(in_chip, AXES, IN_CHIP)  21.2 us
    pallas_call x13, Pallas kernels, call(): pl.pallas_call(body, out_shape=[jax.ShapeDtypeStruct(s, t) for s, t in ou...  16 us
    all_to_all x1, blocking collectives, local(): parts = lax.all_to_all(parts, 'z', 0, 0, tiled=True)  14.2 us
    all_to_all x1, blocking collectives, local(): parts = lax.all_to_all(parts, PLANE, 0, 0, tiled=True)  11.2 us
    all_to_all x1, blocking collectives, local(): own = lax.all_to_all(parts, PLANE, 0, 0, tiled=True)  11.2 us
    ppermute x4, starting transfers between devices, exchange(): lax.ppermute(cross, AXES, CROSS)  4.57 us
    ppermute x1, starting transfers between devices, local(): other = lax.ppermute(own, 'core', swap)  4.01 us
    unnamed x18, local copies, waits for them, and re-layouts  2.04 us
  transfers between devices with their start and end apart: 10, of which 2 were waited for; matrix products, arithmetic and copies ran while one was open for 0% of the time, Pallas kernels for 8%

profile of v6, /device:TPU:1, one launch (start us, length us, event | category | flops | bytes accessed | tf_op | source)
XLA Modules:
  0.0 87.4 jit_solution(8187203400957240287)
XLA Ops:
  0.6 0.0 copy-start.2
  0.6 0.0 copy-start.4
  0.7 0.7 copy-done.2
  1.3 0.0 copy-done.4
  1.3 0.0 copy-start.3
  1.3 0.7 copy-done.3
  2.0 0.0 copy-start
  2.0 0.0 copy-start.6
  2.0 0.0 copy-start.7
  2.0 2.1 %first.1 = (bf16[2,64,256]{2,1,0:T(8,128)(2,1)S(1)}, f32[256,256]{1,0:T(8,128)S(1)}, f32[40,256]{1,0:T(8,128)S(1)}, f32[40,256]{1,0:T(8,128)S(1)}, bf16[2,256,25...) custom-call(s32[1]{0:T(128)} %bitcast.parity_ref, f32[256,256]{1,0:T(8,128)} %state_far.1, f32[256,256]{1,0:T(8,128)} %w_in_far.1, ...), custom_call_target="tpu_custom_call" | custom-call | flops 1724999936 | bytes 1000000 | tf_op jit(solution)/shard_map/first/pallas_call | solution.py:108
  4.2 3.1 %collective-permute-start = (f32[40,256]{1,0:T(8,128)S(1)}, f32[40,256]{1,0:T(8,128)S(1)}, u32[]{:S(2)}, u32[]{:S(2)}) collective-permute-start(f32[40,256]{1,0:T(8,128)S(1)} %get-tuple-element.79), channel_id=1, source_target_pairs={{0,255},{1,2},{2,1},{3,4},{4,3},{5,6},{6,5},{7,8},{8,7},{9,10},{10... | collective-permute-start | bytes 122888 | tf_op jit(solution)/shard_map/ppermute | solution.py:607
  7.3 8.4 %collective-permute-start.1 = (f32[40,256]{1,0:T(8,128)S(1)}, f32[40,256]{1,0:T(8,128)S(1)}, u32[]{:S(2)}, u32[]{:S(2)}) collective-permute-start(f32[40,256]{1,0:T(8,128)S(1)} %get-tuple-element.77.after_ref), channel_id=1, source_target_pairs={{0,1},{1,0},{2,3},{3,2},{4,5},{5,4},{6,7},{7,6},{8,9},{9,8},{10,11... | collective-permute-start | bytes 122888 | tf_op jit(solution)/shard_map/ppermute | solution.py:607
  15.7 0.0 copy-done
  15.7 0.0 copy-done.6
  15.7 0.0 copy-done.7
  15.7 0.0 copy-done.8
  15.7 0.7 copy-done.5
  16.4 1.5 %tables.1 = (f32[256,256]{1,0:T(8,128)S(1)}, f32[256,256]{1,0:T(8,128)S(1)}, f32[256,256]{1,0:T(8,128)S(1)}, f32[64,256]{1,0:T(8,128)S(1)}, bf16[2,256,256]{2,1,...) custom-call(bf16[2,256,256]{2,1,0:T(8,128)(2,1)S(1)} %get-tuple-elem, ...), custom_call_target="tpu_custom_call" | custom-call | flops 1724999936 | bytes 1000000 | tf_op jit(solution)/shard_map/tables/pallas_call | solution.py:108
  17.9 0.0 collective-permute-done.cross
  17.9 0.0 collective-permute-done.1.in_chip
  17.9 2.0 %middle.1 = (f32[256,256]{1,0:T(8,128)S(1)}, f32[256,256]{1,0:T(8,128)S(1)}, f32[256,256]{1,0:T(8,128)S(1)}, f32[256,256]{1,0:T(8,128)S(1)}, bf16[2,64,256]{2,1,...) custom-call(s32[1]{0:T(128)} %bitcast.parity_ref, ...), custom_call_target="tpu_custom_call" | custom-call | flops 2415000064 | bytes 1000000 | tf_op jit(solution)/shard_map/middle/pallas_call | solution.py:108
  20.0 0.1 collective-permute-start.2
  20.1 6.6 %collective-permute-start.3 = (f32[32,256]{1,0:T(8,128)S(1)}, f32[32,256]{1,0:T(8,128)S(1)}, u32[]{:S(2)}, u32[]{:S(2)}) collective-permute-start(f32[32,256]{1,0:T(8,128)S(1)} %get-tuple-element.97), channel_id=1, source_target_pairs={{0,1},{1,0},{2,3},{3,2},{4,5},{5,4},{6,7},{7,6},{8,9},{9,8},{10,11... | collective-permute-start | bytes 98312 | tf_op jit(solution)/shard_map/ppermute | solution.py:607
  26.7 1.3 %rest.1 = (f32[256,256]{1,0:T(8,128)S(1)}, f32[256,256]{1,0:T(8,128)S(1)}, f32[256,256]{1,0:T(8,128)S(1)}, f32[64,256]{1,0:T(8,128)S(1)}, f32[256,256]{1,0:T(8,128)S(1)}) custom-call(f32[256,256]{1,0:T(8,128)S(1)} %get-tuple-element.92.third_ref, f32[256,256]{1,0:T(8,128)S(1)} %get-tuple-element.93.hidden_ref.hidden_third, ...), custom_call_target="tpu_custom_call" | custom-call | flops 1035000000 | bytes 1000000 | tf_op jit(solution)/shard_map/rest/pallas_call | solution.py:108
  27.9 0.1 collective-permute-start.6
  28.0 0.6 collective-permute-start.7
  28.6 0.0 collective-permute-done.2.cross
  28.6 0.0 collective-permute-done.3.in_chip
  28.6 0.0 copy-done.1
  28.6 1.8 %turn.1 = (f32[256,256]{1,0:T(8,128)S(1)}, f32[8,128]{1,0:T(8,128)S(1)}, f32[256,256]{1,0:T(8,128)S(1)}, f32[256,256]{1,0:T(8,128)S(1)}, f32[256,256]{1,0:T(8,12...) custom-call(s32[1]{0:T(128)} %bitcast.parity_ref, ...), custom_call_target="tpu_custom_call" | custom-call | flops 2875000064 | bytes 1000000 | tf_op jit(solution)/shard_map/turn/pallas_call | solution.py:108
  30.4 1.3 %collective-permute-start.4 = (f32[32,256]{1,0:T(8,128)S(1)}, f32[32,256]{1,0:T(8,128)S(1)}, u32[]{:S(2)}, u32[]{:S(2)}) collective-permute-start(f32[32,256]{1,0:T(8,128)S(1)} %get-tuple-element.113), channel_id=1, source_target_pairs={{0,255},{1,2},{2,1},{3,4},{4,3},{5,6},{6,5},{7,8},{8,7},{9,10},{10... | collective-permute-start | bytes 98312 | tf_op jit(solution)/shard_map/ppermute | solution.py:607
  31.7 5.6 %collective-permute-start.5 = (f32[32,256]{1,0:T(8,128)S(1)}, f32[32,256]{1,0:T(8,128)S(1)}, u32[]{:S(2)}, u32[]{:S(2)}) collective-permute-start(f32[32,256]{1,0:T(8,128)S(1)} %get-tuple-element.114), channel_id=1, source_target_pairs={{0,1},{1,0},{2,3},{3,2},{4,5},{5,4},{6,7},{7,6},{8,9},{9,8},{10,11... | collective-permute-start | bytes 98312 | tf_op jit(solution)/shard_map/ppermute | solution.py:607
  37.3 1.6 %beside.1 = (f32[256,256]{1,0:T(8,128)S(1)}, f32[256,256]{1,0:T(8,128)S(1)}, f32[256,256]{1,0:T(8,128)S(1)}, f32[8,128]{1,0:T(8,128)S(1)}, f32[256,256]{1,0:T(8,...) custom-call(f32[256,256]{1,0:T(8,128)S(1)} %get-tuple-element.107.adjoint_ref, ...), custom_call_target="tpu_custom_call" | custom-call | flops 1610000000 | bytes 1000000 | tf_op jit(solution)/shard_map/beside/pallas_call | solution.py:108
  38.9 0.0 collective-permute-done.6.cross.cross_state
  38.9 0.0 collective-permute-done.7.in_chip.in_chip_state
  38.9 0.4 hidden.1
  39.3 0.0 collective-permute-done.4.cross
  39.3 0.0 collective-permute-done.5.in_chip
  39.3 3.4 %back.1 = (f32[16,40,128]{2,1,0:T(8,128)S(1)}, f32[16,40,128]{2,1,0:T(8,128)S(1)}) custom-call(s32[1]{0:T(128)} %bitcast.parity_ref, f32[256,256]{1,0:T(8,128)S(1)} %get-tuple-element.112.base_ref, f32[256,256]{1,0:T(8,128)S(1)} %get-tuple-element.107.adjoint_ref, f32[32,256]{1,0:T(8,128)S(1)} %collective-permute-done.4.cross, ...), custom_call_target="tpu_custom_call" | custom-call | flops 4600000000 | bytes 1000000 | tf_op jit(solution)/shard_map/back/pallas_call | solution.py:108
  42.7 0.5 collective-permute-start.8
  43.2 1.3 %collective-permute-done.8.got_ref = f32[16,40,128]{2,1,0:T(8,128)S(1)} collective-permute-done((f32[16,40,128]{2,1,0:T(8,128)S(1)}, f32[16,40,128]{2,1,0:T(8,128)S(1)}, u32[]{:S(2)}, u32[]{:S(2)}) %collective-permute-start.8) | collective-permute-done | bytes 327712 | tf_op jit(solution)/shard_map/ppermute | solution.py:689
  44.5 11.2 %all_to_all.15.parts_ref = f32[16,40,128]{2,1,0:T(8,128)S(1)} all-to-all(f32[16,40,128]{2,1,0:T(8,128)S(1)} %chip_sum.1), channel_id=1, replica_groups=mesh['x'=4,'y'=4,'z'=8,'core'=2] {'x','y'}, dimensions={0} | all-to-all | bytes 655360 | tf_op jit(solution)/shard_map/all_to_all | solution.py:690
  55.7 14.2 %all_to_all.16.parts_ref = f32[8,40,128]{2,1,0:T(8,128)S(1)} all-to-all(f32[8,40,128]{2,1,0:T(8,128)S(1)} %plane_sum.1), channel_id=1, replica_groups=mesh['x'=4,'y'=4,'z'=8,'core'=2] {'z'}, dimensions={0} | all-to-all | bytes 327680 | tf_op jit(solution)/shard_map/all_to_all | solution.py:692
  70.0 11.2 %all_to_all.17.own_ref = f32[16,32,128]{2,1,0:T(8,128)S(1)} all-to-all(f32[16,32,128]{2,1,0:T(8,128)S(1)} %get-tuple-element.133), channel_id=1, replica_groups=mesh['x'=4,'y'=4,'z'=8,'core'=2] {'x','y'}, dimensions={0} | all-to-all | bytes 524288 | tf_op jit(solution)/shard_map/all_to_all | solution.py:694
  81.2 4.0 %collective-permute-start.9 = (f32[16,32,128]{2,1,0:T(8,128)S(1)}, f32[16,32,128]{2,1,0:T(8,128)S(1)}, u32[]{:S(2)}, u32[]{:S(2)}) collective-permute-start(f32[16,32,128]{2,1,0:T(8,128)S(1)} %all_to_all.17.own_ref), channel_id=1, source_target_pairs={{0,1},{1,0},{2,3},{3,2},{4,5},{5,4},{6,7},{7,6},{8,9},{9,8},{10,11... | collective-permute-start | bytes 786440 | tf_op jit(solution)/shard_map/ppermute | solution.py:695
  85.2 0.7 final.1
  85.9 0.4 collective-permute-done.9.other_ref
  86.4 1.0 %scale.1 = (f32[256,256]{1,0:T(8,128)}, f32[1,256]{1,0:T(1,128)}, f32[256,256]{1,0:T(8,128)}, f32[1,256]{1,0:T(1,128)}, f32[1,1]{1,0:T(1,128)}) custom-call(s32[1]{0:T(128)} %bitcast.parity_ref, f32[16,32,128]{2,1,0:T(8,128)S(1)} %all_to_all.17.own_ref, f32[16,32,128]{2,1,0:T(8,128)S(1)} %collective-permute-done.9.other_ref, ...), custom_call_target="tpu_custom_call" | custom-call | flops 1150000000 | bytes 1000000 | tf_op jit(solution)/shard_map/scale/pallas_call | solution.py:108
  (6 shorter events, 0.1 us)
Async XLA Ops:
  0.6 0.7 copy-start.2
  0.6 0.7 copy-start.4
  1.3 0.7 copy-start.3
  2.0 13.7 %copy-start = (f32[256,256]{1,0:T(8,128)S(1)}, f32[256,256]{1,0:T(8,128)}, u32[]{:S(2)}) copy-start(f32[256,256]{1,0:T(8,128)} %w_out_ref.1) | copy-start | bytes 786436
  2.0 13.7 %copy-start.6 = (bf16[512,256]{1,0:T(8,128)(2,1)S(1)}, bf16[512,256]{1,0:T(8,128)(2,1)}, u32[]{:S(2)}) copy-start(bf16[512,256]{1,0:T(8,128)(2,1)} %constant.13.clone.inner) | copy-start | bytes 786436
  2.0 13.7 %copy-start.7 = (bf16[64,256]{1,0:T(8,128)(2,1)S(1)}, bf16[64,256]{1,0:T(8,128)(2,1)}, u32[]{:S(2)}) copy-start(bf16[64,256]{1,0:T(8,128)(2,1)} %constant.15.clone.lift_t) | copy-start | bytes 98308
  2.0 13.7 %copy-start.8 = (bf16[64,256]{1,0:T(8,128)(2,1)S(1)}, bf16[64,256]{1,0:T(8,128)(2,1)}, u32[]{:S(2)}) copy-start(bf16[64,256]{1,0:T(8,128)(2,1)} %constant.14.clone.leave) | copy-start | bytes 98308
  4.2 13.8 %collective-permute-start = (f32[40,256]{1,0:T(8,128)S(1)}, f32[40,256]{1,0:T(8,128)S(1)}, u32[]{:S(2)}, u32[]{:S(2)}) collective-permute-start(f32[40,256]{1,0:T(8,128)S(1)} %get-tuple-element.79), channel_id=1, source_target_pairs={{0,255},{1,2},{2,1},{3,4},{4,3},{5,6},{6,5},{7,8},{8,7},{9,10},{10... | collective-permute-start | bytes 122888 | tf_op jit(solution)/shard_map/ppermute | solution.py:607
  7.3 10.7 %collective-permute-start.1 = (f32[40,256]{1,0:T(8,128)S(1)}, f32[40,256]{1,0:T(8,128)S(1)}, u32[]{:S(2)}, u32[]{:S(2)}) collective-permute-start(f32[40,256]{1,0:T(8,128)S(1)} %get-tuple-element.77.after_ref), channel_id=1, source_target_pairs={{0,1},{1,0},{2,3},{3,2},{4,5},{5,4},{6,7},{7,6},{8,9},{9,8},{10,11... | collective-permute-start | bytes 122888 | tf_op jit(solution)/shard_map/ppermute | solution.py:607
  15.7 0.7 copy-start.5
  20.0 8.6 %collective-permute-start.2 = (f32[32,256]{1,0:T(8,128)S(1)}, f32[32,256]{1,0:T(8,128)S(1)}, u32[]{:S(2)}, u32[]{:S(2)}) collective-permute-start(f32[32,256]{1,0:T(8,128)S(1)} %get-tuple-element.96), channel_id=1, source_target_pairs={{0,255},{1,2},{2,1},{3,4},{4,3},{5,6},{6,5},{7,8},{8,7},{9,10},{10... | collective-permute-start | bytes 98312 | tf_op jit(solution)/shard_map/ppermute | solution.py:607
  20.1 8.5 %collective-permute-start.3 = (f32[32,256]{1,0:T(8,128)S(1)}, f32[32,256]{1,0:T(8,128)S(1)}, u32[]{:S(2)}, u32[]{:S(2)}) collective-permute-start(f32[32,256]{1,0:T(8,128)S(1)} %get-tuple-element.97), channel_id=1, source_target_pairs={{0,1},{1,0},{2,3},{3,2},{4,5},{5,4},{6,7},{7,6},{8,9},{9,8},{10,11... | collective-permute-start | bytes 98312 | tf_op jit(solution)/shard_map/ppermute | solution.py:607
  26.7 2.0 %copy-start.1 = (f32[256,256]{1,0:T(8,128)S(1)}, f32[256,256]{1,0:T(8,128)}, u32[]{:S(2)}) copy-start(f32[256,256]{1,0:T(8,128)} %target_ref.1) | copy-start | bytes 786436
  27.9 10.9 %collective-permute-start.6 = (f32[256,256]{1,0:T(8,128)S(1)}, f32[256,256]{1,0:T(8,128)S(1)}, u32[]{:S(2)}, u32[]{:S(2)}) collective-permute-start(f32[256,256]{1,0:T(8,128)S(1)} %get-tuple-element.117), channel_id=1, source_target_pairs={{0,255},{1,2},{2,1},{3,4},{4,3},{5,6},{6,5},{7,8},{8,7},{9,10},{10... | collective-permute-start | bytes 786440 | tf_op jit(solution)/shard_map/ppermute | solution.py:607
  28.0 10.8 %collective-permute-start.7 = (f32[256,256]{1,0:T(8,128)S(1)}, f32[256,256]{1,0:T(8,128)S(1)}, u32[]{:S(2)}, u32[]{:S(2)}) collective-permute-start(f32[256,256]{1,0:T(8,128)S(1)} %get-tuple-element.117), channel_id=1, source_target_pairs={{0,1},{1,0},{2,3},{3,2},{4,5},{5,4},{6,7},{7,6},{8,9},{9,8},{10,11... | collective-permute-start | bytes 786440 | tf_op jit(solution)/shard_map/ppermute | solution.py:607
  30.4 8.9 %collective-permute-start.4 = (f32[32,256]{1,0:T(8,128)S(1)}, f32[32,256]{1,0:T(8,128)S(1)}, u32[]{:S(2)}, u32[]{:S(2)}) collective-permute-start(f32[32,256]{1,0:T(8,128)S(1)} %get-tuple-element.113), channel_id=1, source_target_pairs={{0,255},{1,2},{2,1},{3,4},{4,3},{5,6},{6,5},{7,8},{8,7},{9,10},{10... | collective-permute-start | bytes 98312 | tf_op jit(solution)/shard_map/ppermute | solution.py:607
  31.7 7.6 %collective-permute-start.5 = (f32[32,256]{1,0:T(8,128)S(1)}, f32[32,256]{1,0:T(8,128)S(1)}, u32[]{:S(2)}, u32[]{:S(2)}) collective-permute-start(f32[32,256]{1,0:T(8,128)S(1)} %get-tuple-element.114), channel_id=1, source_target_pairs={{0,1},{1,0},{2,3},{3,2},{4,5},{5,4},{6,7},{7,6},{8,9},{9,8},{10,11... | collective-permute-start | bytes 98312 | tf_op jit(solution)/shard_map/ppermute | solution.py:607
  42.7 1.7 %collective-permute-start.8 = (f32[16,40,128]{2,1,0:T(8,128)S(1)}, f32[16,40,128]{2,1,0:T(8,128)S(1)}, u32[]{:S(2)}, u32[]{:S(2)}) collective-permute-start(f32[16,40,128]{2,1,0:T(8,128)S(1)} %get-tuple-element.132), channel_id=1, source_target_pairs={{0,1},{1,0},{2,3},{3,2},{4,5},{5,4},{6,7},{7,6},{8,9},{9,8},{10,11... | collective-permute-start | bytes 983048 | tf_op jit(solution)/shard_map/ppermute | solution.py:689
  81.2 5.2 %collective-permute-start.9 = (f32[16,32,128]{2,1,0:T(8,128)S(1)}, f32[16,32,128]{2,1,0:T(8,128)S(1)}, u32[]{:S(2)}, u32[]{:S(2)}) collective-permute-start(f32[16,32,128]{2,1,0:T(8,128)S(1)} %all_to_all.17.own_ref), channel_id=1, source_target_pairs={{0,1},{1,0},{2,3},{3,2},{4,5},{5,4},{6,7},{7,6},{8,9},{9,8},{10,11... | collective-permute-start | bytes 786440 | tf_op jit(solution)/shard_map/ppermute | solution.py:695

commit v7 on v6

--- a/solution.py
+++ b/solution.py
@@ -168,38 +168,43 @@
         near[face - 2] = one_hot(rows, index_ref[face : face + 1] - 256 * (face ^ 1))
 
 
-def first_kernel(
-    parity_ref, state_far, w_in_far, fixed_far, w_out_far, nbr_far, send_far, b_in_far,
-    arrived_ref, hidden_ref, in_chip_ref, cross_ref, w_in, state_ref,
-    w_in_ref, w_out_ref, fixed, near, nbr_ref, send_ref, b_in, sems,
+def load_kernel(
+    state_far, w_in_far, fixed_far, w_out_far, total_ref, linear_ref, out_ref, w_out, lift, w_in, state_ref,
+    w_in_ref, w_out_ref, fixed, sems,
 ):
     pairs = (
         (state_far, state_ref), (w_in_far, w_in_ref), (fixed_far.at[0:256], fixed), (w_out_far.at[0:16], w_out_ref.at[0:16]),
         (w_out_far.at[48:80], w_out_ref.at[16:48]), (w_out_far.at[112:128], w_out_ref.at[48:64]),
-        (nbr_far, nbr_ref), (send_far, send_ref), (b_in_far, b_in),
     )
     copies = [pltpu.make_async_copy(s, t, sems.at[n]) for n, (s, t) in enumerate(pairs)]
     for copy in copies:
         copy.start()
     copies[0].wait()
-    values = state_ref[...]
-    edge = edge_rows(values)
-    parts = split(values)
+    parts = split(state_ref[...])
+    copies[1].wait()
+    w_in[0], w_in[1] = split(w_in_ref[...])
+    total_ref[...] = mm3(pair(w_in), parts)
+    for copy in copies[2:]:
+        copy.wait()
+    out_ref[...] = mm(fixed[128:192], parts[0]) + mm(fixed[128:192], parts[1])
+    linear_ref[...] = mm3((fixed[0:64], fixed[64:128]), parts)
+    w_out[0], w_out[1] = split(w_out_ref[...])
+    lift[...] = fixed[192:256, 0:64]
+
+
+def first_kernel(
+    parity_ref, state_ref, total_ref, linear_ref, out_ref, w_out, lift, nbr_ref, send_ref, b_in,
+    arrived_ref, hidden_ref, in_chip_ref, cross_ref, near,
+):
+    edge = edge_rows(state_ref)
     parity = parity_ref[0]
     put(parity, *leaving(edge), in_chip_ref, cross_ref)
-    copies[1].wait()
-    w_in[0], w_in[1] = split(w_in_ref[...])
-    copies[8].wait()
-    bias = wide(b_in)
-    hidden = jnp.tanh(mm3(pair(w_in), parts) + bias)
+    hidden = jnp.tanh(total_ref[...] + wide(b_in))
     hidden_ref[...] = hidden
-    for copy in copies[2:8]:
-        copy.wait()
     make_near(nbr_ref, near)
-    arrive_near(mm(fixed[128:192], parts[0]) + mm(fixed[128:192], parts[1]), near, arrived_ref)
-    rates = mm3((fixed[0:64], fixed[64:128]), parts) + mm3(split(w_out_ref[...]), split(hidden))
-    lift = fixed[192:256, 0:64]
-    rates += mm(lift, arrived_ref[0]) + mm(lift, arrived_ref[1])
+    arrive_near(out_ref[...], near, arrived_ref)
+    rates = linear_ref[...] + mm3(pair(w_out), split(hidden))
+    rates += mm(lift[...], arrived_ref[0]) + mm(lift[...], arrived_ref[1])
     put(parity, *leaving(edge + TIME_STEP * rates), in_chip_ref, cross_ref, 16)
     down_index = send_ref[0:1].astype(F32)
     up_index = (send_ref[1:2] - 256).astype(F32)
@@ -619,18 +624,24 @@
     b_in, b_out = b_in.reshape(1, 256), b_out.reshape(1, 256)
     tall, flat, thin = ((512, 256), BF16), ((64, 256), BF16), ((256, 64), BF16)
     arrival = ((2, 64, 256), BF16)
-    arrived, hidden_first, *edge, w_in2, state = call(
-        first_kernel,
-        [arrival, SQUARE, ((40, 256), F32), ((40, 256), F32), PAIR, SQUARE],
-        parity, state, w_in, fixed, w_out, nbr, send, b_in,
-        name="first", micros=1.5,
-        far=range(1, 8),
-        limit=53,
+    strip = ((64, 256), F32)
+    *loaded, w_in2, state = call(
+        load_kernel,
+        [SQUARE, strip, strip, ((2, 64, 256), BF16), ((64, 64), BF16), PAIR, SQUARE],
+        state, w_in, fixed, w_out,
+        name="load", micros=1.3,
+        far=range(4),
+        limit=52.9,
         scratch=[
             pltpu.VMEM((256, 256), F32), pltpu.VMEM((64, 256), F32), pltpu.VMEM((256, 256), BF16),
-            pltpu.VMEM((4, 256, 256), BF16), pltpu.VMEM((6, 256), jnp.int32), pltpu.VMEM((2, 256), jnp.int32),
-            pltpu.VMEM((1, 256), F32), pltpu.SemaphoreType.DMA((9,)),
+            pltpu.SemaphoreType.DMA((6,)),
         ],
+    )
+    arrived, hidden_first, *edge = call(
+        first_kernel,
+        [arrival, SQUARE, ((40, 256), F32), ((40, 256), F32)],
+        parity, state, *loaded, nbr, send, b_in,
+        name="first", micros=0.8, scratch=[pltpu.VMEM((4, 256, 256), BF16)],
     )
     got = exchange(*edge)
     middle = [SQUARE, SQUARE, ((64, 256), F32)]

time: 87.7 us -> 87 us (level)
    pallas_call x13 -> x14, Pallas kernels: 16 us -> 16 us  [call(): pl.pallas_call(body, out_shape=[jax.ShapeDtypeStruct(s, t) for s, t in ou...]
where the time goes in v7:
time: 87 us; the launch traced here: 86.8 us
  blocking collectives  36.6 us (42%)
  starting transfers between devices  30.2 us (35%)
  Pallas kernels  16 us (18%)
  waiting for transfers between devices  1.72 us (2%)
  local copies, waits for them, and re-layouts  1.37 us (2%)
    ppermute x4, starting transfers between devices, exchange(): lax.ppermute(in_chip, AXES, IN_CHIP)  21.2 us
    pallas_call x14, Pallas kernels, call(): pl.pallas_call(body, out_shape=[jax.ShapeDtypeStruct(s, t) for s, t in ou...  16 us
    all_to_all x1, blocking collectives, local(): parts = lax.all_to_all(parts, 'z', 0, 0, tiled=True)  14.2 us
    all_to_all x1, blocking collectives, local(): parts = lax.all_to_all(parts, PLANE, 0, 0, tiled=True)  11.2 us
    all_to_all x1, blocking collectives, local(): own = lax.all_to_all(parts, PLANE, 0, 0, tiled=True)  11.2 us
    ppermute x4, starting transfers between devices, exchange(): lax.ppermute(cross, AXES, CROSS)  4.56 us
    ppermute x1, starting transfers between devices, local(): other = lax.ppermute(own, 'core', swap)  4.01 us
  transfers between devices with their start and end apart: 10, of which 2 were waited for; matrix products, arithmetic and copies ran while one was open for 0% of the time, Pallas kernels for 8%

profile of v7, /device:TPU:1, one launch (start us, length us, event | category | flops | bytes accessed | tf_op | source)
XLA Modules:
  0.0 86.8 jit_solution(13082113680947331405)
XLA Ops:
  0.6 1.7 %load.1 = (f32[256,256]{1,0:T(8,128)S(1)}, f32[64,256]{1,0:T(8,128)S(1)}, f32[64,256]{1,0:T(8,128)S(1)}, bf16[2,64,256]{2,1,0:T(8,128)(2,1)S(1)}, bf16[64,64]{1,...) custom-call(f32[256,256]{1,0:T(8,128)} %state_far.1, f32[256,256]{1,0:T(8,128)} %w_in_far.1, ...), custom_call_target="tpu_custom_call" | custom-call | flops 1495000064 | bytes 1000000 | tf_op jit(solution)/shard_map/load/pallas_call | solution.py:108
  2.4 0.0 copy-start.2
  2.4 0.0 copy-start.3
  2.4 0.0 copy-start.4
  2.4 0.7 copy-done.2
  3.1 0.0 copy-done.3
  3.1 0.0 copy-done.4
  3.1 0.0 copy-start.7
  3.1 0.0 copy-start.8
  3.1 0.4 first.1
  3.5 3.1 %collective-permute-start = (f32[40,256]{1,0:T(8,128)S(1)}, f32[40,256]{1,0:T(8,128)S(1)}, u32[]{:S(2)}, u32[]{:S(2)}) collective-permute-start(f32[40,256]{1,0:T(8,128)S(1)} %get-tuple-element.89), channel_id=1, source_target_pairs={{0,255},{1,2},{2,1},{3,4},{4,3},{5,6},{6,5},{7,8},{8,7},{9,10},{10... | collective-permute-start | bytes 122888 | tf_op jit(solution)/shard_map/ppermute | solution.py:612
  6.7 8.4 %collective-permute-start.1 = (f32[40,256]{1,0:T(8,128)S(1)}, f32[40,256]{1,0:T(8,128)S(1)}, u32[]{:S(2)}, u32[]{:S(2)}) collective-permute-start(f32[40,256]{1,0:T(8,128)S(1)} %get-tuple-element.87.after_ref), channel_id=1, source_target_pairs={{0,1},{1,0},{2,3},{3,2},{4,5},{5,4},{6,7},{7,6},{8,9},{9,8},{10,11... | collective-permute-start | bytes 122888 | tf_op jit(solution)/shard_map/ppermute | solution.py:612
  15.1 0.0 copy-done
  15.1 0.0 copy-done.6
  15.1 0.0 copy-done.7
  15.1 0.0 copy-done.8
  15.1 0.7 copy-done.5
  15.7 1.5 %tables.1 = (f32[256,256]{1,0:T(8,128)S(1)}, f32[256,256]{1,0:T(8,128)S(1)}, f32[256,256]{1,0:T(8,128)S(1)}, f32[64,256]{1,0:T(8,128)S(1)}, bf16[2,256,256]{2,1,...) custom-call(bf16[2,256,256]{2,1,0:T(8,128)(2,1)S(1)} %get-tuple-elem, ...), custom_call_target="tpu_custom_call" | custom-call | flops 1724999936 | bytes 1000000 | tf_op jit(solution)/shard_map/tables/pallas_call | solution.py:108
  17.3 0.0 collective-permute-done.cross
  17.3 0.0 collective-permute-done.1.in_chip
  17.3 2.0 %middle.1 = (f32[256,256]{1,0:T(8,128)S(1)}, f32[256,256]{1,0:T(8,128)S(1)}, f32[256,256]{1,0:T(8,128)S(1)}, f32[256,256]{1,0:T(8,128)S(1)}, bf16[2,64,256]{2,1,...) custom-call(s32[1]{0:T(128)} %bitcast.parity_ref, ...), custom_call_target="tpu_custom_call" | custom-call | flops 2415000064 | bytes 1000000 | tf_op jit(solution)/shard_map/middle/pallas_call | solution.py:108
  19.3 0.1 collective-permute-start.2
  19.4 6.6 %collective-permute-start.3 = (f32[32,256]{1,0:T(8,128)S(1)}, f32[32,256]{1,0:T(8,128)S(1)}, u32[]{:S(2)}, u32[]{:S(2)}) collective-permute-start(f32[32,256]{1,0:T(8,128)S(1)} %get-tuple-element.107), channel_id=1, source_target_pairs={{0,1},{1,0},{2,3},{3,2},{4,5},{5,4},{6,7},{7,6},{8,9},{9,8},{10,11... | collective-permute-start | bytes 98312 | tf_op jit(solution)/shard_map/ppermute | solution.py:612
  26.0 1.3 %rest.1 = (f32[256,256]{1,0:T(8,128)S(1)}, f32[256,256]{1,0:T(8,128)S(1)}, f32[256,256]{1,0:T(8,128)S(1)}, f32[64,256]{1,0:T(8,128)S(1)}, f32[256,256]{1,0:T(8,128)S(1)}) custom-call(f32[256,256]{1,0:T(8,128)S(1)} %get-tuple-element.102.third_ref, f32[256,256]{1,0:T(8,128)S(1)} %get-tuple-element.103.hidden_ref.hidden_third, ...), custom_call_target="tpu_custom_call" | custom-call | flops 1035000000 | bytes 1000000 | tf_op jit(solution)/shard_map/rest/pallas_call | solution.py:108
  27.3 0.1 collective-permute-start.6
  27.4 0.6 collective-permute-start.7
  28.0 0.0 collective-permute-done.2.cross
  28.0 0.0 collective-permute-done.3.in_chip
  28.0 0.0 copy-done.1
  28.0 1.8 %turn.1 = (f32[256,256]{1,0:T(8,128)S(1)}, f32[8,128]{1,0:T(8,128)S(1)}, f32[256,256]{1,0:T(8,128)S(1)}, f32[256,256]{1,0:T(8,128)S(1)}, f32[256,256]{1,0:T(8,12...) custom-call(s32[1]{0:T(128)} %bitcast.parity_ref, ...), custom_call_target="tpu_custom_call" | custom-call | flops 2875000064 | bytes 1000000 | tf_op jit(solution)/shard_map/turn/pallas_call | solution.py:108
  29.8 1.3 %collective-permute-start.4 = (f32[32,256]{1,0:T(8,128)S(1)}, f32[32,256]{1,0:T(8,128)S(1)}, u32[]{:S(2)}, u32[]{:S(2)}) collective-permute-start(f32[32,256]{1,0:T(8,128)S(1)} %get-tuple-element.123), channel_id=1, source_target_pairs={{0,255},{1,2},{2,1},{3,4},{4,3},{5,6},{6,5},{7,8},{8,7},{9,10},{10... | collective-permute-start | bytes 98312 | tf_op jit(solution)/shard_map/ppermute | solution.py:612
  31.1 5.6 %collective-permute-start.5 = (f32[32,256]{1,0:T(8,128)S(1)}, f32[32,256]{1,0:T(8,128)S(1)}, u32[]{:S(2)}, u32[]{:S(2)}) collective-permute-start(f32[32,256]{1,0:T(8,128)S(1)} %get-tuple-element.124), channel_id=1, source_target_pairs={{0,1},{1,0},{2,3},{3,2},{4,5},{5,4},{6,7},{7,6},{8,9},{9,8},{10,11... | collective-permute-start | bytes 98312 | tf_op jit(solution)/shard_map/ppermute | solution.py:612
  36.7 1.6 %beside.1 = (f32[256,256]{1,0:T(8,128)S(1)}, f32[256,256]{1,0:T(8,128)S(1)}, f32[256,256]{1,0:T(8,128)S(1)}, f32[8,128]{1,0:T(8,128)S(1)}, f32[256,256]{1,0:T(8,...) custom-call(f32[256,256]{1,0:T(8,128)S(1)} %get-tuple-element.117.adjoint_ref, ...), custom_call_target="tpu_custom_call" | custom-call | flops 1610000000 | bytes 1000000 | tf_op jit(solution)/shard_map/beside/pallas_call | solution.py:108
  38.2 0.0 collective-permute-done.6.cross.cross_state
  38.3 0.0 collective-permute-done.7.in_chip.in_chip_state
  38.3 0.4 hidden.1
  38.7 0.0 collective-permute-done.4.cross
  38.7 0.0 collective-permute-done.5.in_chip
  38.7 3.4 %back.1 = (f32[16,40,128]{2,1,0:T(8,128)S(1)}, f32[16,40,128]{2,1,0:T(8,128)S(1)}) custom-call(s32[1]{0:T(128)} %bitcast.parity_ref, f32[256,256]{1,0:T(8,128)S(1)} %get-tuple-element.122.base_ref, f32[256,256]{1,0:T(8,128)S(1)} %get-tuple-element.117.adjoint_ref, f32[32,256]{1,0:T(8,128)S(1)} %collective-permute-done.4.cross, ...), custom_call_target="tpu_custom_call" | custom-call | flops 4600000000 | bytes 1000000 | tf_op jit(solution)/shard_map/back/pallas_call | solution.py:108
  42.1 0.5 collective-permute-start.8
  42.5 1.3 %collective-permute-done.8.got_ref = f32[16,40,128]{2,1,0:T(8,128)S(1)} collective-permute-done((f32[16,40,128]{2,1,0:T(8,128)S(1)}, f32[16,40,128]{2,1,0:T(8,128)S(1)}, u32[]{:S(2)}, u32[]{:S(2)}) %collective-permute-start.8) | collective-permute-done | bytes 327712 | tf_op jit(solution)/shard_map/ppermute | solution.py:700
  43.9 11.2 %all_to_all.15.parts_ref = f32[16,40,128]{2,1,0:T(8,128)S(1)} all-to-all(f32[16,40,128]{2,1,0:T(8,128)S(1)} %chip_sum.1), channel_id=1, replica_groups=mesh['x'=4,'y'=4,'z'=8,'core'=2] {'x','y'}, dimensions={0} | all-to-all | bytes 655360 | tf_op jit(solution)/shard_map/all_to_all | solution.py:701
  55.1 14.2 %all_to_all.16.parts_ref = f32[8,40,128]{2,1,0:T(8,128)S(1)} all-to-all(f32[8,40,128]{2,1,0:T(8,128)S(1)} %plane_sum.1), channel_id=1, replica_groups=mesh['x'=4,'y'=4,'z'=8,'core'=2] {'z'}, dimensions={0} | all-to-all | bytes 327680 | tf_op jit(solution)/shard_map/all_to_all | solution.py:703
  69.4 11.2 %all_to_all.17.own_ref = f32[16,32,128]{2,1,0:T(8,128)S(1)} all-to-all(f32[16,32,128]{2,1,0:T(8,128)S(1)} %get-tuple-element.143), channel_id=1, replica_groups=mesh['x'=4,'y'=4,'z'=8,'core'=2] {'x','y'}, dimensions={0} | all-to-all | bytes 524288 | tf_op jit(solution)/shard_map/all_to_all | solution.py:705
  80.5 4.0 %collective-permute-start.9 = (f32[16,32,128]{2,1,0:T(8,128)S(1)}, f32[16,32,128]{2,1,0:T(8,128)S(1)}, u32[]{:S(2)}, u32[]{:S(2)}) collective-permute-start(f32[16,32,128]{2,1,0:T(8,128)S(1)} %all_to_all.17.own_ref), channel_id=1, source_target_pairs={{0,1},{1,0},{2,3},{3,2},{4,5},{5,4},{6,7},{7,6},{8,9},{9,8},{10,11... | collective-permute-start | bytes 786440 | tf_op jit(solution)/shard_map/ppermute | solution.py:706
  84.6 0.7 final.1
  85.3 0.4 collective-permute-done.9.other_ref
  85.7 1.0 %scale.1 = (f32[256,256]{1,0:T(8,128)}, f32[1,256]{1,0:T(1,128)}, f32[256,256]{1,0:T(8,128)}, f32[1,256]{1,0:T(1,128)}, f32[1,1]{1,0:T(1,128)}) custom-call(s32[1]{0:T(128)} %bitcast.parity_ref, f32[16,32,128]{2,1,0:T(8,128)S(1)} %all_to_all.17.own_ref, f32[16,32,128]{2,1,0:T(8,128)S(1)} %collective-permute-done.9.other_ref, ...), custom_call_target="tpu_custom_call" | custom-call | flops 1150000000 | bytes 1000000 | tf_op jit(solution)/shard_map/scale/pallas_call | solution.py:108
  (7 shorter events, 0.1 us)
Async XLA Ops:
  2.4 0.7 copy-start.2
  2.4 0.7 copy-start.3
  2.4 0.7 copy-start.4
  3.1 12.0 %copy-start = (f32[256,256]{1,0:T(8,128)S(1)}, f32[256,256]{1,0:T(8,128)}, u32[]{:S(2)}) copy-start(f32[256,256]{1,0:T(8,128)} %w_out_ref.1) | copy-start | bytes 786436
  3.1 12.0 %copy-start.6 = (bf16[512,256]{1,0:T(8,128)(2,1)S(1)}, bf16[512,256]{1,0:T(8,128)(2,1)}, u32[]{:S(2)}) copy-start(bf16[512,256]{1,0:T(8,128)(2,1)} %constant.13.clone.inner) | copy-start | bytes 786436
  3.1 12.0 %copy-start.7 = (bf16[64,256]{1,0:T(8,128)(2,1)S(1)}, bf16[64,256]{1,0:T(8,128)(2,1)}, u32[]{:S(2)}) copy-start(bf16[64,256]{1,0:T(8,128)(2,1)} %constant.15.clone.lift_t) | copy-start | bytes 98308
  3.1 12.0 %copy-start.8 = (bf16[64,256]{1,0:T(8,128)(2,1)S(1)}, bf16[64,256]{1,0:T(8,128)(2,1)}, u32[]{:S(2)}) copy-start(bf16[64,256]{1,0:T(8,128)(2,1)} %constant.14.clone.leave) | copy-start | bytes 98308
  3.5 13.8 %collective-permute-start = (f32[40,256]{1,0:T(8,128)S(1)}, f32[40,256]{1,0:T(8,128)S(1)}, u32[]{:S(2)}, u32[]{:S(2)}) collective-permute-start(f32[40,256]{1,0:T(8,128)S(1)} %get-tuple-element.89), channel_id=1, source_target_pairs={{0,255},{1,2},{2,1},{3,4},{4,3},{5,6},{6,5},{7,8},{8,7},{9,10},{10... | collective-permute-start | bytes 122888 | tf_op jit(solution)/shard_map/ppermute | solution.py:612
  6.7 10.6 %collective-permute-start.1 = (f32[40,256]{1,0:T(8,128)S(1)}, f32[40,256]{1,0:T(8,128)S(1)}, u32[]{:S(2)}, u32[]{:S(2)}) collective-permute-start(f32[40,256]{1,0:T(8,128)S(1)} %get-tuple-element.87.after_ref), channel_id=1, source_target_pairs={{0,1},{1,0},{2,3},{3,2},{4,5},{5,4},{6,7},{7,6},{8,9},{9,8},{10,11... | collective-permute-start | bytes 122888 | tf_op jit(solution)/shard_map/ppermute | solution.py:612
  15.1 0.7 copy-start.5
  19.3 8.6 %collective-permute-start.2 = (f32[32,256]{1,0:T(8,128)S(1)}, f32[32,256]{1,0:T(8,128)S(1)}, u32[]{:S(2)}, u32[]{:S(2)}) collective-permute-start(f32[32,256]{1,0:T(8,128)S(1)} %get-tuple-element.106), channel_id=1, source_target_pairs={{0,255},{1,2},{2,1},{3,4},{4,3},{5,6},{6,5},{7,8},{8,7},{9,10},{10... | collective-permute-start | bytes 98312 | tf_op jit(solution)/shard_map/ppermute | solution.py:612
  19.4 8.5 %collective-permute-start.3 = (f32[32,256]{1,0:T(8,128)S(1)}, f32[32,256]{1,0:T(8,128)S(1)}, u32[]{:S(2)}, u32[]{:S(2)}) collective-permute-start(f32[32,256]{1,0:T(8,128)S(1)} %get-tuple-element.107), channel_id=1, source_target_pairs={{0,1},{1,0},{2,3},{3,2},{4,5},{5,4},{6,7},{7,6},{8,9},{9,8},{10,11... | collective-permute-start | bytes 98312 | tf_op jit(solution)/shard_map/ppermute | solution.py:612
  26.0 2.0 %copy-start.1 = (f32[256,256]{1,0:T(8,128)S(1)}, f32[256,256]{1,0:T(8,128)}, u32[]{:S(2)}) copy-start(f32[256,256]{1,0:T(8,128)} %target_ref.1) | copy-start | bytes 786436
  27.3 10.9 %collective-permute-start.6 = (f32[256,256]{1,0:T(8,128)S(1)}, f32[256,256]{1,0:T(8,128)S(1)}, u32[]{:S(2)}, u32[]{:S(2)}) collective-permute-start(f32[256,256]{1,0:T(8,128)S(1)} %get-tuple-element.127), channel_id=1, source_target_pairs={{0,255},{1,2},{2,1},{3,4},{4,3},{5,6},{6,5},{7,8},{8,7},{9,10},{10... | collective-permute-start | bytes 786440 | tf_op jit(solution)/shard_map/ppermute | solution.py:612
  27.4 10.8 %collective-permute-start.7 = (f32[256,256]{1,0:T(8,128)S(1)}, f32[256,256]{1,0:T(8,128)S(1)}, u32[]{:S(2)}, u32[]{:S(2)}) collective-permute-start(f32[256,256]{1,0:T(8,128)S(1)} %get-tuple-element.127), channel_id=1, source_target_pairs={{0,1},{1,0},{2,3},{3,2},{4,5},{5,4},{6,7},{7,6},{8,9},{9,8},{10,11... | collective-permute-start | bytes 786440 | tf_op jit(solution)/shard_map/ppermute | solution.py:612
  29.8 8.9 %collective-permute-start.4 = (f32[32,256]{1,0:T(8,128)S(1)}, f32[32,256]{1,0:T(8,128)S(1)}, u32[]{:S(2)}, u32[]{:S(2)}) collective-permute-start(f32[32,256]{1,0:T(8,128)S(1)} %get-tuple-element.123), channel_id=1, source_target_pairs={{0,255},{1,2},{2,1},{3,4},{4,3},{5,6},{6,5},{7,8},{8,7},{9,10},{10... | collective-permute-start | bytes 98312 | tf_op jit(solution)/shard_map/ppermute | solution.py:612
  31.1 7.6 %collective-permute-start.5 = (f32[32,256]{1,0:T(8,128)S(1)}, f32[32,256]{1,0:T(8,128)S(1)}, u32[]{:S(2)}, u32[]{:S(2)}) collective-permute-start(f32[32,256]{1,0:T(8,128)S(1)} %get-tuple-element.124), channel_id=1, source_target_pairs={{0,1},{1,0},{2,3},{3,2},{4,5},{5,4},{6,7},{7,6},{8,9},{9,8},{10,11... | collective-permute-start | bytes 98312 | tf_op jit(solution)/shard_map/ppermute | solution.py:612
  42.1 1.7 %collective-permute-start.8 = (f32[16,40,128]{2,1,0:T(8,128)S(1)}, f32[16,40,128]{2,1,0:T(8,128)S(1)}, u32[]{:S(2)}, u32[]{:S(2)}) collective-permute-start(f32[16,40,128]{2,1,0:T(8,128)S(1)} %get-tuple-element.142), channel_id=1, source_target_pairs={{0,1},{1,0},{2,3},{3,2},{4,5},{5,4},{6,7},{7,6},{8,9},{9,8},{10,11... | collective-permute-start | bytes 983048 | tf_op jit(solution)/shard_map/ppermute | solution.py:700
  80.5 5.2 %collective-permute-start.9 = (f32[16,32,128]{2,1,0:T(8,128)S(1)}, f32[16,32,128]{2,1,0:T(8,128)S(1)}, u32[]{:S(2)}, u32[]{:S(2)}) collective-permute-start(f32[16,32,128]{2,1,0:T(8,128)S(1)} %all_to_all.17.own_ref), channel_id=1, source_target_pairs={{0,1},{1,0},{2,3},{3,2},{4,5},{5,4},{6,7},{7,6},{8,9},{9,8},{10,11... | collective-permute-start | bytes 786440 | tf_op jit(solution)/shard_map/ppermute | solution.py:706
